TPU v7x, 256 devices: a whole 4x4x8 slice. The times are simulated.
256 devices in a mesh: row: 32 (over z_lo, y, core), col: 8 (over z_hi, x).
Axes of the slice: x: 4, y: 4, z: 8 (z_hi: 2, z_lo: 4; z = z_hi * 4 + z_lo), core: 2. Of those that a mesh axis runs over, the one named last changes fastest.
Arguments:
- mask_params: float32 [2048, 1200], P('row', 'col'), may hold values from -6 to 6
- target_bits: int32 [2048, 40], P('row', 'col'), may hold values from 0 to 1073741823
- kern_real: float32 [64, 768], replicated, may hold values from -0.09375 to 0.09375
- kern_imag: float32 [64, 768], replicated, may hold values from -0.09375 to 0.09375
- socs_weights: float32 [12], replicated, may hold values from 0.02 to 0.2
Outputs:
- mask_grad: float32 [2048, 1200], P('row', 'col')
- intensity: float32 [2048, 1200], P('row', 'col')
All inputs are finite; a program needn't handle non-finite values.
Results may differ from a plain program's by a relative error of at most 0.0002.
Values sent between devices are 32-bit elements; how exact they have to be, the bound alone decides.
No kernel may reach another device: no remote copies, remote signals or barrier semaphores. Data moves between devices by JAX's collectives and lax.ppermute only.
A program may use at most 128 MiB of HBM per device.

v0:
```python
import functools
import math

import jax
import jax.numpy as jnp
import ml_dtypes
import numpy as np
from jax import lax
from jax.experimental import pallas as pl
from jax.experimental.pallas import tpu as pltpu
from jax.sharding import PartitionSpec as P

H = 32
KS = 64
ITERS = 3
ROWS = 128
sharpness = 2.0
steepness = 4.0
threshold = 0.8
step_size = 1.0
f32 = jnp.float32
bf16 = jnp.bfloat16


def up(value, unit):
    return -(-value // unit) * unit


def halves(table):
    table = table.astype(np.float32)
    high = table.astype(ml_dtypes.bfloat16)
    low = (table - high.astype(np.float32)).astype(ml_dtypes.bfloat16)
    return high, low


def angles(left, right, length):
    product = np.outer(left.astype(np.int64), right.astype(np.int64)) % length
    return product * (2.0 * math.pi / length)


def grown(table, rows, cols):
    return np.pad(table, [(0, rows - table.shape[0]), (0, cols - table.shape[1])])


def left_stack(table):
    high, low = halves(table)
    return np.concatenate([high, high, low], 1)


def right_stack(table):
    high, low = halves(table)
    return np.concatenate([high, high, low], 0)


class Geometry:
    def __init__(self, width):
        self.mask = width
        self.field = width - 2 * H
        self.grad = width - 4 * H
        self.length = width | 1
        self.freqs = (self.length + 1) // 2
        self.freqs_up = up(self.freqs, 16)
        self.mask_up = up(self.mask, 16)
        self.field_up = up(self.field, 16)
        self.grad_up = up(self.grad, 8)

    def tables(self):
        freq = np.arange(self.freqs)
        fu = self.freqs_up

        def forward(count, count_up):
            phase = angles(freq, np.arange(count), self.length)
            return np.concatenate(
                [grown(np.cos(phase), fu, count_up), grown(-np.sin(phase), fu, count_up)], 0
            )

        def inverse(places, count_up):
            phase = angles(places, freq, self.length)
            weight = np.where(freq == 0, 1.0, 2.0) / (self.length * ROWS)
            return np.concatenate(
                [
                    grown(np.cos(phase) * weight, count_up, fu),
                    grown(-np.sin(phase) * weight, count_up, fu),
                ],
                1,
            )

        taps = angles(freq, np.arange(KS) - H, self.length)
        return dict(
            mask_cols=left_stack(forward(self.mask, self.mask_up)),
            field_cols=left_stack(inverse(np.arange(self.field) + H, self.field_up)),
            source_cols=left_stack(forward(self.field, self.field_up)),
            grad_cols=left_stack(inverse(np.arange(self.grad) + H, self.grad_up)),
            tap_cols=left_stack(
                np.concatenate([grown(np.cos(taps), fu, KS), grown(np.sin(taps), fu, KS)], 1)
            ),
        )


def row_tables():
    freq = np.arange(ROWS)

    def complex_table(phase, sign):
        cos, sin = np.cos(phase), sign * np.sin(phase)
        return np.block([[cos, sin], [-sin, cos]])

    def side(table):
        high, low = halves(table)
        return np.concatenate([high, low], 1)

    places = np.arange(64) + H
    field = complex_table(angles(freq, places, ROWS), 1.0)
    field_swapped = np.concatenate([field[:, 64:], field[:, :64]], 1)
    source = complex_table(angles(np.arange(64), freq, ROWS), -1.0)
    source_swapped = np.concatenate([source[64:], source[:64]], 0)
    taps = angles(np.arange(KS) - H, freq, ROWS)
    tap = np.concatenate([np.cos(taps), -np.sin(taps)], 1)
    zero = np.zeros_like(tap)
    return dict(
        mask_rows=right_stack(complex_table(angles(freq, freq, ROWS), -1.0)),
        field_rows=side(field),
        field_rows_swapped=side(field_swapped),
        source_rows=right_stack(source),
        source_rows_swapped=right_stack(source_swapped),
        grad_rows=right_stack(complex_table(angles(freq, freq - H, ROWS), 1.0)),
        tap_rows=right_stack(np.block([[tap, zero], [zero, tap]])),
    )


def split(value):
    high = value.astype(bf16)
    return high, (value - high.astype(f32)).astype(bf16)


def dot(left, right):
    return lax.dot_general(
        left, right, (((1,), (0,)), ((), ())), preferred_element_type=f32
    )


def left_dot(table, value):
    high, low = split(value)
    return dot(table, jnp.concatenate([high, low, high], 0))


def right_dot(value, table):
    high, low = split(value)
    return dot(jnp.concatenate([high, low, high], 1), table)


def sigmoid(value):
    return 1.0 / (1.0 + jnp.exp(-value))


def swap_halves(value):
    return pltpu.roll(value, 64, 1)


def window(shape, first_col, first_row, whole_cols, whole_rows):
    col = lax.broadcasted_iota(jnp.int32, shape, 0) + first_col
    row = lax.broadcasted_iota(jnp.int32, shape, 1) + first_row
    return (col >= 0) & (col < whole_cols) & (row >= 0) & (row < whole_rows)


def setup_kernel(geos, kern_real, kern_imag, tap_rows, *rest):
    tables, outs, scratch = rest[: len(geos)], rest[len(geos) : -1], rest[-1]
    kernels = kern_real.shape[1] // KS
    both = jnp.concatenate([kern_real[...], kern_imag[...]], 0)
    for start in range(0, both.shape[1], 128):
        part = both[:, start : start + 128].T
        scratch[start : start + 128, :] = right_dot(part, tap_rows[...])
    for k in range(kernels):
        half = scratch[k * KS : (k + 1) * KS, :]
        turned = jnp.concatenate(
            [half[:, 128:256], -half[:, 0:128], half[:, 384:512], -half[:, 256:384]], 1
        )
        high, low = split(jnp.concatenate([half, turned], 0))
        stacked = jnp.concatenate([high, low, high], 0)
        for geo, table, out in zip(geos, tables, outs):
            spec = dot(table[...], stacked)
            count = geo.freqs_up
            out[2 * k * count : (2 * k + 1) * count, :] = spec[:, :256]
            out[(2 * k + 1) * count : (2 * k + 2) * count, :] = spec[:, 256:]


def one_step(geo, mask, target, inside, weights, spec, tabs, fields):
    count = geo.freqs_up
    kernels = weights.shape[0]
    lane = lax.broadcasted_iota(jnp.int32, (count, 128), 1) < 64
    across = left_dot(tabs["mask_cols"][...], mask)
    mask_spec = right_dot(
        jnp.concatenate([across[:count], across[count:]], 1), tabs["mask_rows"][...]
    )
    mask_re, mask_im = mask_spec[:, :128], mask_spec[:, 128:]

    def down(index, table):
        place = spec[index * count : (index + 1) * count, :]
        re, im = place[:, :128], place[:, 128:]
        product = jnp.concatenate(
            [re * mask_re - im * mask_im, re * mask_im + im * mask_re], 1
        )
        high, low = split(product)
        wide = dot(high, table[...])
        return wide[:, :128] + wide[:, 128:] + dot(low, table[:, :128])

    intensity = jnp.zeros((geo.field_up, 128), f32)
    for k in range(0, kernels, 2):
        parts = []
        for j in (k, k + 1):
            first = down(2 * j, tabs["field_rows"])
            second = down(2 * j + 1, tabs["field_rows_swapped"])
            parts.append(
                jnp.concatenate(
                    [
                        jnp.where(lane, first, second),
                        swap_halves(jnp.where(lane, second, first)),
                    ],
                    0,
                )
            )
        field = left_dot(tabs["field_cols"][...], jnp.concatenate(parts, 1))
        for j in (0, 1):
            own = field[:, j * 128 : (j + 1) * 128]
            fields[k + j] = own
            intensity = intensity + weights[k + j] * (own * own)
    intensity = intensity + swap_halves(intensity)
    resist = sigmoid(steepness * (intensity - threshold))
    cotangent = 2.0 * (resist - target) * steepness * resist * (1.0 - resist)
    cotangent = jnp.where(inside, cotangent, 0.0)
    total_re = jnp.zeros((count, 128), f32)
    total_im = jnp.zeros((count, 128), f32)
    for k in range(0, kernels, 2):
        source = jnp.concatenate(
            [(2.0 * weights[j] * cotangent) * fields[j] for j in (k, k + 1)], 1
        )
        across = left_dot(tabs["source_cols"][...], source)
        for j in (0, 1):
            re = across[:count, j * 128 : (j + 1) * 128]
            im = swap_halves(across[count:, j * 128 : (j + 1) * 128])
            for index, value, table in (
                (0, jnp.where(lane, re, im), tabs["source_rows"]),
                (1, jnp.where(lane, im, re), tabs["source_rows_swapped"]),
            ):
                got = right_dot(value, table[...])
                got_re, got_im = got[:, :128], got[:, 128:]
                start = (2 * (k + j) + index) * count
                place = spec[start : start + count, :]
                re_k, im_k = place[:, :128], place[:, 128:]
                total_re = total_re + (re_k * got_re + im_k * got_im)
                total_im = total_im + (re_k * got_im - im_k * got_re)
    back = right_dot(jnp.concatenate([total_re, total_im], 1), tabs["grad_rows"][...])
    grad = left_dot(
        tabs["grad_cols"][...], jnp.concatenate([back[:, :128], back[:, 128:]], 0)
    )
    return intensity, grad[: geo.grad]


STEP_TABLES = (
    "mask_cols",
    "mask_rows",
    "field_rows",
    "field_rows_swapped",
    "field_cols",
    "source_cols",
    "source_rows",
    "source_rows_swapped",
    "grad_rows",
    "grad_cols",
)


def prep_kernel(place, own, across, within, bits, params, target, to_left, to_right, tall):
    even = place[0] % 2 == 0
    cols = own.shape[1]
    tall[...] = jnp.zeros_like(tall)
    tall[0:32, :cols] = jnp.where(even, across[32:64, :], within[32:64, :])
    tall[32:96, :cols] = own[...]
    tall[96:128, :cols] = jnp.where(even, within[0:32, :], across[0:32, :])
    params[...] = tall[...].T[:cols]
    col = lax.broadcasted_iota(jnp.int32, (64, tall.shape[1]), 1)
    word = jnp.zeros_like(col)
    for index in range(bits.shape[1]):
        word = jnp.where(col // 30 == index, bits[:, index : index + 1], word)
    bit = jnp.bitwise_and(jnp.right_shift(word, col % 30), 1).astype(f32)
    target[...] = jnp.concatenate([bit, bit], 0).T[:cols]
    to_left[0:128, :] = params[0:128, :]
    to_left[128:224, :] = target[0:96, :]
    to_right[0:128, :] = params[cols - 128 : cols, :]
    to_right[128:224, :] = target[cols - 96 : cols, :]


def gathered(even, own, across, within):
    lane = lax.broadcasted_iota(jnp.int32, own.shape, 1) >= 64
    above = jnp.where(even, across[...], within[...])
    below = jnp.where(even, within[...], across[...])
    return own[...] + swap_halves(jnp.where(lane, above, below))


def stepped(params, grad):
    field = sigmoid(sharpness * params)
    return params - step_size * sharpness * field * (1.0 - field) * grad


def masked(geo, place, tile, whole, params, col_offset):
    first_col = place[1] * tile[1] + col_offset
    first_row = place[0] * tile[0] - H
    inside = window(params.shape, first_col, first_row, whole[1], whole[0])
    return jnp.where(inside, sigmoid(sharpness * params), 0.0)


def field_window(geo, place, tile, whole, col_offset):
    first_col = place[1] * tile[1] + col_offset + H
    return window((geo.field_up, 128), first_col, 0, whole[1], 1 << 30)


def first_kernel(
    geo, tile, whole, place, weights, own, target, left, right, spec, *rest
):
    tabs = dict(zip(STEP_TABLES, rest))
    spread, params_out, target_out, params, goal, fields = rest[len(STEP_TABLES) :]
    cols = own.shape[0]
    params[...] = jnp.zeros_like(params)
    params[0:128, :] = left[0:128, :]
    params[128 : 128 + cols, :] = own[...]
    params[128 + cols : 256 + cols, :] = right[0:128, :]
    goal[...] = jnp.zeros_like(goal)
    goal[0:96, :] = left[128:224, :]
    goal[96 : 96 + cols, :] = target[...]
    goal[96 + cols : 192 + cols, :] = right[128:224, :]
    mask = masked(geo, place, tile, whole, params[...], -128)
    inside = field_window(geo, place, tile, whole, -128)
    _, grad = one_step(geo, mask, goal[...], inside, weights, spec, tabs, fields)
    spread[...] = grad
    params_out[...] = params[64 : 64 + params_out.shape[0], :]
    target_out[...] = goal[64 : 64 + target_out.shape[0], :]


def second_kernel(
    geo, tile, whole, place, weights, own, across, within, old, target, spec, *rest
):
    tabs = dict(zip(STEP_TABLES, rest))
    spread, params_out, params, goal, fields = rest[len(STEP_TABLES) :]
    even = place[0] % 2 == 0
    width = own.shape[0]
    params[...] = jnp.zeros_like(params)
    params[0:width, :] = stepped(old[...], gathered(even, own, across, within))
    goal[...] = jnp.zeros_like(goal)
    goal[0 : target.shape[0], :] = target[...]
    mask = masked(geo, place, tile, whole, params[...], -64)
    inside = field_window(geo, place, tile, whole, -64)
    _, grad = one_step(geo, mask, goal[...], inside, weights, spec, tabs, fields)
    spread[...] = grad
    params_out[...] = params[64 : 64 + params_out.shape[0], :]


def update_kernel(place, own, across, within, old, params, to_left, to_right):
    even = place[0] % 2 == 0
    params[...] = stepped(old[...], gathered(even, own, across, within))
    cols = params.shape[0]
    to_left[...] = params[0:64, :]
    to_right[...] = params[cols - 64 : cols, :]


def third_kernel(
    geo, tile, whole, place, weights, own, left, right, target, spec, *rest
):
    tabs = dict(zip(STEP_TABLES, rest))
    spread, intensity_out, params, goal, fields = rest[len(STEP_TABLES) :]
    cols = own.shape[0]
    params[...] = jnp.zeros_like(params)
    params[0:64, :] = left[...]
    params[64 : 64 + cols, :] = own[...]
    params[64 + cols : 128 + cols, :] = right[...]
    goal[...] = jnp.zeros_like(goal)
    goal[0 : target.shape[0], :] = target[...]
    mask = masked(geo, place, tile, whole, params[...], -64)
    inside = field_window(geo, place, tile, whole, -64)
    aim = goal[0 : geo.field_up, :]
    intensity, grad = one_step(geo, mask, aim, inside, weights, spec, tabs, fields)
    spread[...] = grad
    goal[0 : geo.field_up, :] = intensity
    goal[0:256, :] = jnp.concatenate(
        [goal[H : H + cols, :], jnp.zeros((256 - cols, 128), f32)], 0
    )
    intensity_out[...] = goal[0:256, :].T[:64, :cols]


def final_kernel(place, own, across, within, out, wide):
    even = place[0] % 2 == 0
    cols = own.shape[0]
    wide[...] = jnp.zeros_like(wide)
    wide[0:cols, :] = gathered(even, own, across, within)
    out[...] = wide[...].T[H : H + 64, :cols]


def call(kernel, name, out_shapes, scratch, args, scalars):
    specs = [pl.BlockSpec(memory_space=pltpu.SMEM)] * scalars
    specs += [pl.BlockSpec(memory_space=pltpu.VMEM)] * (len(args) - scalars)
    return pl.pallas_call(
        kernel,
        name=name,
        out_shape=[jax.ShapeDtypeStruct(shape, f32) for shape in out_shapes],
        in_specs=specs,
        out_specs=[pl.BlockSpec(memory_space=pltpu.VMEM)] * len(out_shapes),
        scratch_shapes=[pltpu.VMEM(shape, f32) for shape in scratch],
        compiler_params=pltpu.CompilerParams(vmem_limit_bytes=56 * 1024 * 1024),
    )(*args)


def per_device(rows, cols, mask_params, target_bits, kern_real, kern_imag, socs_weights):
    tile = mask_params.shape
    whole = (tile[0] * rows, tile[1] * cols)
    kernels = kern_real.shape[1] // KS
    near = [(i, i ^ 1) for i in range(rows)]
    far = [(i, i + 1) for i in range(1, rows - 1, 2)]
    far = far + [(b, a) for a, b in far]
    right = [(i, i + 1) for i in range(cols - 1)]
    left = [(b, a) for a, b in right]
    place = jnp.stack([lax.axis_index("row"), lax.axis_index("col")]).astype(jnp.int32)

    def row_exchange(value):
        return lax.ppermute(value, "row", far), lax.ppermute(value, "row", near)

    def col_exchange(to_left, to_right):
        return lax.ppermute(to_right, "col", right), lax.ppermute(to_left, "col", left)

    wide, slim = Geometry(tile[1] + 8 * H), Geometry(tile[1] + 4 * H)
    shared = row_tables()
    wide_tabs, slim_tabs = {**wide.tables(), **shared}, {**slim.tables(), **shared}

    def tabs(table):
        return [jnp.asarray(table[name]) for name in STEP_TABLES]

    across, within = row_exchange(mask_params)
    n = tile[1]
    params, target, to_left, to_right = call(
        prep_kernel,
        "prep",
        [(n, 128), (n, 128), (224, 128), (224, 128)],
        [(128, 256)],
        [place, mask_params, across, within, target_bits],
        1,
    )
    from_left, from_right = col_exchange(to_left, to_right)
    wide_spec, slim_spec = call(
        functools.partial(setup_kernel, (wide, slim)),
        "spectra",
        [(2 * kernels * geo.freqs_up, 256) for geo in (wide, slim)],
        [(kernels * KS, 512)],
        [
            kern_real,
            kern_imag,
            jnp.asarray(shared["tap_rows"]),
            jnp.asarray(wide_tabs["tap_cols"]),
            jnp.asarray(slim_tabs["tap_cols"]),
        ],
        0,
    )

    def scratch(geo):
        return [(geo.mask_up, 128), (geo.field_up, 128), (kernels, geo.field_up, 128)]

    spread, params, target = call(
        functools.partial(first_kernel, wide, tile, whole),
        "first",
        [(wide.grad, 128), (slim.mask, 128), (slim.field, 128)],
        scratch(wide),
        [place, socs_weights, params, target, from_left, from_right, wide_spec, *tabs(wide_tabs)],
        2,
    )
    across, within = row_exchange(spread)
    spread, params = call(
        functools.partial(second_kernel, slim, tile, whole),
        "second",
        [(slim.grad, 128), (n, 128)],
        scratch(slim),
        [place, socs_weights, spread, across, within, params, target, slim_spec, *tabs(slim_tabs)],
        2,
    )
    across, within = row_exchange(spread)
    params, to_left, to_right = call(
        update_kernel,
        "update",
        [(n, 128), (64, 128), (64, 128)],
        [],
        [place, spread, across, within, params],
        1,
    )
    from_left, from_right = col_exchange(to_left, to_right)
    third_scratch = scratch(slim)
    third_scratch[1] = (max(256, slim.field_up), 128)
    spread, intensity = call(
        functools.partial(third_kernel, slim, tile, whole),
        "third",
        [(slim.grad, 128), tile],
        third_scratch,
        [place, socs_weights, params, from_left, from_right, target, slim_spec, *tabs(slim_tabs)],
        2,
    )
    across, within = row_exchange(spread)
    (mask_grad,) = call(
        final_kernel,
        "final",
        [tile],
        [(256, 128)],
        [place, spread, across, within],
        1,
    )
    return mask_grad, intensity


def solution(mesh):
    placed = (P("row", "col"), P("row", "col"), P(), P(), P())
    return jax.shard_map(
        functools.partial(per_device, mesh.shape["row"], mesh.shape["col"]),
        mesh=mesh,
        in_specs=placed,
        out_specs=(P("row", "col"), P("row", "col")),
        check_vma=False,
    )
```

profile of v0, /device:TPU:38, one launch (start us, length us, event | category | flops | bytes accessed | tf_op | source)
XLA Modules:
  0.0 122.8 jit_solution(13272850103400409085)
XLA Ops:
  0.6 3.9 %collective-permute-start = (f32[64,150]{1,0:T(8,128)}, f32[64,150]{1,0:T(8,128)S(1)}, u32[]{:S(2)}, u32[]{:S(2)}) collective-permute-start(f32[64,150]{1,0:T(8,128)} %own.1), channel_id=1, source_target_pairs={{8,16},{24,32},{40,48},{56,64},{72,80},{88,96},{104,112},{120,128}... | collective-permute-start | bytes 115208 | tf_op jit(solution)/shard_map/ppermute | solution.py:422
  4.5 0.1 collective-permute-start.1
  4.7 0.6 pad_add_fusion.place
  5.3 1.4 %copy.24.bits = s32[64,5]{1,0:T(8,128)} copy(s32[64,5]{0,1:T(8,128)} %param.23) | data formatting | bytes 2560 | tf_op args[1]
  6.6 1.9 %collective-permute-done.across = f32[64,150]{1,0:T(8,128)S(1)} collective-permute-done((f32[64,150]{1,0:T(8,128)}, f32[64,150]{1,0:T(8,128)S(1)}, u32[]{:S(2)}, u32[]{:S(2)}) %collective-permute-start) | collective-permute-done | bytes 38432 | tf_op jit(solution)/shard_map/ppermute | solution.py:422
  8.5 0.0 copy-start.8
  8.5 0.0 collective-permute-done.1.within
  8.5 0.6 copy-done.8
  9.2 0.0 copy-start.9
  9.2 0.6 copy-done.9
  9.8 1.9 %prep.1 = (f32[150,128]{1,0:T(8,128)}, f32[150,128]{1,0:T(8,128)}, f32[224,128]{1,0:T(8,128)}, f32[224,128]{1,0:T(8,128)}) custom-call(s32[2]{0:T(128)} %pad_add_fusion.place, f32[64,150]{1,0:T(8,128)} %own.1, f32[64,150]{1,0:T(8,128)} %copy-done.8, f32[64,150]{1,0:T(8,128)} %copy-done.9, s32[64,5]{1,0:T(8,128)} %copy.24.bits), custom_call_target="tpu_custom_call" | custom-call | tf_op jit(solution)/shard_map/prep/pallas_call | solution.py:399
  11.7 8.1 %collective-permute-start.2 = (f32[224,128]{1,0:T(8,128)}, f32[224,128]{1,0:T(8,128)S(1)}, u32[]{:S(2)}, u32[]{:S(2)}) collective-permute-start(f32[224,128]{1,0:T(8,128)} %get-tuple-element.20), channel_id=1, source_target_pairs={{0,1},{1,2},{2,3},{3,4},{4,5},{5,6},{6,7},{8,9},{9,10},{10,11},{11... | collective-permute-start | bytes 344072 | tf_op jit(solution)/shard_map/ppermute | solution.py:425
  19.8 1.9 %collective-permute-start.3 = (f32[224,128]{1,0:T(8,128)}, f32[224,128]{1,0:T(8,128)S(1)}, u32[]{:S(2)}, u32[]{:S(2)}) collective-permute-start(f32[224,128]{1,0:T(8,128)} %get-tuple-element.21), channel_id=1, source_target_pairs={{1,0},{2,1},{3,2},{4,3},{5,4},{6,5},{7,6},{9,8},{10,9},{11,10},{12... | collective-permute-start | bytes 344072 | tf_op jit(solution)/shard_map/ppermute | solution.py:425
  21.7 7.5 %spectra.1 = (f32[4992,256]{1,0:T(8,128)}, f32[3456,256]{1,0:T(8,128)}) custom-call(f32[64,768]{1,0:T(8,128)} %kern_real.1, f32[64,768]{1,0:T(8,128)} %kern_imag.1, bf16[384,512]{1,0:T(8,128)(2,1)} %constant.43.clone.tap_rows, bf16[208,384]{1,0:T(8,128)(2,1)} %constant.44.clone.rest_0_, bf16[144,384]{1,0:T(8,128)(2,1)} %constant.45.clone.rest_1_), custom_call_target="tpu_custom_call" | custom-call | tf_op jit(solution)/shard_map/spectra/pallas_call | solution.py:399
  29.2 0.0 collective-permute-done.2.left
  29.2 0.0 copy-start.2
  29.2 5.5 %collective-permute-done.3.right = f32[224,128]{1,0:T(8,128)S(1)} collective-permute-done((f32[224,128]{1,0:T(8,128)}, f32[224,128]{1,0:T(8,128)S(1)}, u32[]{:S(2)}, u32[]{:S(2)}) %collective-permute-start.3) | collective-permute-done | bytes 114720 | tf_op jit(solution)/shard_map/ppermute | solution.py:425
  34.7 0.0 copy-start.3
  34.7 0.0 copy-done.2
  34.7 0.6 copy-done.3
  35.3 16.5 %first.1 = (f32[278,128]{1,0:T(8,128)}, f32[278,128]{1,0:T(8,128)}, f32[214,128]{1,0:T(8,128)}) custom-call(s32[2]{0:T(128)} %pad_add_fusion.place, f32[12]{0:T(128)} %weights.5, f32[150,128]{1,0:T(8,128)} %get-tuple-element.18.own, f32[150,128]{1,0:T(8,128)} %get-tuple-element.19.target, f32[224,128]{1,0:T(8,128)} %copy-done.2, f32[224,128]{1,0:T(8,128)} %copy-done.3, ...), custom_call_target="tpu_custom_call" | custom-call | tf_op jit(solution)/shard_map/first/pallas_call | solution.py:399
  51.8 0.0 collective-permute-start.5
  51.8 2.3 %collective-permute-start.4 = (f32[278,128]{1,0:T(8,128)}, f32[278,128]{1,0:T(8,128)S(1)}, u32[]{:S(2)}, u32[]{:S(2)}) collective-permute-start(f32[278,128]{1,0:T(8,128)} %get-tuple-element.23.own), channel_id=1, source_target_pairs={{8,16},{24,32},{40,48},{56,64},{72,80},{88,96},{104,112},{120,128}... | collective-permute-start | bytes 427016 | tf_op jit(solution)/shard_map/ppermute | solution.py:422
  54.0 0.0 collective-permute-done.5.within
  54.0 0.0 copy-start
  54.0 6.5 %collective-permute-done.4.across = f32[278,128]{1,0:T(8,128)S(1)} collective-permute-done((f32[278,128]{1,0:T(8,128)}, f32[278,128]{1,0:T(8,128)S(1)}, u32[]{:S(2)}, u32[]{:S(2)}) %collective-permute-start.4) | collective-permute-done | bytes 142368 | tf_op jit(solution)/shard_map/ppermute | solution.py:422
  60.5 0.0 copy-start.1
  60.5 0.0 copy-done
  60.5 0.7 copy-done.1
  61.2 11.9 %second.1 = (f32[150,128]{1,0:T(8,128)}, f32[150,128]{1,0:T(8,128)}) custom-call(s32[2]{0:T(128)} %pad_add_fusion.place, f32[12]{0:T(128)} %weights.5, f32[278,128]{1,0:T(8,128)} %get-tuple-element.23.own, f32[278,128]{1,0:T(8,128)} %copy-done.1, f32[278,128]{1,0:T(8,128)} %copy-done, f32[278,128]{1,0:T(8,128)} %get-tuple-element.24.old, ...), custom_call_target="tpu_custom_call" | custom-call | tf_op jit(solution)/shard_map/second/pallas_call | solution.py:399
  73.0 0.0 collective-permute-start.7
  73.1 2.1 %collective-permute-start.6 = (f32[150,128]{1,0:T(8,128)}, f32[150,128]{1,0:T(8,128)S(1)}, u32[]{:S(2)}, u32[]{:S(2)}) collective-permute-start(f32[150,128]{1,0:T(8,128)} %get-tuple-element.27.own), channel_id=1, source_target_pairs={{8,16},{24,32},{40,48},{56,64},{72,80},{88,96},{104,112},{120,128}... | collective-permute-start | bytes 230408 | tf_op jit(solution)/shard_map/ppermute | solution.py:422
  75.1 0.0 collective-permute-done.7.within
  75.2 0.0 copy-start.4
  75.2 5.9 %collective-permute-done.6.across = f32[150,128]{1,0:T(8,128)S(1)} collective-permute-done((f32[150,128]{1,0:T(8,128)}, f32[150,128]{1,0:T(8,128)S(1)}, u32[]{:S(2)}, u32[]{:S(2)}) %collective-permute-start.6) | collective-permute-done | bytes 76832 | tf_op jit(solution)/shard_map/ppermute | solution.py:422
  81.1 0.0 copy-start.5
  81.1 0.0 copy-done.4
  81.1 0.6 copy-done.5
  81.7 1.8 %update.1 = (f32[150,128]{1,0:T(8,128)}, f32[64,128]{1,0:T(8,128)}, f32[64,128]{1,0:T(8,128)}) custom-call(s32[2]{0:T(128)} %pad_add_fusion.place, f32[150,128]{1,0:T(8,128)} %get-tuple-element.27.own, f32[150,128]{1,0:T(8,128)} %copy-done.5, f32[150,128]{1,0:T(8,128)} %copy-done.4, f32[150,128]{1,0:T(8,128)} %get-tuple-element.28.old), custom_call_target="tpu_custom_call" | custom-call | tf_op jit(solution)/shard_map/update/pallas_call | solution.py:399
  83.5 4.5 %collective-permute-start.8 = (f32[64,128]{1,0:T(8,128)}, f32[64,128]{1,0:T(8,128)S(1)}, u32[]{:S(2)}, u32[]{:S(2)}) collective-permute-start(f32[64,128]{1,0:T(8,128)} %get-tuple-element.30), channel_id=1, source_target_pairs={{0,1},{1,2},{2,3},{3,4},{4,5},{5,6},{6,7},{8,9},{9,10},{10,11},{11... | collective-permute-start | bytes 98312 | tf_op jit(solution)/shard_map/ppermute | solution.py:425
  88.0 2.1 %collective-permute-start.9 = (f32[64,128]{1,0:T(8,128)}, f32[64,128]{1,0:T(8,128)S(1)}, u32[]{:S(2)}, u32[]{:S(2)}) collective-permute-start(f32[64,128]{1,0:T(8,128)} %get-tuple-element.31), channel_id=1, source_target_pairs={{1,0},{2,1},{3,2},{4,3},{5,4},{6,5},{7,6},{9,8},{10,9},{11,10},{12... | collective-permute-start | bytes 98312 | tf_op jit(solution)/shard_map/ppermute | solution.py:425
  90.2 0.0 collective-permute-done.8.left
  90.2 0.0 copy-start.10
  90.2 9.9 %collective-permute-done.9.right = f32[64,128]{1,0:T(8,128)S(1)} collective-permute-done((f32[64,128]{1,0:T(8,128)}, f32[64,128]{1,0:T(8,128)S(1)}, u32[]{:S(2)}, u32[]{:S(2)}) %collective-permute-start.9) | collective-permute-done | bytes 32800 | tf_op jit(solution)/shard_map/ppermute | solution.py:425
  100.0 0.0 copy-start.11
  100.0 0.0 copy-done.10
  100.0 0.6 copy-done.11
  100.7 11.7 %third.1 = (f32[150,128]{1,0:T(8,128)}, f32[64,150]{1,0:T(8,128)}) custom-call(s32[2]{0:T(128)} %pad_add_fusion.place, f32[12]{0:T(128)} %weights.5, f32[150,128]{1,0:T(8,128)} %get-tuple-element.29.own, f32[64,128]{1,0:T(8,128)} %copy-done.10, f32[64,128]{1,0:T(8,128)} %copy-done.11, f32[214,128]{1,0:T(8,128)} %get-tuple-element.25.target, ...), custom_call_target="tpu_custom_call" | custom-call | tf_op jit(solution)/shard_map/third/pallas_call | solution.py:399
  112.3 0.0 collective-permute-start.11
  112.3 2.8 %collective-permute-start.10 = (f32[150,128]{1,0:T(8,128)}, f32[150,128]{1,0:T(8,128)S(1)}, u32[]{:S(2)}, u32[]{:S(2)}) collective-permute-start(f32[150,128]{1,0:T(8,128)} %get-tuple-element.32.own), channel_id=1, source_target_pairs={{8,16},{24,32},{40,48},{56,64},{72,80},{88,96},{104,112},{120,128}... | collective-permute-start | bytes 230408 | tf_op jit(solution)/shard_map/ppermute | solution.py:422
  115.2 0.0 collective-permute-done.11.within
  115.2 0.0 copy-start.6
  115.2 5.2 %collective-permute-done.10.across = f32[150,128]{1,0:T(8,128)S(1)} collective-permute-done((f32[150,128]{1,0:T(8,128)}, f32[150,128]{1,0:T(8,128)S(1)}, u32[]{:S(2)}, u32[]{:S(2)}) %collective-permute-start.10) | collective-permute-done | bytes 76832 | tf_op jit(solution)/shard_map/ppermute | solution.py:422
  120.4 0.0 copy-done.6
  120.4 0.0 copy-start.7
  120.4 0.6 copy-done.7
  121.0 1.8 %final.1 = f32[64,150]{1,0:T(8,128)} custom-call(s32[2]{0:T(128)} %pad_add_fusion.place, f32[150,128]{1,0:T(8,128)} %get-tuple-element.32.own, f32[150,128]{1,0:T(8,128)} %copy-done.7, f32[150,128]{1,0:T(8,128)} %copy-done.6), custom_call_target="tpu_custom_call" | custom-call | tf_op jit(solution)/shard_map/final/pallas_call | solution.py:399
Async XLA Ops:
  0.6 7.9 %collective-permute-start = (f32[64,150]{1,0:T(8,128)}, f32[64,150]{1,0:T(8,128)S(1)}, u32[]{:S(2)}, u32[]{:S(2)}) collective-permute-start(f32[64,150]{1,0:T(8,128)} %own.1), channel_id=1, source_target_pairs={{8,16},{24,32},{40,48},{56,64},{72,80},{88,96},{104,112},{120,128}... | collective-permute-start | bytes 115208 | tf_op jit(solution)/shard_map/ppermute | solution.py:422
  4.5 4.0 %collective-permute-start.1 = (f32[64,150]{1,0:T(8,128)}, f32[64,150]{1,0:T(8,128)S(1)}, u32[]{:S(2)}, u32[]{:S(2)}) collective-permute-start(f32[64,150]{1,0:T(8,128)} %own.1), channel_id=1, source_target_pairs={{0,8},{8,0},{16,24},{24,16},{32,40},{40,32},{48,56},{56,48},{64,72... | collective-permute-start | bytes 115208 | tf_op jit(solution)/shard_map/ppermute | solution.py:422
  8.5 0.6 copy-start.8
  9.2 0.6 copy-start.9
  11.7 17.5 %collective-permute-start.2 = (f32[224,128]{1,0:T(8,128)}, f32[224,128]{1,0:T(8,128)S(1)}, u32[]{:S(2)}, u32[]{:S(2)}) collective-permute-start(f32[224,128]{1,0:T(8,128)} %get-tuple-element.20), channel_id=1, source_target_pairs={{0,1},{1,2},{2,3},{3,4},{4,5},{5,6},{6,7},{8,9},{9,10},{10,11},{11... | collective-permute-start | bytes 344072 | tf_op jit(solution)/shard_map/ppermute | solution.py:425
  19.8 14.8 %collective-permute-start.3 = (f32[224,128]{1,0:T(8,128)}, f32[224,128]{1,0:T(8,128)S(1)}, u32[]{:S(2)}, u32[]{:S(2)}) collective-permute-start(f32[224,128]{1,0:T(8,128)} %get-tuple-element.21), channel_id=1, source_target_pairs={{1,0},{2,1},{3,2},{4,3},{5,4},{6,5},{7,6},{9,8},{10,9},{11,10},{12... | collective-permute-start | bytes 344072 | tf_op jit(solution)/shard_map/ppermute | solution.py:425
  29.2 5.5 %copy-start.2 = (f32[224,128]{1,0:T(8,128)}, f32[224,128]{1,0:T(8,128)S(1)}, u32[]{:S(2)}) copy-start(f32[224,128]{1,0:T(8,128)S(1)} %collective-permute-done.2.left) | copy-start | bytes 344068
  34.7 0.6 copy-start.3
  51.8 2.3 %collective-permute-start.5 = (f32[278,128]{1,0:T(8,128)}, f32[278,128]{1,0:T(8,128)S(1)}, u32[]{:S(2)}, u32[]{:S(2)}) collective-permute-start(f32[278,128]{1,0:T(8,128)} %get-tuple-element.23.own), channel_id=1, source_target_pairs={{0,8},{8,0},{16,24},{24,16},{32,40},{40,32},{48,56},{56,48},{64,72... | collective-permute-start | bytes 427016 | tf_op jit(solution)/shard_map/ppermute | solution.py:422
  51.8 8.7 %collective-permute-start.4 = (f32[278,128]{1,0:T(8,128)}, f32[278,128]{1,0:T(8,128)S(1)}, u32[]{:S(2)}, u32[]{:S(2)}) collective-permute-start(f32[278,128]{1,0:T(8,128)} %get-tuple-element.23.own), channel_id=1, source_target_pairs={{8,16},{24,32},{40,48},{56,64},{72,80},{88,96},{104,112},{120,128}... | collective-permute-start | bytes 427016 | tf_op jit(solution)/shard_map/ppermute | solution.py:422
  54.0 6.5 %copy-start = (f32[278,128]{1,0:T(8,128)}, f32[278,128]{1,0:T(8,128)S(1)}, u32[]{:S(2)}) copy-start(f32[278,128]{1,0:T(8,128)S(1)} %collective-permute-done.5.within) | copy-start | bytes 427012
  60.5 0.7 copy-start.1
  73.0 2.1 %collective-permute-start.7 = (f32[150,128]{1,0:T(8,128)}, f32[150,128]{1,0:T(8,128)S(1)}, u32[]{:S(2)}, u32[]{:S(2)}) collective-permute-start(f32[150,128]{1,0:T(8,128)} %get-tuple-element.27.own), channel_id=1, source_target_pairs={{0,8},{8,0},{16,24},{24,16},{32,40},{40,32},{48,56},{56,48},{64,72... | collective-permute-start | bytes 230408 | tf_op jit(solution)/shard_map/ppermute | solution.py:422
  73.1 8.0 %collective-permute-start.6 = (f32[150,128]{1,0:T(8,128)}, f32[150,128]{1,0:T(8,128)S(1)}, u32[]{:S(2)}, u32[]{:S(2)}) collective-permute-start(f32[150,128]{1,0:T(8,128)} %get-tuple-element.27.own), channel_id=1, source_target_pairs={{8,16},{24,32},{40,48},{56,64},{72,80},{88,96},{104,112},{120,128}... | collective-permute-start | bytes 230408 | tf_op jit(solution)/shard_map/ppermute | solution.py:422
  75.2 5.9 %copy-start.4 = (f32[150,128]{1,0:T(8,128)}, f32[150,128]{1,0:T(8,128)S(1)}, u32[]{:S(2)}) copy-start(f32[150,128]{1,0:T(8,128)S(1)} %collective-permute-done.7.within) | copy-start | bytes 230404
  81.1 0.6 copy-start.5
  83.5 6.7 %collective-permute-start.8 = (f32[64,128]{1,0:T(8,128)}, f32[64,128]{1,0:T(8,128)S(1)}, u32[]{:S(2)}, u32[]{:S(2)}) collective-permute-start(f32[64,128]{1,0:T(8,128)} %get-tuple-element.30), channel_id=1, source_target_pairs={{0,1},{1,2},{2,3},{3,4},{4,5},{5,6},{6,7},{8,9},{9,10},{10,11},{11... | collective-permute-start | bytes 98312 | tf_op jit(solution)/shard_map/ppermute | solution.py:425
  88.0 12.0 %collective-permute-start.9 = (f32[64,128]{1,0:T(8,128)}, f32[64,128]{1,0:T(8,128)S(1)}, u32[]{:S(2)}, u32[]{:S(2)}) collective-permute-start(f32[64,128]{1,0:T(8,128)} %get-tuple-element.31), channel_id=1, source_target_pairs={{1,0},{2,1},{3,2},{4,3},{5,4},{6,5},{7,6},{9,8},{10,9},{11,10},{12... | collective-permute-start | bytes 98312 | tf_op jit(solution)/shard_map/ppermute | solution.py:425
  90.2 9.9 %copy-start.10 = (f32[64,128]{1,0:T(8,128)}, f32[64,128]{1,0:T(8,128)S(1)}, u32[]{:S(2)}) copy-start(f32[64,128]{1,0:T(8,128)S(1)} %collective-permute-done.8.left) | copy-start | bytes 98308
  100.0 0.6 copy-start.11
  112.3 2.8 %collective-permute-start.11 = (f32[150,128]{1,0:T(8,128)}, f32[150,128]{1,0:T(8,128)S(1)}, u32[]{:S(2)}, u32[]{:S(2)}) collective-permute-start(f32[150,128]{1,0:T(8,128)} %get-tuple-element.32.own), channel_id=1, source_target_pairs={{0,8},{8,0},{16,24},{24,16},{32,40},{40,32},{48,56},{56,48},{64,72... | collective-permute-start | bytes 230408 | tf_op jit(solution)/shard_map/ppermute | solution.py:422
  112.3 8.0 %collective-permute-start.10 = (f32[150,128]{1,0:T(8,128)}, f32[150,128]{1,0:T(8,128)S(1)}, u32[]{:S(2)}, u32[]{:S(2)}) collective-permute-start(f32[150,128]{1,0:T(8,128)} %get-tuple-element.32.own), channel_id=1, source_target_pairs={{8,16},{24,32},{40,48},{56,64},{72,80},{88,96},{104,112},{120,128}... | collective-permute-start | bytes 230408 | tf_op jit(solution)/shard_map/ppermute | solution.py:422
  115.2 5.2 %copy-start.6 = (f32[150,128]{1,0:T(8,128)}, f32[150,128]{1,0:T(8,128)S(1)}, u32[]{:S(2)}) copy-start(f32[150,128]{1,0:T(8,128)S(1)} %collective-permute-done.11.within) | copy-start | bytes 230404
  120.4 0.6 copy-start.7
where the time goes:
time: 123 us
  Pallas kernels  52.9 us (43%)
  waiting for transfers between devices  34.8 us (28%)
  starting transfers between devices  27.9 us (23%)
  local copies, waits for them, and re-layouts  5.81 us (5%)
    pallas_call x7, Pallas kernels, call(): pl.pallas_call(kernel, name=name, out_shape=[jax.ShapeDtypeStruct(shape,...  52.9 us
    ppermute x8, waiting for transfers between devices, row_exchange(): return (lax.ppermute(value, 'row', far), lax.ppermute(value, 'row', near))  19.5 us
    ppermute x2, waiting for transfers between devices, col_exchange(): lax.ppermute(to_left, 'col', left)  15.3 us
    ppermute x2, starting transfers between devices, col_exchange(): lax.ppermute(to_right, 'col', right)  12.6 us
    ppermute x8, starting transfers between devices, row_exchange(): return (lax.ppermute(value, 'row', far), lax.ppermute(value, 'row', near))  11.2 us
    unnamed x25, local copies, waits for them, and re-layouts  5.81 us
    ppermute x2, starting transfers between devices, col_exchange(): lax.ppermute(to_left, 'col', left)  4.06 us
  transfers between devices with their start and end apart: 12, of which 6 were waited for; matrix products, arithmetic and copies ran while one was open for 2% of the time, Pallas kernels for 6%

commit v1 on v0

--- a/solution.py
+++ b/solution.py
@@ -162,8 +162,17 @@
     return (col >= 0) & (col < whole_cols) & (row >= 0) & (row < whole_rows)
 
 
-def setup_kernel(geos, kern_real, kern_imag, tap_rows, *rest):
-    tables, outs, scratch = rest[: len(geos)], rest[len(geos) : -1], rest[-1]
+def setup_kernel(geos, held, kern_real, kern_imag, tap_rows, *rest):
+    tables, rest = rest[: len(geos)], rest[len(geos) :]
+    sources, rest = rest[:held], rest[held:]
+    outs, rest = rest[: len(geos)], rest[len(geos) :]
+    targets, (scratch, sems) = rest[:held], rest[held:]
+    copies = [
+        pltpu.make_async_copy(source, target, sems.at[index])
+        for index, (source, target) in enumerate(zip(sources, targets))
+    ]
+    for copy in copies:
+        copy.start()
     kernels = kern_real.shape[1] // KS
     both = jnp.concatenate([kern_real[...], kern_imag[...]], 0)
     for start in range(0, both.shape[1], 128):
@@ -181,6 +190,8 @@
             count = geo.freqs_up
             out[2 * k * count : (2 * k + 1) * count, :] = spec[:, :256]
             out[(2 * k + 1) * count : (2 * k + 2) * count, :] = spec[:, 256:]
+    for copy in copies:
+        copy.wait()
 
 
 def one_step(geo, mask, target, inside, weights, spec, tabs, fields):
@@ -255,18 +266,16 @@
     return intensity, grad[: geo.grad]
 
 
-STEP_TABLES = (
-    "mask_cols",
+COLUMN_TABLES = ("mask_cols", "field_cols", "source_cols", "grad_cols")
+ROW_TABLES = (
     "mask_rows",
     "field_rows",
     "field_rows_swapped",
-    "field_cols",
-    "source_cols",
     "source_rows",
     "source_rows_swapped",
     "grad_rows",
-    "grad_cols",
 )
+STEP_TABLES = COLUMN_TABLES + ROW_TABLES
 
 
 def prep_kernel(place, own, across, within, bits, params, target, to_left, to_right, tall):
@@ -394,16 +403,22 @@
 
 
 def call(kernel, name, out_shapes, scratch, args, scalars):
+    args = args[:scalars] + [
+        pltpu.with_memory_space_constraint(arg, pltpu.VMEM) for arg in args[scalars:]
+    ]
     specs = [pl.BlockSpec(memory_space=pltpu.SMEM)] * scalars
     specs += [pl.BlockSpec(memory_space=pltpu.VMEM)] * (len(args) - scalars)
     return pl.pallas_call(
         kernel,
         name=name,
-        out_shape=[jax.ShapeDtypeStruct(shape, f32) for shape in out_shapes],
+        out_shape=[
+            shape if isinstance(shape, jax.ShapeDtypeStruct) else pltpu.VMEM(shape, f32)
+            for shape in out_shapes
+        ],
         in_specs=specs,
         out_specs=[pl.BlockSpec(memory_space=pltpu.VMEM)] * len(out_shapes),
         scratch_shapes=[pltpu.VMEM(shape, f32) for shape in scratch],
-        compiler_params=pltpu.CompilerParams(vmem_limit_bytes=56 * 1024 * 1024),
+        compiler_params=pltpu.CompilerParams(vmem_limit_bytes=24 * 1024 * 1024),
     )(*args)
 
 
@@ -426,10 +441,7 @@
 
     wide, slim = Geometry(tile[1] + 8 * H), Geometry(tile[1] + 4 * H)
     shared = row_tables()
-    wide_tabs, slim_tabs = {**wide.tables(), **shared}, {**slim.tables(), **shared}
-
-    def tabs(table):
-        return [jnp.asarray(table[name]) for name in STEP_TABLES]
+    wide_tabs, slim_tabs = wide.tables(), slim.tables()
 
     across, within = row_exchange(mask_params)
     n = tile[1]
@@ -442,20 +454,39 @@
         1,
     )
     from_left, from_right = col_exchange(to_left, to_right)
-    wide_spec, slim_spec = call(
-        functools.partial(setup_kernel, (wide, slim)),
-        "spectra",
-        [(2 * kernels * geo.freqs_up, 256) for geo in (wide, slim)],
-        [(kernels * KS, 512)],
-        [
-            kern_real,
-            kern_imag,
-            jnp.asarray(shared["tap_rows"]),
-            jnp.asarray(wide_tabs["tap_cols"]),
-            jnp.asarray(slim_tabs["tap_cols"]),
+    names = [(label, name) for label in ("wide", "slim") for name in COLUMN_TABLES]
+    names += [("shared", name) for name in ROW_TABLES]
+    made = {"wide": wide_tabs, "slim": slim_tabs, "shared": shared}
+    tables = [jnp.asarray(made[label][name]) for label, name in names]
+    inputs = [
+        kern_real,
+        kern_imag,
+        jnp.asarray(shared["tap_rows"]),
+        jnp.asarray(wide_tabs["tap_cols"]),
+        jnp.asarray(slim_tabs["tap_cols"]),
+    ]
+    wide_spec, slim_spec, *held = pl.pallas_call(
+        functools.partial(setup_kernel, (wide, slim), len(tables)),
+        name="spectra",
+        out_shape=[
+            pltpu.VMEM((2 * kernels * geo.freqs_up, 256), f32) for geo in (wide, slim)
+        ]
+        + [pltpu.VMEM(table.shape, table.dtype) for table in tables],
+        in_specs=[pl.BlockSpec(memory_space=pltpu.VMEM)] * len(inputs)
+        + [pl.BlockSpec(memory_space=pltpu.HBM)] * len(tables),
+        out_specs=[pl.BlockSpec(memory_space=pltpu.VMEM)] * (2 + len(tables)),
+        scratch_shapes=[
+            pltpu.VMEM((kernels * KS, 512), f32),
+            pltpu.SemaphoreType.DMA((len(tables),)),
         ],
-        0,
-    )
+        compiler_params=pltpu.CompilerParams(vmem_limit_bytes=24 * 1024 * 1024),
+    )(*[pltpu.with_memory_space_constraint(arg, pltpu.HBM) for arg in inputs + tables])
+    place_of = {key: table for key, table in zip(names, held)}
+
+    def tabs(label):
+        return [place_of[label, name] for name in COLUMN_TABLES] + [
+            place_of["shared", name] for name in ROW_TABLES
+        ]
 
     def scratch(geo):
         return [(geo.mask_up, 128), (geo.field_up, 128), (kernels, geo.field_up, 128)]
@@ -465,7 +496,7 @@
         "first",
         [(wide.grad, 128), (slim.mask, 128), (slim.field, 128)],
         scratch(wide),
-        [place, socs_weights, params, target, from_left, from_right, wide_spec, *tabs(wide_tabs)],
+        [place, socs_weights, params, target, from_left, from_right, wide_spec, *tabs("wide")],
         2,
     )
     across, within = row_exchange(spread)
@@ -474,7 +505,7 @@
         "second",
         [(slim.grad, 128), (n, 128)],
         scratch(slim),
-        [place, socs_weights, spread, across, within, params, target, slim_spec, *tabs(slim_tabs)],
+        [place, socs_weights, spread, across, within, params, target, slim_spec, *tabs("slim")],
         2,
     )
     across, within = row_exchange(spread)
@@ -492,16 +523,16 @@
     spread, intensity = call(
         functools.partial(third_kernel, slim, tile, whole),
         "third",
-        [(slim.grad, 128), tile],
+        [(slim.grad, 128), jax.ShapeDtypeStruct(tile, f32)],
         third_scratch,
-        [place, socs_weights, params, from_left, from_right, target, slim_spec, *tabs(slim_tabs)],
+        [place, socs_weights, params, from_left, from_right, target, slim_spec, *tabs("slim")],
         2,
     )
     across, within = row_exchange(spread)
     (mask_grad,) = call(
         final_kernel,
         "final",
-        [tile],
+        [jax.ShapeDtypeStruct(tile, f32)],
         [(256, 128)],
         [place, spread, across, within],
         1,

time: 123 us -> 106 us (0.86)
  Pallas kernels: 52.9 us -> 39.6 us
  local copies, waits for them, and re-layouts: 5.81 us -> 1.62 us
    pallas_call x7, Pallas kernels: 52.9 us -> 39.6 us  [the longest x6 33.5 us: call(): pl.pallas_call(kernel, name=name, out_shape=[shape if isinstance(shape, j...]
    unnamed x25 -> x5, local copies, waits for them, and re-layouts: 5.81 us -> 1.62 us
    ppermute x8, starting transfers between devices: 11.2 us -> 12.7 us  [row_exchange(): return (lax.ppermute(value, 'row', far), lax.ppermute(value, 'row', near))]
  transfers between devices with their start and end apart: 12 -> 12, of which waited for: 6 -> 6; matrix products, arithmetic and copies ran while one was open for 2% -> 1% of each run, Pallas kernels for 6% -> 6%
where the time goes in v1:
time: 106 us; the launch traced here: 105 us
  Pallas kernels  39.6 us (37%)
  waiting for transfers between devices  34.3 us (32%)
  starting transfers between devices  28.9 us (27%)
  local copies, waits for them, and re-layouts  1.62 us (2%)
    pallas_call x6, Pallas kernels, call(): pl.pallas_call(kernel, name=name, out_shape=[shape if isinstance(shape, j...  33.5 us
    ppermute x8, waiting for transfers between devices, row_exchange(): return (lax.ppermute(value, 'row', far), lax.ppermute(value, 'row', near))  18.7 us
    ppermute x2, waiting for transfers between devices, col_exchange(): lax.ppermute(to_left, 'col', left)  15.7 us
    ppermute x8, starting transfers between devices, row_exchange(): return (lax.ppermute(value, 'row', far), lax.ppermute(value, 'row', near))  12.7 us
    ppermute x2, starting transfers between devices, col_exchange(): lax.ppermute(to_right, 'col', right)  12.2 us
    pallas_call x1, Pallas kernels, per_device(): pl.pallas_call(functools.partial(setup_kernel, (wide, slim), len(tables))...  6.07 us
    ppermute x2, starting transfers between devices, col_exchange(): lax.ppermute(to_left, 'col', left)  4.06 us
  transfers between devices with their start and end apart: 12, of which 6 were waited for; matrix products, arithmetic and copies ran while one was open for 1% of the time, Pallas kernels for 6%

profile of v1, /device:TPU:38, one launch (start us, length us, event | category | flops | bytes accessed | tf_op | source)
XLA Modules:
  0.0 105.3 jit_solution(6841617369069583944)
XLA Ops:
  0.6 3.9 %collective-permute-start = (f32[64,150]{1,0:T(8,128)}, f32[64,150]{1,0:T(8,128)S(1)}, u32[]{:S(2)}, u32[]{:S(2)}) collective-permute-start(f32[64,150]{1,0:T(8,128)} %own.1), channel_id=1, source_target_pairs={{8,16},{24,32},{40,48},{56,64},{72,80},{88,96},{104,112},{120,128}... | collective-permute-start | bytes 115208 | tf_op jit(solution)/shard_map/ppermute | solution.py:437
  4.5 0.1 collective-permute-start.1
  4.7 0.1 pad_add_fusion.place
  4.7 0.8 copy.24.bits
  5.5 3.0 %collective-permute-done.across = f32[64,150]{1,0:T(8,128)S(1)} collective-permute-done((f32[64,150]{1,0:T(8,128)}, f32[64,150]{1,0:T(8,128)S(1)}, u32[]{:S(2)}, u32[]{:S(2)}) %collective-permute-start) | collective-permute-done | bytes 38432 | tf_op jit(solution)/shard_map/ppermute | solution.py:437
  8.5 0.0 collective-permute-done.1.within
  8.5 0.0 copy-start
  8.5 0.8 copy-done
  9.4 0.8 prep.1
  10.2 8.1 %collective-permute-start.2 = (f32[224,128]{1,0:T(8,128)S(1)}, f32[224,128]{1,0:T(8,128)S(1)}, u32[]{:S(2)}, u32[]{:S(2)}) collective-permute-start(f32[224,128]{1,0:T(8,128)S(1)} %get-tuple-element.34), channel_id=1, source_target_pairs={{0,1},{1,2},{2,3},{3,4},{4,5},{5,6},{6,7},{8,9},{9,10},{10,11},{11... | collective-permute-start | bytes 344072 | tf_op jit(solution)/shard_map/ppermute | solution.py:440
  18.3 0.0 copy-start.1
  18.3 1.9 %collective-permute-start.3 = (f32[224,128]{1,0:T(8,128)S(1)}, f32[224,128]{1,0:T(8,128)S(1)}, u32[]{:S(2)}, u32[]{:S(2)}) collective-permute-start(f32[224,128]{1,0:T(8,128)S(1)} %get-tuple-element.35), channel_id=1, source_target_pairs={{1,0},{2,1},{3,2},{4,3},{5,4},{6,5},{7,6},{9,8},{10,9},{11,10},{12... | collective-permute-start | bytes 344072 | tf_op jit(solution)/shard_map/ppermute | solution.py:440
  20.2 6.1 %spectra.1 = (f32[4992,256]{1,0:T(8,128)S(1)}, f32[3456,256]{1,0:T(8,128)S(1)}, bf16[416,1248]{1,0:T(8,128)(2,1)S(1)}, bf16[352,1248]{1,0:T(8,128)(2,1)S(1)}, bf...) custom-call(f32[64,768]{1,0:T(8,128)} %kern_real.1, ...), custom_call_target="tpu_custom_call" | custom-call | tf_op jit(solution)/shard_map/spectra/pallas_call | solution.py:468
  26.3 0.0 collective-permute-done.2.left
  26.3 5.9 %collective-permute-done.3.right = f32[224,128]{1,0:T(8,128)S(1)} collective-permute-done((f32[224,128]{1,0:T(8,128)S(1)}, f32[224,128]{1,0:T(8,128)S(1)}, u32[]{:S(2)}, u32[]{:S(2)}) %collective-permute-start.3) | collective-permute-done | bytes 114720 | tf_op jit(solution)/shard_map/ppermute | solution.py:440
  32.2 0.0 copy-done.1
  32.2 12.7 %first.1 = (f32[278,128]{1,0:T(8,128)S(1)}, f32[278,128]{1,0:T(8,128)S(1)}, f32[214,128]{1,0:T(8,128)S(1)}) custom-call(s32[2]{0:T(128)S(1)} %pad_add_fusion.place, f32[12]{0:T(128)S(1)} %copy-done.1, f32[150,128]{1,0:T(8,128)S(1)} %get-tuple-element.32.own, f32[150,128]{1,0:T(8,128)S(1)} %get-tuple-element.33.target, ...), custom_call_target="tpu_custom_call" | custom-call | tf_op jit(solution)/shard_map/first/pallas_call | solution.py:411
  45.0 0.1 collective-permute-start.5
  45.1 3.0 %collective-permute-start.4 = (f32[278,128]{1,0:T(8,128)S(1)}, f32[278,128]{1,0:T(8,128)S(1)}, u32[]{:S(2)}, u32[]{:S(2)}) collective-permute-start(f32[278,128]{1,0:T(8,128)S(1)} %get-tuple-element.47.own), channel_id=1, source_target_pairs={{8,16},{24,32},{40,48},{56,64},{72,80},{88,96},{104,112},{120,128}... | collective-permute-start | bytes 427016 | tf_op jit(solution)/shard_map/ppermute | solution.py:437
  48.1 0.0 collective-permute-done.5.within
  48.1 5.5 %collective-permute-done.4.across = f32[278,128]{1,0:T(8,128)S(1)} collective-permute-done((f32[278,128]{1,0:T(8,128)S(1)}, f32[278,128]{1,0:T(8,128)S(1)}, u32[]{:S(2)}, u32[]{:S(2)}) %collective-permute-start.4) | collective-permute-done | bytes 142368 | tf_op jit(solution)/shard_map/ppermute | solution.py:437
  53.6 8.8 %second.1 = (f32[150,128]{1,0:T(8,128)S(1)}, f32[150,128]{1,0:T(8,128)S(1)}) custom-call(s32[2]{0:T(128)S(1)} %pad_add_fusion.place, f32[12]{0:T(128)S(1)} %copy-done.1, f32[278,128]{1,0:T(8,128)S(1)} %get-tuple-element.47.own, f32[278,128]{1,0:T(8,128)S(1)} %collective-permute-done.4.across, f32[278,128]{1,0:T(8,128)S(1)} %collective-permute-done.5.within, ...), custom_call_target="tpu_custom_call" | custom-call | tf_op jit(solution)/shard_map/second/pallas_call | solution.py:411
  62.4 0.1 collective-permute-start.7
  62.5 2.8 %collective-permute-start.6 = (f32[150,128]{1,0:T(8,128)S(1)}, f32[150,128]{1,0:T(8,128)S(1)}, u32[]{:S(2)}, u32[]{:S(2)}) collective-permute-start(f32[150,128]{1,0:T(8,128)S(1)} %get-tuple-element.55.own), channel_id=1, source_target_pairs={{8,16},{24,32},{40,48},{56,64},{72,80},{88,96},{104,112},{120,128}... | collective-permute-start | bytes 230408 | tf_op jit(solution)/shard_map/ppermute | solution.py:437
  65.3 0.0 collective-permute-done.7.within
  65.3 5.0 %collective-permute-done.6.across = f32[150,128]{1,0:T(8,128)S(1)} collective-permute-done((f32[150,128]{1,0:T(8,128)S(1)}, f32[150,128]{1,0:T(8,128)S(1)}, u32[]{:S(2)}, u32[]{:S(2)}) %collective-permute-start.6) | collective-permute-done | bytes 76832 | tf_op jit(solution)/shard_map/ppermute | solution.py:437
  70.3 0.6 update.1
  70.9 4.1 %collective-permute-start.8 = (f32[64,128]{1,0:T(8,128)S(1)}, f32[64,128]{1,0:T(8,128)S(1)}, u32[]{:S(2)}, u32[]{:S(2)}) collective-permute-start(f32[64,128]{1,0:T(8,128)S(1)} %get-tuple-element.58), channel_id=1, source_target_pairs={{0,1},{1,2},{2,3},{3,4},{4,5},{5,6},{6,7},{8,9},{9,10},{10,11},{11... | collective-permute-start | bytes 98312 | tf_op jit(solution)/shard_map/ppermute | solution.py:440
  75.0 2.1 %collective-permute-start.9 = (f32[64,128]{1,0:T(8,128)S(1)}, f32[64,128]{1,0:T(8,128)S(1)}, u32[]{:S(2)}, u32[]{:S(2)}) collective-permute-start(f32[64,128]{1,0:T(8,128)S(1)} %get-tuple-element.59), channel_id=1, source_target_pairs={{1,0},{2,1},{3,2},{4,3},{5,4},{6,5},{7,6},{9,8},{10,9},{11,10},{12... | collective-permute-start | bytes 98312 | tf_op jit(solution)/shard_map/ppermute | solution.py:440
  77.2 0.0 collective-permute-done.8.left
  77.2 9.8 %collective-permute-done.9.right = f32[64,128]{1,0:T(8,128)S(1)} collective-permute-done((f32[64,128]{1,0:T(8,128)S(1)}, f32[64,128]{1,0:T(8,128)S(1)}, u32[]{:S(2)}, u32[]{:S(2)}) %collective-permute-start.9) | collective-permute-done | bytes 32800 | tf_op jit(solution)/shard_map/ppermute | solution.py:440
  86.9 9.2 %third.1 = (f32[150,128]{1,0:T(8,128)S(1)}, f32[64,150]{1,0:T(8,128)}) custom-call(s32[2]{0:T(128)S(1)} %pad_add_fusion.place, f32[12]{0:T(128)S(1)} %copy-done.1, f32[150,128]{1,0:T(8,128)S(1)} %get-tuple-element.57.own, f32[64,128]{1,0:T(8,128)S(1)} %collective-permute-done.8.left, f32[64,128]{1,0:T(8,128)S(1)} %collective-permute-done.9.right, ...), custom_call_target="tpu_custom_call" | custom-call | tf_op jit(solution)/shard_map/third/pallas_call | solution.py:411
  96.2 0.0 collective-permute-start.11
  96.2 2.7 %collective-permute-start.10 = (f32[150,128]{1,0:T(8,128)S(1)}, f32[150,128]{1,0:T(8,128)S(1)}, u32[]{:S(2)}, u32[]{:S(2)}) collective-permute-start(f32[150,128]{1,0:T(8,128)S(1)} %get-tuple-element.60.own), channel_id=1, source_target_pairs={{8,16},{24,32},{40,48},{56,64},{72,80},{88,96},{104,112},{120,128}... | collective-permute-start | bytes 230408 | tf_op jit(solution)/shard_map/ppermute | solution.py:437
  98.9 0.0 collective-permute-done.11.within
  98.9 5.1 %collective-permute-done.10.across = f32[150,128]{1,0:T(8,128)S(1)} collective-permute-done((f32[150,128]{1,0:T(8,128)S(1)}, f32[150,128]{1,0:T(8,128)S(1)}, u32[]{:S(2)}, u32[]{:S(2)}) %collective-permute-start.10) | collective-permute-done | bytes 76832 | tf_op jit(solution)/shard_map/ppermute | solution.py:437
  104.0 1.3 %final.1 = f32[64,150]{1,0:T(8,128)} custom-call(s32[2]{0:T(128)S(1)} %pad_add_fusion.place, f32[150,128]{1,0:T(8,128)S(1)} %get-tuple-element.60.own, f32[150,128]{1,0:T(8,128)S(1)} %collective-permute-done.10.across, f32[150,128]{1,0:T(8,128)S(1)} %collective-permute-done.11.within), custom_call_target="tpu_custom_call" | custom-call | tf_op jit(solution)/shard_map/final/pallas_call | solution.py:411
Async XLA Ops:
  0.6 7.9 %collective-permute-start = (f32[64,150]{1,0:T(8,128)}, f32[64,150]{1,0:T(8,128)S(1)}, u32[]{:S(2)}, u32[]{:S(2)}) collective-permute-start(f32[64,150]{1,0:T(8,128)} %own.1), channel_id=1, source_target_pairs={{8,16},{24,32},{40,48},{56,64},{72,80},{88,96},{104,112},{120,128}... | collective-permute-start | bytes 115208 | tf_op jit(solution)/shard_map/ppermute | solution.py:437
  4.5 4.0 %collective-permute-start.1 = (f32[64,150]{1,0:T(8,128)}, f32[64,150]{1,0:T(8,128)S(1)}, u32[]{:S(2)}, u32[]{:S(2)}) collective-permute-start(f32[64,150]{1,0:T(8,128)} %own.1), channel_id=1, source_target_pairs={{0,8},{8,0},{16,24},{24,16},{32,40},{40,32},{48,56},{56,48},{64,72... | collective-permute-start | bytes 115208 | tf_op jit(solution)/shard_map/ppermute | solution.py:437
  8.5 0.8 copy-start
  10.2 16.1 %collective-permute-start.2 = (f32[224,128]{1,0:T(8,128)S(1)}, f32[224,128]{1,0:T(8,128)S(1)}, u32[]{:S(2)}, u32[]{:S(2)}) collective-permute-start(f32[224,128]{1,0:T(8,128)S(1)} %get-tuple-element.34), channel_id=1, source_target_pairs={{0,1},{1,2},{2,3},{3,4},{4,5},{5,6},{6,7},{8,9},{9,10},{10,11},{11... | collective-permute-start | bytes 344072 | tf_op jit(solution)/shard_map/ppermute | solution.py:440
  18.3 13.9 %copy-start.1 = (f32[12]{0:T(128)S(1)}, f32[12]{0:T(128)}, u32[]{:S(2)}) copy-start(f32[12]{0:T(128)} %weights.5) | copy-start | bytes 148
  18.3 13.9 %collective-permute-start.3 = (f32[224,128]{1,0:T(8,128)S(1)}, f32[224,128]{1,0:T(8,128)S(1)}, u32[]{:S(2)}, u32[]{:S(2)}) collective-permute-start(f32[224,128]{1,0:T(8,128)S(1)} %get-tuple-element.35), channel_id=1, source_target_pairs={{1,0},{2,1},{3,2},{4,3},{5,4},{6,5},{7,6},{9,8},{10,9},{11,10},{12... | collective-permute-start | bytes 344072 | tf_op jit(solution)/shard_map/ppermute | solution.py:440
  45.0 3.1 %collective-permute-start.5 = (f32[278,128]{1,0:T(8,128)S(1)}, f32[278,128]{1,0:T(8,128)S(1)}, u32[]{:S(2)}, u32[]{:S(2)}) collective-permute-start(f32[278,128]{1,0:T(8,128)S(1)} %get-tuple-element.47.own), channel_id=1, source_target_pairs={{0,8},{8,0},{16,24},{24,16},{32,40},{40,32},{48,56},{56,48},{64,72... | collective-permute-start | bytes 427016 | tf_op jit(solution)/shard_map/ppermute | solution.py:437
  45.1 8.5 %collective-permute-start.4 = (f32[278,128]{1,0:T(8,128)S(1)}, f32[278,128]{1,0:T(8,128)S(1)}, u32[]{:S(2)}, u32[]{:S(2)}) collective-permute-start(f32[278,128]{1,0:T(8,128)S(1)} %get-tuple-element.47.own), channel_id=1, source_target_pairs={{8,16},{24,32},{40,48},{56,64},{72,80},{88,96},{104,112},{120,128}... | collective-permute-start | bytes 427016 | tf_op jit(solution)/shard_map/ppermute | solution.py:437
  62.4 2.9 %collective-permute-start.7 = (f32[150,128]{1,0:T(8,128)S(1)}, f32[150,128]{1,0:T(8,128)S(1)}, u32[]{:S(2)}, u32[]{:S(2)}) collective-permute-start(f32[150,128]{1,0:T(8,128)S(1)} %get-tuple-element.55.own), channel_id=1, source_target_pairs={{0,8},{8,0},{16,24},{24,16},{32,40},{40,32},{48,56},{56,48},{64,72... | collective-permute-start | bytes 230408 | tf_op jit(solution)/shard_map/ppermute | solution.py:437
  62.5 7.8 %collective-permute-start.6 = (f32[150,128]{1,0:T(8,128)S(1)}, f32[150,128]{1,0:T(8,128)S(1)}, u32[]{:S(2)}, u32[]{:S(2)}) collective-permute-start(f32[150,128]{1,0:T(8,128)S(1)} %get-tuple-element.55.own), channel_id=1, source_target_pairs={{8,16},{24,32},{40,48},{56,64},{72,80},{88,96},{104,112},{120,128}... | collective-permute-start | bytes 230408 | tf_op jit(solution)/shard_map/ppermute | solution.py:437
  70.9 6.2 %collective-permute-start.8 = (f32[64,128]{1,0:T(8,128)S(1)}, f32[64,128]{1,0:T(8,128)S(1)}, u32[]{:S(2)}, u32[]{:S(2)}) collective-permute-start(f32[64,128]{1,0:T(8,128)S(1)} %get-tuple-element.58), channel_id=1, source_target_pairs={{0,1},{1,2},{2,3},{3,4},{4,5},{5,6},{6,7},{8,9},{9,10},{10,11},{11... | collective-permute-start | bytes 98312 | tf_op jit(solution)/shard_map/ppermute | solution.py:440
  75.0 11.9 %collective-permute-start.9 = (f32[64,128]{1,0:T(8,128)S(1)}, f32[64,128]{1,0:T(8,128)S(1)}, u32[]{:S(2)}, u32[]{:S(2)}) collective-permute-start(f32[64,128]{1,0:T(8,128)S(1)} %get-tuple-element.59), channel_id=1, source_target_pairs={{1,0},{2,1},{3,2},{4,3},{5,4},{6,5},{7,6},{9,8},{10,9},{11,10},{12... | collective-permute-start | bytes 98312 | tf_op jit(solution)/shard_map/ppermute | solution.py:440
  96.2 2.7 %collective-permute-start.11 = (f32[150,128]{1,0:T(8,128)S(1)}, f32[150,128]{1,0:T(8,128)S(1)}, u32[]{:S(2)}, u32[]{:S(2)}) collective-permute-start(f32[150,128]{1,0:T(8,128)S(1)} %get-tuple-element.60.own), channel_id=1, source_target_pairs={{0,8},{8,0},{16,24},{24,16},{32,40},{40,32},{48,56},{56,48},{64,72... | collective-permute-start | bytes 230408 | tf_op jit(solution)/shard_map/ppermute | solution.py:437
  96.2 7.8 %collective-permute-start.10 = (f32[150,128]{1,0:T(8,128)S(1)}, f32[150,128]{1,0:T(8,128)S(1)}, u32[]{:S(2)}, u32[]{:S(2)}) collective-permute-start(f32[150,128]{1,0:T(8,128)S(1)} %get-tuple-element.60.own), channel_id=1, source_target_pairs={{8,16},{24,32},{40,48},{56,64},{72,80},{88,96},{104,112},{120,128}... | collective-permute-start | bytes 230408 | tf_op jit(solution)/shard_map/ppermute | solution.py:437

commit v2 on v1

v2 whole, which is shorter than its diff:
```python
import functools
import math

import jax
import jax.numpy as jnp
import ml_dtypes
import numpy as np
from jax import lax
from jax.experimental import pallas as pl
from jax.experimental.pallas import tpu as pltpu
from jax.sharding import PartitionSpec as P

H = 32
KS = 64
ITERS = 3
ROWS = 128
sharpness = 2.0
steepness = 4.0
threshold = 0.8
step_size = 1.0
f32 = jnp.float32
bf16 = jnp.bfloat16
VMEM_LIMIT = 28 * 1024 * 1024


def up(value, unit):
    return -(-value // unit) * unit


def halves(table):
    table = table.astype(np.float32)
    high = table.astype(ml_dtypes.bfloat16)
    low = (table - high.astype(np.float32)).astype(ml_dtypes.bfloat16)
    return high, low


def angles(left, right, length):
    product = np.outer(left.astype(np.int64), right.astype(np.int64)) % length
    return product * (2.0 * math.pi / length)


def grown(table, rows, cols):
    return np.pad(table, [(0, rows - table.shape[0]), (0, cols - table.shape[1])])


def left_stack(table):
    high, low = halves(table)
    return np.concatenate([high, high, low], 1)


def right_stack(table):
    high, low = halves(table)
    return np.concatenate([high, high, low], 0)


class Geometry:
    def __init__(self, width):
        self.mask = width
        self.field = width - 2 * H
        self.grad = width - 4 * H
        self.length = width | 1
        self.freqs = (self.length + 1) // 2
        self.freqs_up = up(self.freqs, 16)
        self.mask_up = up(self.mask, 16)
        self.half = self.field // 2
        self.half_up = up(self.half, 16)
        self.grad_up = up(self.grad, 32)

    def tables(self):
        freq = np.arange(self.freqs)
        fu, hu = self.freqs_up, self.half_up
        middle = H + (self.field - 1) / 2.0
        weight = np.where(freq == 0, 1.0, 2.0) / (self.length * ROWS)

        def phases(places):
            return angles(freq, np.round(2 * places), 2 * self.length)

        def complex_table(phase, sign, rows, cols, axis):
            parts = [grown(np.cos(phase), rows, cols), grown(sign * np.sin(phase), rows, cols)]
            return np.concatenate(parts, axis)

        mask = phases(np.arange(self.mask) - middle)
        half = phases(np.arange(self.half) + 0.5)
        grad = phases(np.arange(self.grad) + 2 * H - middle)
        taps = phases(np.arange(KS) - H)
        grad_table = np.concatenate(
            [
                grown((np.cos(grad) * weight[:, None]).T, self.grad_up, fu),
                grown((-np.sin(grad) * weight[:, None]).T, self.grad_up, fu),
            ],
            1,
        )
        return dict(
            mask_cols=left_stack(complex_table(mask, -1.0, fu, self.mask_up, 0)),
            field_even=left_stack(grown((np.cos(half) * weight[:, None]).T, hu, fu)),
            field_odd=left_stack(grown((np.sin(half) * weight[:, None]).T, hu, fu)),
            source_even=left_stack(grown(np.cos(half), fu, hu)),
            source_odd=left_stack(grown(-np.sin(half), fu, hu)),
            grad_cols=left_stack(grad_table),
            tap_cols=left_stack(complex_table(taps, 1.0, fu, KS, 1)),
        )


def row_tables():
    freq = np.arange(ROWS)

    def complex_table(phase, sign):
        cos, sin = np.cos(phase), sign * np.sin(phase)
        return np.block([[cos, sin], [-sin, cos]])

    def side(table):
        high, low = halves(table)
        return np.concatenate([high, low], 1)

    places = np.arange(64) + H
    field = complex_table(angles(freq, places, ROWS), 1.0)
    field_swapped = np.concatenate([field[:, 64:], field[:, :64]], 1)
    source = complex_table(angles(np.arange(64), freq, ROWS), -1.0)
    source_swapped = np.concatenate([source[64:], source[:64]], 0)
    taps = angles(np.arange(KS) - H, freq, ROWS)
    tap = np.concatenate([np.cos(taps), -np.sin(taps)], 1)
    zero = np.zeros_like(tap)
    return dict(
        mask_rows=right_stack(complex_table(angles(freq, freq, ROWS), -1.0)),
        field_rows=side(field),
        field_rows_swapped=side(field_swapped),
        source_rows=right_stack(source),
        source_rows_swapped=right_stack(source_swapped),
        grad_rows=right_stack(complex_table(angles(freq, freq - H, ROWS), 1.0)),
        tap_rows=right_stack(np.block([[tap, zero], [zero, tap]])),
    )


def split(value):
    high = value.astype(bf16)
    return high, (value - high.astype(f32)).astype(bf16)


def dot(left, right):
    return lax.dot_general(
        left, right, (((1,), (0,)), ((), ())), preferred_element_type=f32
    )


def left_dot(table, value):
    high, low = split(value)
    return dot(table, jnp.concatenate([high, low, high], 0))


def right_dot(value, table):
    high, low = split(value)
    return dot(jnp.concatenate([high, low, high], 1), table)


def sigmoid(value):
    return 1.0 / (1.0 + jnp.exp(-value))


def swap_halves(value):
    return pltpu.roll(value, 64, 1)


def window(shape, first_col, first_row, whole_cols, whole_rows):
    col = lax.broadcasted_iota(jnp.int32, shape, 0) + first_col
    row = lax.broadcasted_iota(jnp.int32, shape, 1) + first_row
    return (col >= 0) & (col < whole_cols) & (row >= 0) & (row < whole_rows)


def setup_kernel(geos, held, kern_real, kern_imag, tap_rows, *rest):
    tables, rest = rest[: len(geos)], rest[len(geos) :]
    sources, rest = rest[:held], rest[held:]
    outs, rest = rest[: len(geos)], rest[len(geos) :]
    targets, (scratch, sems) = rest[:held], rest[held:]
    copies = [
        pltpu.make_async_copy(source, target, sems.at[index])
        for index, (source, target) in enumerate(zip(sources, targets))
    ]
    for copy in copies:
        copy.start()
    kernels = kern_real.shape[1] // KS
    both = jnp.concatenate([kern_real[...], kern_imag[...]], 0)
    for start in range(0, both.shape[1], 128):
        part = both[:, start : start + 128].T
        scratch[start : start + 128, :] = right_dot(part, tap_rows[...])
    for k in range(kernels):
        half = scratch[k * KS : (k + 1) * KS, :]
        turned = jnp.concatenate(
            [half[:, 128:256], -half[:, 0:128], half[:, 384:512], -half[:, 256:384]], 1
        )
        high, low = split(jnp.concatenate([half, turned], 0))
        stacked = jnp.concatenate([high, low, high], 0)
        for geo, table, out in zip(geos, tables, outs):
            spec = dot(table[...], stacked)
            count = geo.freqs_up
            out[2 * k * count : (2 * k + 1) * count, :] = spec[:, :256]
            out[(2 * k + 1) * count : (2 * k + 2) * count, :] = spec[:, 256:]
    for copy in copies:
        copy.wait()


def one_step(geo, mask, target, inside, weights, spec, tabs, fields):
    count = geo.freqs_up
    group = weights.shape[0]
    kernels = weights.shape[0]
    lane = lax.broadcasted_iota(jnp.int32, (count, 128), 1) < 64
    across = left_dot(tabs["mask_cols"][...], mask)
    mask_spec = right_dot(
        jnp.concatenate([across[:count], across[count:]], 1), tabs["mask_rows"][...]
    )
    mask_re, mask_im = mask_spec[:, :128], mask_spec[:, 128:]

    def product(index):
        place = spec[index * count : (index + 1) * count, :]
        re, im = place[:, :128], place[:, 128:]
        return jnp.concatenate(
            [re * mask_re - im * mask_im, re * mask_im + im * mask_re], 1
        )

    def down(indices, table):
        high, low = split(jnp.concatenate([product(i) for i in indices], 0))
        wide = dot(high, table[...])
        got = wide[:, :128] + wide[:, 128:] + dot(low, table[:, :128])
        return [got[i * count : (i + 1) * count] for i in range(len(indices))]

    zero = jnp.zeros((geo.half_up, 128), f32)
    intensity = [zero, zero]
    for k in range(0, kernels, group):
        ks = range(k, k + group)
        firsts = down([2 * j for j in ks], tabs["field_rows"])
        seconds = down([2 * j + 1 for j in ks], tabs["field_rows_swapped"])
        evens = [jnp.where(lane, a, b) for a, b in zip(firsts, seconds)]
        odds = [swap_halves(jnp.where(lane, b, a)) for a, b in zip(firsts, seconds)]
        even = left_dot(tabs["field_even"][...], jnp.concatenate(evens, 1))
        odd = left_dot(tabs["field_odd"][...], jnp.concatenate(odds, 1))
        for side, field in enumerate((even - odd, even + odd)):
            for j in range(group):
                own = field[:, j * 128 : (j + 1) * 128]
                fields[side, k + j] = own
                intensity[side] = intensity[side] + weights[k + j] * (own * own)
    cotangent = []
    for side in (0, 1):
        intensity[side] = intensity[side] + swap_halves(intensity[side])
        resist = sigmoid(steepness * (intensity[side] - threshold))
        slope = 2.0 * (resist - target[side]) * steepness * resist * (1.0 - resist)
        cotangent.append(jnp.where(inside[side], slope, 0.0))
    total_re = jnp.zeros((count, 128), f32)
    total_im = jnp.zeros((count, 128), f32)
    for k in range(0, kernels, group):
        ks = range(k, k + group)
        right, left = (
            jnp.concatenate(
                [(2.0 * weights[j] * cotangent[side]) * fields[side, j] for j in ks],
                1,
            )
            for side in (0, 1)
        )
        even = left_dot(tabs["source_even"][...], right + left)
        odd = left_dot(tabs["source_odd"][...], right - left)
        res = [even[:, j * 128 : (j + 1) * 128] for j in range(group)]
        ims = [swap_halves(odd[:, j * 128 : (j + 1) * 128]) for j in range(group)]
        for index, values, table in (
            (0, [jnp.where(lane, a, b) for a, b in zip(res, ims)], tabs["source_rows"]),
            (1, [jnp.where(lane, b, a) for a, b in zip(res, ims)], tabs["source_rows_swapped"]),
        ):
            got = right_dot(jnp.concatenate(values, 0), table[...])
            for j in range(group):
                got_re, got_im = (
                    got[j * count : (j + 1) * count, :128],
                    got[j * count : (j + 1) * count, 128:],
                )
                start = (2 * (k + j) + index) * count
                place = spec[start : start + count, :]
                re_k, im_k = place[:, :128], place[:, 128:]
                total_re = total_re + (re_k * got_re + im_k * got_im)
                total_im = total_im + (re_k * got_im - im_k * got_re)
    back = right_dot(jnp.concatenate([total_re, total_im], 1), tabs["grad_rows"][...])
    grad = left_dot(
        tabs["grad_cols"][...], jnp.concatenate([back[:, :128], back[:, 128:]], 0)
    )
    return intensity, grad


COLUMN_TABLES = (
    "mask_cols",
    "field_even",
    "field_odd",
    "source_even",
    "source_odd",
    "grad_cols",
)
ROW_TABLES = (
    "mask_rows",
    "field_rows",
    "field_rows_swapped",
    "source_rows",
    "source_rows_swapped",
    "grad_rows",
)
STEP_TABLES = COLUMN_TABLES + ROW_TABLES


def lanes(shape):
    return lax.broadcasted_iota(jnp.int32, shape, 1) < 64


def early_kernel(own, bits, params, target, tall):
    cols = own.shape[1]
    tall[...] = jnp.zeros_like(tall)
    tall[32:96, :cols] = own[...]
    params[...] = tall[...].T[:cols]
    col = lax.broadcasted_iota(jnp.int32, (64, tall.shape[1]), 1)
    word = jnp.zeros_like(col)
    for index in range(bits.shape[1]):
        word = jnp.where(col // 30 == index, bits[:, index : index + 1], word)
    bit = jnp.bitwise_and(jnp.right_shift(word, col % 30), 1).astype(f32)
    target[...] = jnp.concatenate([bit, bit], 0).T[:cols]


def prep_kernel(place, own, target, across, within, params, to_first, to_second, tall):
    even = place[0] % 2 == 0
    cols = own.shape[0]
    tall[...] = jnp.zeros_like(tall)
    tall[0:32, :cols] = jnp.where(even, across[32:64, :], within[32:64, :])
    tall[96:128, :cols] = jnp.where(even, within[0:32, :], across[0:32, :])
    params[...] = own[...] + tall[...].T[:cols]
    right = place[1] % 2 == 0
    left_lanes = lanes((48, 128))

    def packed(start):
        return jnp.where(left_lanes, target[start : start + 48], target[start + 48 : start + 96])

    to_left = jnp.concatenate([params[0:128, :], packed(0)], 0)
    to_right = jnp.concatenate([params[cols - 128 : cols, :], packed(cols - 96)], 0)
    to_first[...] = jnp.where(right, to_right, to_left)
    to_second[...] = jnp.where(right, to_left, to_right)


def spread_out(place, grad, spread, to_far, to_near):
    even = place[0] % 2 == 0
    half = to_far.shape[0]
    spread[...] = grad
    turned = swap_halves(grad)
    straight = jnp.where(even, grad, turned)
    crossed = jnp.where(even, turned, grad)
    left_lanes = lanes((half, 128))
    to_far[...] = jnp.where(left_lanes, straight[:half], crossed[half:])
    to_near[...] = jnp.where(left_lanes, crossed[:half], straight[half:])


def gathered(place, spread, far, near):
    even = place[0] % 2 == 0
    far, near = far[...], near[...]
    left_lanes = lanes(far.shape)
    far_turned, near_turned = swap_halves(far), swap_halves(near)
    straight = jnp.concatenate(
        [jnp.where(left_lanes, far, near_turned), jnp.where(left_lanes, far_turned, near)], 0
    )
    crossed = jnp.concatenate(
        [jnp.where(left_lanes, near, far_turned), jnp.where(left_lanes, near_turned, far)], 0
    )
    return spread[...] + jnp.where(even, straight, crossed)


def stepped(params, grad):
    field = sigmoid(sharpness * params)
    return params - step_size * sharpness * field * (1.0 - field) * grad


def masked(place, tile, whole, params, col_offset):
    first_col = place[1] * tile[1] + col_offset
    first_row = place[0] * tile[0] - H
    inside = window(params.shape, first_col, first_row, whole[1], whole[0])
    return jnp.where(inside, sigmoid(sharpness * params), 0.0)


def field_window(geo, place, tile, whole, col_offset):
    middle = place[1] * tile[1] + col_offset + H + geo.half
    step = lax.broadcasted_iota(jnp.int32, (geo.half_up, 128), 0)
    return [(col >= 0) & (col < whole[1]) for col in (middle + step, middle - 1 - step)]


def first_kernel(
    geo, tile, whole, place, weights, own, target, first, second, spec, mirror, *rest
):
    tabs = dict(zip(STEP_TABLES, rest))
    rest = rest[len(STEP_TABLES) :]
    spread, to_far, to_near, params_out, goal_out, params, goal, fields = rest
    cols = own.shape[0]
    right_first = place[1] % 2 == 0
    left = jnp.where(right_first, second[...], first[...])
    right = jnp.where(right_first, first[...], second[...])
    params[...] = jnp.zeros_like(params)
    params[0:128, :] = left[0:128, :]
    params[128 : 128 + cols, :] = own[...]
    params[128 + cols : 256 + cols, :] = right[0:128, :]
    left_lanes = lanes((48, 128))
    goal[...] = jnp.zeros_like(goal)
    for start, side in ((0, left), (96 + cols, right)):
        packed = side[128:176, :]
        turned = swap_halves(packed)
        goal[start : start + 48, :] = jnp.where(left_lanes, packed, turned)
        goal[start + 48 : start + 96, :] = jnp.where(left_lanes, turned, packed)
    goal[96 : 96 + cols, :] = target[...]
    goals = [
        goal[geo.half : geo.half + geo.half_up, :],
        dot(mirror[...], goal[0 : mirror.shape[1], :].astype(bf16)),
    ]
    for side in (0, 1):
        goal_out[side] = goals[side][: goal_out.shape[1]]
    params_out[...] = params[64 : 64 + params_out.shape[0], :]
    mask = masked(place, tile, whole, params[...], -128)
    inside = field_window(geo, place, tile, whole, -128)
    _, grad = one_step(geo, mask, goals, inside, weights, spec, tabs, fields)
    spread_out(place, grad, spread, to_far, to_near)


def second_kernel(geo, tile, whole, place, weights, own, far, near, old, goal, spec, *rest):
    tabs = dict(zip(STEP_TABLES, rest))
    spread, to_far, to_near, params_out, fields = rest[len(STEP_TABLES) :]
    params = stepped(old[...], gathered(place, own, far, near))
    params_out[...] = params[64 : 64 + params_out.shape[0], :]
    mask = masked(place, tile, whole, params, -64)
    inside = field_window(geo, place, tile, whole, -64)
    goals = [goal[0], goal[1]]
    _, grad = one_step(geo, mask, goals, inside, weights, spec, tabs, fields)
    spread_out(place, grad, spread, to_far, to_near)


def update_kernel(cols, place, own, far, near, old, params, to_first, to_second):
    params[...] = stepped(old[...], gathered(place, own, far, near))
    right = place[1] % 2 == 0
    to_left, to_right = params[0:64, :], params[cols - 64 : cols, :]
    to_first[...] = jnp.where(right, to_right, to_left)
    to_second[...] = jnp.where(right, to_left, to_right)


def third_kernel(
    geo, tile, whole, place, weights, own, first, second, goal, spec, mirror, *rest
):
    tabs = dict(zip(STEP_TABLES, rest))
    rest = rest[len(STEP_TABLES) :]
    spread, to_far, to_near, intensity_out, params, flat, fields = rest
    cols = tile[1]
    right_first = place[1] % 2 == 0
    params[...] = jnp.zeros_like(params)
    params[0:64, :] = jnp.where(right_first, second[...], first[...])
    params[64 : 64 + cols, :] = own[0:cols, :]
    params[64 + cols : 128 + cols, :] = jnp.where(right_first, first[...], second[...])
    mask = masked(place, tile, whole, params[...], -64)
    inside = field_window(geo, place, tile, whole, -64)
    goals = [goal[0], goal[1]]
    intensity, grad = one_step(geo, mask, goals, inside, weights, spec, tabs, fields)
    spread_out(place, grad, spread, to_far, to_near)
    high, low = split(intensity[1])
    rest = (intensity[1] - high.astype(f32) - low.astype(f32)).astype(bf16)
    turned = dot(mirror[...], high) + (dot(mirror[...], low) + dot(mirror[...], rest))
    flat[...] = jnp.zeros_like(flat)
    flat[0 : cols // 2, :] = turned[0 : cols // 2]
    flat[cols // 2 : cols, :] = intensity[0][0 : cols // 2]
    intensity_out[...] = flat[...].T[:64, :cols]


def final_kernel(cols, place, own, far, near, out, wide):
    wide[...] = jnp.zeros_like(wide)
    wide[0 : own.shape[0], :] = gathered(place, own, far, near)
    out[...] = wide[...].T[H : H + 64, :cols]


def mirror_table(rows, rows_up, cols_up):
    table = np.zeros((rows_up, cols_up), np.float32)
    table[np.arange(rows), rows - 1 - np.arange(rows)] = 1.0
    return table.astype(ml_dtypes.bfloat16)


def call(kernel, name, out_shapes, scratch, args, scalars):
    args = args[:scalars] + [
        pltpu.with_memory_space_constraint(arg, pltpu.VMEM) for arg in args[scalars:]
    ]
    specs = [pl.BlockSpec(memory_space=pltpu.SMEM)] * scalars
    specs += [pl.BlockSpec(memory_space=pltpu.VMEM)] * (len(args) - scalars)
    return pl.pallas_call(
        kernel,
        name=name,
        out_shape=[
            shape if isinstance(shape, jax.ShapeDtypeStruct) else pltpu.VMEM(shape, f32)
            for shape in out_shapes
        ],
        in_specs=specs,
        out_specs=[pl.BlockSpec(memory_space=pltpu.VMEM)] * len(out_shapes),
        scratch_shapes=[pltpu.VMEM(shape, f32) for shape in scratch],
        compiler_params=pltpu.CompilerParams(vmem_limit_bytes=VMEM_LIMIT),
    )(*args)


def per_device(rows, cols, mask_params, target_bits, kern_real, kern_imag, socs_weights):
    tile = mask_params.shape
    whole = (tile[0] * rows, tile[1] * cols)
    kernels = kern_real.shape[1] // KS
    place = jnp.stack([lax.axis_index("row"), lax.axis_index("col")]).astype(jnp.int32)

    def swaps(count, start):
        pairs = [(i, i + 1) for i in range(start, count - 1, 2)]
        return pairs + [(b, a) for a, b in pairs]

    def row_exchange(to_far, to_near):
        far = lax.ppermute(to_far, "row", swaps(rows, 1))
        return far, lax.ppermute(to_near, "row", swaps(rows, 0))

    def col_exchange(to_first, to_second):
        first = lax.ppermute(to_first, "col", swaps(cols, 0))
        return first, lax.ppermute(to_second, "col", swaps(cols, 1))

    wide, slim = Geometry(tile[1] + 8 * H), Geometry(tile[1] + 4 * H)
    shared = row_tables()
    shared["wide_mirror"] = mirror_table(wide.half, wide.half_up, wide.half_up)
    shared["slim_mirror"] = mirror_table(tile[1] // 2, up(tile[1] // 2, 16), slim.half_up)
    made = {"wide": wide.tables(), "slim": slim.tables(), "shared": shared}
    n = tile[1]
    far, near = row_exchange(mask_params, mask_params)
    params, target = call(
        early_kernel,
        "early",
        [(n, 128), (n, 128)],
        [(128, 256)],
        [mask_params, target_bits],
        0,
    )
    params, to_first, to_second = call(
        prep_kernel,
        "prep",
        [(n, 128), (176, 128), (176, 128)],
        [(128, 256)],
        [place, params, target, far, near],
        1,
    )
    first, second = col_exchange(to_first, to_second)
    names = [(label, name) for label in ("wide", "slim") for name in COLUMN_TABLES]
    names += [("shared", name) for name in ROW_TABLES + ("wide_mirror", "slim_mirror")]
    tables = [jnp.asarray(made[label][name]) for label, name in names]
    inputs = [
        kern_real,
        kern_imag,
        jnp.asarray(shared["tap_rows"]),
        jnp.asarray(made["wide"]["tap_cols"]),
        jnp.asarray(made["slim"]["tap_cols"]),
    ]
    wide_spec, slim_spec, *held = pl.pallas_call(
        functools.partial(setup_kernel, (wide, slim), len(tables)),
        name="spectra",
        out_shape=[
            pltpu.VMEM((2 * kernels * geo.freqs_up, 256), f32) for geo in (wide, slim)
        ]
        + [pltpu.VMEM(table.shape, table.dtype) for table in tables],
        in_specs=[pl.BlockSpec(memory_space=pltpu.VMEM)] * len(inputs)
        + [pl.BlockSpec(memory_space=pltpu.HBM)] * len(tables),
        out_specs=[pl.BlockSpec(memory_space=pltpu.VMEM)] * (2 + len(tables)),
        scratch_shapes=[
            pltpu.VMEM((kernels * KS, 512), f32),
            pltpu.SemaphoreType.DMA((len(tables),)),
        ],
        compiler_params=pltpu.CompilerParams(vmem_limit_bytes=VMEM_LIMIT),
    )(*[pltpu.with_memory_space_constraint(arg, pltpu.HBM) for arg in inputs + tables])
    place_of = {key: table for key, table in zip(names, held)}

    def tabs(label):
        return [place_of[label, name] for name in COLUMN_TABLES] + [
            place_of["shared", name] for name in ROW_TABLES
        ]

    def spreads(geo):
        return [(geo.grad_up, 128)] + [(geo.grad_up // 2, 128)] * 2

    def fields(geo):
        return (2, kernels, geo.half_up, 128)

    spread, to_far, to_near, params, goal = call(
        functools.partial(first_kernel, wide, tile, whole),
        "first",
        spreads(wide) + [(slim.mask_up, 128), (2, slim.half_up, 128)],
        [(wide.mask_up, 128), (wide.half + wide.half_up, 128), fields(wide)],
        [place, socs_weights, params, target, first, second, wide_spec]
        + [place_of["shared", "wide_mirror"], *tabs("wide")],
        2,
    )
    far, near = row_exchange(to_far, to_near)
    spread, to_far, to_near, params = call(
        functools.partial(second_kernel, slim, tile, whole),
        "second",
        spreads(slim) + [(slim.grad_up, 128)],
        [fields(slim)],
        [place, socs_weights, spread, far, near, params, goal, slim_spec, *tabs("slim")],
        2,
    )
    far, near = row_exchange(to_far, to_near)
    params, to_first, to_second = call(
        functools.partial(update_kernel, n),
        "update",
        [(slim.grad_up, 128), (64, 128), (64, 128)],
        [],
        [place, spread, far, near, params],
        1,
    )
    first, second = col_exchange(to_first, to_second)
    spread, to_far, to_near, intensity = call(
        functools.partial(third_kernel, slim, tile, whole),
        "third",
        spreads(slim) + [jax.ShapeDtypeStruct(tile, f32)],
        [(slim.mask_up, 128), (256, 128), fields(slim)],
        [place, socs_weights, params, first, second, goal, slim_spec]
        + [place_of["shared", "slim_mirror"], *tabs("slim")],
        2,
    )
    far, near = row_exchange(to_far, to_near)
    (mask_grad,) = call(
        functools.partial(final_kernel, n),
        "final",
        [jax.ShapeDtypeStruct(tile, f32)],
        [(256, 128)],
        [place, spread, far, near],
        1,
    )
    return mask_grad, intensity


def solution(mesh):
    placed = (P("row", "col"), P("row", "col"), P(), P(), P())
    return jax.shard_map(
        functools.partial(per_device, mesh.shape["row"], mesh.shape["col"]),
        mesh=mesh,
        in_specs=placed,
        out_specs=(P("row", "col"), P("row", "col")),
        check_vma=False,
    )
```

time: 106 us -> 81.9 us (0.77)
  waiting for transfers between devices: 34.3 us -> 15.3 us
  Pallas kernels: 39.6 us -> 28.8 us
  starting transfers between devices: 28.9 us -> 35 us
    ppermute x12, waiting for transfers between devices: 34.3 us -> 15.3 us  [the longest x4 10.1 us: row_exchange(): far = lax.ppermute(to_far, 'row', swaps(rows, 1))]
    pallas_call x6 -> x7, Pallas kernels: 33.5 us -> 23 us  [call(): pl.pallas_call(kernel, name=name, out_shape=[shape if isinstance(shape, j...]
    ppermute x12, starting transfers between devices: 28.9 us -> 35 us  [the longest x4 18 us: row_exchange(): far = lax.ppermute(to_far, 'row', swaps(rows, 1))]
  transfers between devices with their start and end apart: 12 -> 12, of which waited for: 6 -> 5; matrix products, arithmetic and copies ran while one was open for 1% -> 1% of each run, Pallas kernels for 6% -> 7%
where the time goes in v2:
time: 81.9 us; the launch traced here: 81.6 us
  starting transfers between devices  35 us (43%)
  Pallas kernels  28.8 us (35%)
  waiting for transfers between devices  15.3 us (19%)
  local copies, waits for them, and re-layouts  1.62 us (2%)
    pallas_call x7, Pallas kernels, call(): pl.pallas_call(kernel, name=name, out_shape=[shape if isinstance(shape, j...  23 us
    ppermute x4, starting transfers between devices, row_exchange(): far = lax.ppermute(to_far, 'row', swaps(rows, 1))  18 us
    ppermute x2, starting transfers between devices, col_exchange(): return (first, lax.ppermute(to_second, 'col', swaps(cols, 1)))  15.4 us
    ppermute x4, waiting for transfers between devices, row_exchange(): far = lax.ppermute(to_far, 'row', swaps(rows, 1))  10.1 us
    pallas_call x1, Pallas kernels, per_device(): pl.pallas_call(functools.partial(setup_kernel, (wide, slim), len(tables))...  5.77 us
    ppermute x2, waiting for transfers between devices, col_exchange(): return (first, lax.ppermute(to_second, 'col', swaps(cols, 1)))  5.19 us
  transfers between devices with their start and end apart: 12, of which 5 were waited for; matrix products, arithmetic and copies ran while one was open for 1% of the time, Pallas kernels for 7%

profile of v2, /device:TPU:38, one launch (start us, length us, event | category | flops | bytes accessed | tf_op | source)
XLA Modules:
  0.0 81.6 jit_solution(11405042847713834622)
XLA Ops:
  0.6 0.1 collective-permute-start.1
  0.7 4.6 %collective-permute-start = (f32[64,150]{1,0:T(8,128)}, f32[64,150]{1,0:T(8,128)S(1)}, u32[]{:S(2)}, u32[]{:S(2)}) collective-permute-start(f32[64,150]{1,0:T(8,128)} %own.1), channel_id=1, source_target_pairs={{8,16},{24,32},{40,48},{56,64},{72,80},{88,96},{104,112},{120,128}... | collective-permute-start | bytes 115208 | tf_op jit(solution)/shard_map/ppermute | solution.py:506
  5.3 0.1 pad_add_fusion.place
  5.4 0.8 copy.30.bits
  6.2 0.0 copy-start
  6.2 0.8 %copy-done = f32[64,150]{1,0:T(8,128)S(1)} copy-done((f32[64,150]{1,0:T(8,128)S(1)}, f32[64,150]{1,0:T(8,128)}, u32[]{:S(2)}) %copy-start) | copy-done | bytes 38424
  7.0 0.0 copy-start.1
  7.0 0.2 early.1
  7.2 0.0 collective-permute-done.1.within
  7.2 1.4 %collective-permute-done.across = f32[64,150]{1,0:T(8,128)S(1)} collective-permute-done((f32[64,150]{1,0:T(8,128)}, f32[64,150]{1,0:T(8,128)S(1)}, u32[]{:S(2)}, u32[]{:S(2)}) %collective-permute-start) | collective-permute-done | bytes 38432 | tf_op jit(solution)/shard_map/ppermute | solution.py:506
  8.6 0.7 prep.1
  9.3 0.9 %collective-permute-start.2 = (f32[176,128]{1,0:T(8,128)S(1)}, f32[176,128]{1,0:T(8,128)S(1)}, u32[]{:S(2)}, u32[]{:S(2)}) collective-permute-start(f32[176,128]{1,0:T(8,128)S(1)} %get-tuple-element.48), channel_id=1, source_target_pairs={{0,1},{2,3},{4,5},{6,7},{1,0},{3,2},{5,4},{7,6},{8,9},{10,11},{12,... | collective-permute-start | bytes 270344 | tf_op jit(solution)/shard_map/ppermute | solution.py:510
  10.2 8.8 %collective-permute-start.3 = (f32[176,128]{1,0:T(8,128)S(1)}, f32[176,128]{1,0:T(8,128)S(1)}, u32[]{:S(2)}, u32[]{:S(2)}) collective-permute-start(f32[176,128]{1,0:T(8,128)S(1)} %get-tuple-element.49), channel_id=1, source_target_pairs={{1,2},{3,4},{5,6},{2,1},{4,3},{6,5},{9,10},{11,12},{13,14},{10,9},... | collective-permute-start | bytes 270344 | tf_op jit(solution)/shard_map/ppermute | solution.py:511
  19.0 5.8 %spectra.1 = (f32[4992,256]{1,0:T(8,128)S(1)}, f32[3456,256]{1,0:T(8,128)S(1)}, bf16[416,1248]{1,0:T(8,128)(2,1)S(1)}, bf16[176,624]{1,0:T(8,128)(2,1)S(1)}, bf1...) custom-call(f32[64,768]{1,0:T(8,128)} %kern_real.1, ...), custom_call_target="tpu_custom_call" | custom-call | tf_op jit(solution)/shard_map/spectra/pallas_call | solution.py:547
  24.8 0.0 collective-permute-done.2.first
  24.8 0.0 collective-permute-done.3.second
  24.8 0.0 copy-done.1
  24.8 8.7 %first.1 = (f32[288,128]{1,0:T(8,128)S(1)}, f32[144,128]{1,0:T(8,128)S(1)}, f32[144,128]{1,0:T(8,128)S(1)}, f32[288,128]{1,0:T(8,128)S(1)}, f32[2,112,128]{2,1,0:T(8,128)S(1)}) custom-call(s32[2]{0:T(128)S(1)} %pad_add_fusion.place, f32[12]{0:T(128)S(1)} %copy-done.1, f32[150,128]{1,0:T(8,128)S(1)} %get-tuple-element.47.own, ...), custom_call_target="tpu_custom_call" | custom-call | tf_op jit(solution)/shard_map/first/pallas_call | solution.py:481
  33.5 4.9 %collective-permute-start.4 = (f32[144,128]{1,0:T(8,128)S(1)}, f32[144,128]{1,0:T(8,128)S(1)}, u32[]{:S(2)}, u32[]{:S(2)}) collective-permute-start(f32[144,128]{1,0:T(8,128)S(1)} %get-tuple-element.65), channel_id=1, source_target_pairs={{8,16},{24,32},{40,48},{56,64},{72,80},{88,96},{104,112},{120,128}... | collective-permute-start | bytes 221192 | tf_op jit(solution)/shard_map/ppermute | solution.py:506
  38.4 0.3 collective-permute-start.5
  38.7 2.6 %collective-permute-done.4.far = f32[144,128]{1,0:T(8,128)S(1)} collective-permute-done((f32[144,128]{1,0:T(8,128)S(1)}, f32[144,128]{1,0:T(8,128)S(1)}, u32[]{:S(2)}, u32[]{:S(2)}) %collective-permute-start.4) | collective-permute-done | bytes 73760 | tf_op jit(solution)/shard_map/ppermute | solution.py:506
  41.3 0.0 collective-permute-done.5.near
  41.3 5.4 %second.1 = (f32[160,128]{1,0:T(8,128)S(1)}, f32[80,128]{1,0:T(8,128)S(1)}, f32[80,128]{1,0:T(8,128)S(1)}, f32[160,128]{1,0:T(8,128)S(1)}) custom-call(s32[2]{0:T(128)S(1)} %pad_add_fusion.place, f32[12]{0:T(128)S(1)} %copy-done.1, f32[288,128]{1,0:T(8,128)S(1)} %get-tuple-element.64.own, f32[144,128]{1,0:T(8,128)S(1)} %collective-permute-done.4.far, ...), custom_call_target="tpu_custom_call" | custom-call | tf_op jit(solution)/shard_map/second/pallas_call | solution.py:481
  46.8 4.9 %collective-permute-start.6 = (f32[80,128]{1,0:T(8,128)S(1)}, f32[80,128]{1,0:T(8,128)S(1)}, u32[]{:S(2)}, u32[]{:S(2)}) collective-permute-start(f32[80,128]{1,0:T(8,128)S(1)} %get-tuple-element.77), channel_id=1, source_target_pairs={{8,16},{24,32},{40,48},{56,64},{72,80},{88,96},{104,112},{120,128}... | collective-permute-start | bytes 122888 | tf_op jit(solution)/shard_map/ppermute | solution.py:506
  51.6 0.1 collective-permute-start.7
  51.7 2.4 %collective-permute-done.6.far = f32[80,128]{1,0:T(8,128)S(1)} collective-permute-done((f32[80,128]{1,0:T(8,128)S(1)}, f32[80,128]{1,0:T(8,128)S(1)}, u32[]{:S(2)}, u32[]{:S(2)}) %collective-permute-start.6) | collective-permute-done | bytes 40992 | tf_op jit(solution)/shard_map/ppermute | solution.py:506
  54.2 0.0 collective-permute-done.7.near
  54.2 0.6 update.1
  54.8 0.1 collective-permute-start.8
  54.9 6.6 %collective-permute-start.9 = (f32[64,128]{1,0:T(8,128)S(1)}, f32[64,128]{1,0:T(8,128)S(1)}, u32[]{:S(2)}, u32[]{:S(2)}) collective-permute-start(f32[64,128]{1,0:T(8,128)S(1)} %get-tuple-element.82), channel_id=1, source_target_pairs={{1,2},{3,4},{5,6},{2,1},{4,3},{6,5},{9,10},{11,12},{13,14},{10,9},... | collective-permute-start | bytes 98312 | tf_op jit(solution)/shard_map/ppermute | solution.py:511
  61.6 0.0 collective-permute-done.8.first
  61.6 5.2 %collective-permute-done.9.second = f32[64,128]{1,0:T(8,128)S(1)} collective-permute-done((f32[64,128]{1,0:T(8,128)S(1)}, f32[64,128]{1,0:T(8,128)S(1)}, u32[]{:S(2)}, u32[]{:S(2)}) %collective-permute-start.9) | collective-permute-done | bytes 32800 | tf_op jit(solution)/shard_map/ppermute | solution.py:511
  66.8 6.0 %third.1 = (f32[160,128]{1,0:T(8,128)S(1)}, f32[80,128]{1,0:T(8,128)S(1)}, f32[80,128]{1,0:T(8,128)S(1)}, f32[64,150]{1,0:T(8,128)}) custom-call(s32[2]{0:T(128)S(1)} %pad_add_fusion.place, f32[12]{0:T(128)S(1)} %copy-done.1, f32[160,128]{1,0:T(8,128)S(1)} %get-tuple-element.80.own, f32[64,128]{1,0:T(8,128)S(1)} %collective-permute-done.8.first, ...), custom_call_target="tpu_custom_call" | custom-call | tf_op jit(solution)/shard_map/third/pallas_call | solution.py:481
  72.8 3.7 %collective-permute-start.10 = (f32[80,128]{1,0:T(8,128)S(1)}, f32[80,128]{1,0:T(8,128)S(1)}, u32[]{:S(2)}, u32[]{:S(2)}) collective-permute-start(f32[80,128]{1,0:T(8,128)S(1)} %get-tuple-element.85), channel_id=1, source_target_pairs={{8,16},{24,32},{40,48},{56,64},{72,80},{88,96},{104,112},{120,128}... | collective-permute-start | bytes 122888 | tf_op jit(solution)/shard_map/ppermute | solution.py:506
  76.5 0.1 collective-permute-start.11
  76.6 3.6 %collective-permute-done.10.far = f32[80,128]{1,0:T(8,128)S(1)} collective-permute-done((f32[80,128]{1,0:T(8,128)S(1)}, f32[80,128]{1,0:T(8,128)S(1)}, u32[]{:S(2)}, u32[]{:S(2)}) %collective-permute-start.10) | collective-permute-done | bytes 40992 | tf_op jit(solution)/shard_map/ppermute | solution.py:506
  80.2 0.0 collective-permute-done.11.near
  80.2 1.3 %final.1 = f32[64,150]{1,0:T(8,128)} custom-call(s32[2]{0:T(128)S(1)} %pad_add_fusion.place, f32[160,128]{1,0:T(8,128)S(1)} %get-tuple-element.84.own, f32[80,128]{1,0:T(8,128)S(1)} %collective-permute-done.10.far, f32[80,128]{1,0:T(8,128)S(1)} %collective-permute-done.11.near), custom_call_target="tpu_custom_call" | custom-call | tf_op jit(solution)/shard_map/final/pallas_call | solution.py:481
Async XLA Ops:
  0.6 6.6 %collective-permute-start.1 = (f32[64,150]{1,0:T(8,128)}, f32[64,150]{1,0:T(8,128)S(1)}, u32[]{:S(2)}, u32[]{:S(2)}) collective-permute-start(f32[64,150]{1,0:T(8,128)} %own.1), channel_id=1, source_target_pairs={{0,8},{16,24},{32,40},{48,56},{64,72},{80,88},{96,104},{112,120},{... | collective-permute-start | bytes 115208 | tf_op jit(solution)/shard_map/ppermute | solution.py:507
  0.7 7.9 %collective-permute-start = (f32[64,150]{1,0:T(8,128)}, f32[64,150]{1,0:T(8,128)S(1)}, u32[]{:S(2)}, u32[]{:S(2)}) collective-permute-start(f32[64,150]{1,0:T(8,128)} %own.1), channel_id=1, source_target_pairs={{8,16},{24,32},{40,48},{56,64},{72,80},{88,96},{104,112},{120,128}... | collective-permute-start | bytes 115208 | tf_op jit(solution)/shard_map/ppermute | solution.py:506
  6.2 0.8 %copy-start = (f32[64,150]{1,0:T(8,128)S(1)}, f32[64,150]{1,0:T(8,128)}, u32[]{:S(2)}) copy-start(f32[64,150]{1,0:T(8,128)} %own.1) | copy-start | bytes 115204
  7.0 17.8 %copy-start.1 = (f32[12]{0:T(128)S(1)}, f32[12]{0:T(128)}, u32[]{:S(2)}) copy-start(f32[12]{0:T(128)} %weights.5) | copy-start | bytes 148
  9.3 15.5 %collective-permute-start.2 = (f32[176,128]{1,0:T(8,128)S(1)}, f32[176,128]{1,0:T(8,128)S(1)}, u32[]{:S(2)}, u32[]{:S(2)}) collective-permute-start(f32[176,128]{1,0:T(8,128)S(1)} %get-tuple-element.48), channel_id=1, source_target_pairs={{0,1},{2,3},{4,5},{6,7},{1,0},{3,2},{5,4},{7,6},{8,9},{10,11},{12,... | collective-permute-start | bytes 270344 | tf_op jit(solution)/shard_map/ppermute | solution.py:510
  10.2 14.6 %collective-permute-start.3 = (f32[176,128]{1,0:T(8,128)S(1)}, f32[176,128]{1,0:T(8,128)S(1)}, u32[]{:S(2)}, u32[]{:S(2)}) collective-permute-start(f32[176,128]{1,0:T(8,128)S(1)} %get-tuple-element.49), channel_id=1, source_target_pairs={{1,2},{3,4},{5,6},{2,1},{4,3},{6,5},{9,10},{11,12},{13,14},{10,9},... | collective-permute-start | bytes 270344 | tf_op jit(solution)/shard_map/ppermute | solution.py:511
  33.5 7.8 %collective-permute-start.4 = (f32[144,128]{1,0:T(8,128)S(1)}, f32[144,128]{1,0:T(8,128)S(1)}, u32[]{:S(2)}, u32[]{:S(2)}) collective-permute-start(f32[144,128]{1,0:T(8,128)S(1)} %get-tuple-element.65), channel_id=1, source_target_pairs={{8,16},{24,32},{40,48},{56,64},{72,80},{88,96},{104,112},{120,128}... | collective-permute-start | bytes 221192 | tf_op jit(solution)/shard_map/ppermute | solution.py:506
  38.4 2.9 %collective-permute-start.5 = (f32[144,128]{1,0:T(8,128)S(1)}, f32[144,128]{1,0:T(8,128)S(1)}, u32[]{:S(2)}, u32[]{:S(2)}) collective-permute-start(f32[144,128]{1,0:T(8,128)S(1)} %get-tuple-element.66), channel_id=1, source_target_pairs={{0,8},{16,24},{32,40},{48,56},{64,72},{80,88},{96,104},{112,120},{... | collective-permute-start | bytes 221192 | tf_op jit(solution)/shard_map/ppermute | solution.py:507
  46.8 7.4 %collective-permute-start.6 = (f32[80,128]{1,0:T(8,128)S(1)}, f32[80,128]{1,0:T(8,128)S(1)}, u32[]{:S(2)}, u32[]{:S(2)}) collective-permute-start(f32[80,128]{1,0:T(8,128)S(1)} %get-tuple-element.77), channel_id=1, source_target_pairs={{8,16},{24,32},{40,48},{56,64},{72,80},{88,96},{104,112},{120,128}... | collective-permute-start | bytes 122888 | tf_op jit(solution)/shard_map/ppermute | solution.py:506
  51.6 2.5 %collective-permute-start.7 = (f32[80,128]{1,0:T(8,128)S(1)}, f32[80,128]{1,0:T(8,128)S(1)}, u32[]{:S(2)}, u32[]{:S(2)}) collective-permute-start(f32[80,128]{1,0:T(8,128)S(1)} %get-tuple-element.78), channel_id=1, source_target_pairs={{0,8},{16,24},{32,40},{48,56},{64,72},{80,88},{96,104},{112,120},{... | collective-permute-start | bytes 122888 | tf_op jit(solution)/shard_map/ppermute | solution.py:507
  54.8 6.7 %collective-permute-start.8 = (f32[64,128]{1,0:T(8,128)S(1)}, f32[64,128]{1,0:T(8,128)S(1)}, u32[]{:S(2)}, u32[]{:S(2)}) collective-permute-start(f32[64,128]{1,0:T(8,128)S(1)} %get-tuple-element.81), channel_id=1, source_target_pairs={{0,1},{2,3},{4,5},{6,7},{1,0},{3,2},{5,4},{7,6},{8,9},{10,11},{12,... | collective-permute-start | bytes 98312 | tf_op jit(solution)/shard_map/ppermute | solution.py:510
  54.9 11.8 %collective-permute-start.9 = (f32[64,128]{1,0:T(8,128)S(1)}, f32[64,128]{1,0:T(8,128)S(1)}, u32[]{:S(2)}, u32[]{:S(2)}) collective-permute-start(f32[64,128]{1,0:T(8,128)S(1)} %get-tuple-element.82), channel_id=1, source_target_pairs={{1,2},{3,4},{5,6},{2,1},{4,3},{6,5},{9,10},{11,12},{13,14},{10,9},... | collective-permute-start | bytes 98312 | tf_op jit(solution)/shard_map/ppermute | solution.py:511
  72.8 7.4 %collective-permute-start.10 = (f32[80,128]{1,0:T(8,128)S(1)}, f32[80,128]{1,0:T(8,128)S(1)}, u32[]{:S(2)}, u32[]{:S(2)}) collective-permute-start(f32[80,128]{1,0:T(8,128)S(1)} %get-tuple-element.85), channel_id=1, source_target_pairs={{8,16},{24,32},{40,48},{56,64},{72,80},{88,96},{104,112},{120,128}... | collective-permute-start | bytes 122888 | tf_op jit(solution)/shard_map/ppermute | solution.py:506
  76.5 3.7 %collective-permute-start.11 = (f32[80,128]{1,0:T(8,128)S(1)}, f32[80,128]{1,0:T(8,128)S(1)}, u32[]{:S(2)}, u32[]{:S(2)}) collective-permute-start(f32[80,128]{1,0:T(8,128)S(1)} %get-tuple-element.86), channel_id=1, source_target_pairs={{0,8},{16,24},{32,40},{48,56},{64,72},{80,88},{96,104},{112,120},{... | collective-permute-start | bytes 122888 | tf_op jit(solution)/shard_map/ppermute | solution.py:507

commit v3 on v2

--- a/solution.py
+++ b/solution.py
@@ -160,48 +160,53 @@
     return pltpu.roll(value, 64, 1)
 
 
+def is_even(place, axis, shape):
+    return jnp.broadcast_to(place[axis : axis + 1, : shape[1]], shape) % 2 == 0
+
+
 def window(shape, first_col, first_row, whole_cols, whole_rows):
     col = lax.broadcasted_iota(jnp.int32, shape, 0) + first_col
     row = lax.broadcasted_iota(jnp.int32, shape, 1) + first_row
     return (col >= 0) & (col < whole_cols) & (row >= 0) & (row < whole_rows)
 
 
-def setup_kernel(geos, held, kern_real, kern_imag, tap_rows, *rest):
-    tables, rest = rest[: len(geos)], rest[len(geos) :]
-    sources, rest = rest[:held], rest[held:]
-    outs, rest = rest[: len(geos)], rest[len(geos) :]
-    targets, (scratch, sems) = rest[:held], rest[held:]
+def column_spectra(geo, half, table, out):
+    count = geo.freqs_up
+    for k in range(out.shape[0] // (2 * count)):
+        part = half[k * KS : (k + 1) * KS, :]
+        turned = jnp.concatenate(
+            [part[:, 128:256], -part[:, 0:128], part[:, 384:512], -part[:, 256:384]], 1
+        )
+        spec = left_dot(table[...], jnp.concatenate([part, turned], 0))
+        out[2 * k * count : (2 * k + 1) * count, :] = spec[:, :256]
+        out[(2 * k + 1) * count : (2 * k + 2) * count, :] = spec[:, 256:]
+
+
+def setup_kernel(geo, held, kern_real, kern_imag, tap_rows, tap_cols, *rest):
+    sources, (out, half), rest = rest[:held], rest[held : held + 2], rest[held + 2 :]
+    targets, sems = rest[:held], rest[held]
     copies = [
         pltpu.make_async_copy(source, target, sems.at[index])
         for index, (source, target) in enumerate(zip(sources, targets))
     ]
     for copy in copies:
         copy.start()
-    kernels = kern_real.shape[1] // KS
     both = jnp.concatenate([kern_real[...], kern_imag[...]], 0)
     for start in range(0, both.shape[1], 128):
         part = both[:, start : start + 128].T
-        scratch[start : start + 128, :] = right_dot(part, tap_rows[...])
-    for k in range(kernels):
-        half = scratch[k * KS : (k + 1) * KS, :]
-        turned = jnp.concatenate(
-            [half[:, 128:256], -half[:, 0:128], half[:, 384:512], -half[:, 256:384]], 1
-        )
-        high, low = split(jnp.concatenate([half, turned], 0))
-        stacked = jnp.concatenate([high, low, high], 0)
-        for geo, table, out in zip(geos, tables, outs):
-            spec = dot(table[...], stacked)
-            count = geo.freqs_up
-            out[2 * k * count : (2 * k + 1) * count, :] = spec[:, :256]
-            out[(2 * k + 1) * count : (2 * k + 2) * count, :] = spec[:, 256:]
+        half[start : start + 128, :] = right_dot(part, tap_rows[...])
+    column_spectra(geo, half, tap_cols, out)
     for copy in copies:
         copy.wait()
 
 
+def slim_kernel(geo, half, tap_cols, out):
+    column_spectra(geo, half, tap_cols, out)
+
+
 def one_step(geo, mask, target, inside, weights, spec, tabs, fields):
     count = geo.freqs_up
-    group = weights.shape[0]
-    kernels = weights.shape[0]
+    group = kernels = fields.shape[1]
     lane = lax.broadcasted_iota(jnp.int32, (count, 128), 1) < 64
     across = left_dot(tabs["mask_cols"][...], mask)
     mask_spec = right_dot(
@@ -236,7 +241,7 @@
             for j in range(group):
                 own = field[:, j * 128 : (j + 1) * 128]
                 fields[side, k + j] = own
-                intensity[side] = intensity[side] + weights[k + j] * (own * own)
+                intensity[side] = intensity[side] + weights[k + j : k + j + 1, :] * (own * own)
     cotangent = []
     for side in (0, 1):
         intensity[side] = intensity[side] + swap_halves(intensity[side])
@@ -249,7 +254,10 @@
         ks = range(k, k + group)
         right, left = (
             jnp.concatenate(
-                [(2.0 * weights[j] * cotangent[side]) * fields[side, j] for j in ks],
+                [
+                    (2.0 * weights[j : j + 1, :] * cotangent[side]) * fields[side, j]
+                    for j in ks
+                ],
                 1,
             )
             for side in (0, 1)
@@ -317,13 +325,13 @@
 
 
 def prep_kernel(place, own, target, across, within, params, to_first, to_second, tall):
-    even = place[0] % 2 == 0
+    even = is_even(place, 0, (32, own.shape[0]))
     cols = own.shape[0]
     tall[...] = jnp.zeros_like(tall)
     tall[0:32, :cols] = jnp.where(even, across[32:64, :], within[32:64, :])
     tall[96:128, :cols] = jnp.where(even, within[0:32, :], across[0:32, :])
     params[...] = own[...] + tall[...].T[:cols]
-    right = place[1] % 2 == 0
+    right = is_even(place, 1, (176, 128))
     left_lanes = lanes((48, 128))
 
     def packed(start):
@@ -336,7 +344,7 @@
 
 
 def spread_out(place, grad, spread, to_far, to_near):
-    even = place[0] % 2 == 0
+    even = is_even(place, 0, grad.shape)
     half = to_far.shape[0]
     spread[...] = grad
     turned = swap_halves(grad)
@@ -348,7 +356,7 @@
 
 
 def gathered(place, spread, far, near):
-    even = place[0] % 2 == 0
+    even = is_even(place, 0, spread.shape)
     far, near = far[...], near[...]
     left_lanes = lanes(far.shape)
     far_turned, near_turned = swap_halves(far), swap_halves(near)
@@ -367,14 +375,14 @@
 
 
 def masked(place, tile, whole, params, col_offset):
-    first_col = place[1] * tile[1] + col_offset
-    first_row = place[0] * tile[0] - H
+    first_col = place[1:2, :128] * tile[1] + col_offset
+    first_row = place[0:1, :128] * tile[0] - H
     inside = window(params.shape, first_col, first_row, whole[1], whole[0])
     return jnp.where(inside, sigmoid(sharpness * params), 0.0)
 
 
 def field_window(geo, place, tile, whole, col_offset):
-    middle = place[1] * tile[1] + col_offset + H + geo.half
+    middle = place[1:2, :128] * tile[1] + col_offset + H + geo.half
     step = lax.broadcasted_iota(jnp.int32, (geo.half_up, 128), 0)
     return [(col >= 0) & (col < whole[1]) for col in (middle + step, middle - 1 - step)]
 
@@ -386,7 +394,7 @@
     rest = rest[len(STEP_TABLES) :]
     spread, to_far, to_near, params_out, goal_out, params, goal, fields = rest
     cols = own.shape[0]
-    right_first = place[1] % 2 == 0
+    right_first = is_even(place, 1, first.shape)
     left = jnp.where(right_first, second[...], first[...])
     right = jnp.where(right_first, first[...], second[...])
     params[...] = jnp.zeros_like(params)
@@ -428,20 +436,20 @@
 
 def update_kernel(cols, place, own, far, near, old, params, to_first, to_second):
     params[...] = stepped(old[...], gathered(place, own, far, near))
-    right = place[1] % 2 == 0
+    right = is_even(place, 1, (64, 128))
     to_left, to_right = params[0:64, :], params[cols - 64 : cols, :]
     to_first[...] = jnp.where(right, to_right, to_left)
     to_second[...] = jnp.where(right, to_left, to_right)
 
 
 def third_kernel(
-    geo, tile, whole, place, weights, own, first, second, goal, spec, mirror, *rest
+    geo, tile, whole, place, weights, own, first, second, goal, spec, *rest
 ):
     tabs = dict(zip(STEP_TABLES, rest))
     rest = rest[len(STEP_TABLES) :]
-    spread, to_far, to_near, intensity_out, params, flat, fields = rest
+    spread, to_far, to_near, intensity_out, params, fields = rest
     cols = tile[1]
-    right_first = place[1] % 2 == 0
+    right_first = is_even(place, 1, (64, 128))
     params[...] = jnp.zeros_like(params)
     params[0:64, :] = jnp.where(right_first, second[...], first[...])
     params[64 : 64 + cols, :] = own[0:cols, :]
@@ -451,13 +459,18 @@
     goals = [goal[0], goal[1]]
     intensity, grad = one_step(geo, mask, goals, inside, weights, spec, tabs, fields)
     spread_out(place, grad, spread, to_far, to_near)
+    for side in (0, 1):
+        intensity_out[side] = intensity[side]
+
+
+def intensity_kernel(cols, intensity, mirror, out, flat):
     high, low = split(intensity[1])
     rest = (intensity[1] - high.astype(f32) - low.astype(f32)).astype(bf16)
     turned = dot(mirror[...], high) + (dot(mirror[...], low) + dot(mirror[...], rest))
     flat[...] = jnp.zeros_like(flat)
     flat[0 : cols // 2, :] = turned[0 : cols // 2]
     flat[cols // 2 : cols, :] = intensity[0][0 : cols // 2]
-    intensity_out[...] = flat[...].T[:64, :cols]
+    out[...] = flat[...].T[:64, :cols]
 
 
 def final_kernel(cols, place, own, far, near, out, wide):
@@ -472,12 +485,7 @@
     return table.astype(ml_dtypes.bfloat16)
 
 
-def call(kernel, name, out_shapes, scratch, args, scalars):
-    args = args[:scalars] + [
-        pltpu.with_memory_space_constraint(arg, pltpu.VMEM) for arg in args[scalars:]
-    ]
-    specs = [pl.BlockSpec(memory_space=pltpu.SMEM)] * scalars
-    specs += [pl.BlockSpec(memory_space=pltpu.VMEM)] * (len(args) - scalars)
+def call(kernel, name, out_shapes, scratch, args):
     return pl.pallas_call(
         kernel,
         name=name,
@@ -485,18 +493,20 @@
             shape if isinstance(shape, jax.ShapeDtypeStruct) else pltpu.VMEM(shape, f32)
             for shape in out_shapes
         ],
-        in_specs=specs,
+        in_specs=[pl.BlockSpec(memory_space=pltpu.VMEM)] * len(args),
         out_specs=[pl.BlockSpec(memory_space=pltpu.VMEM)] * len(out_shapes),
         scratch_shapes=[pltpu.VMEM(shape, f32) for shape in scratch],
         compiler_params=pltpu.CompilerParams(vmem_limit_bytes=VMEM_LIMIT),
-    )(*args)
+    )(*[pltpu.with_memory_space_constraint(arg, pltpu.VMEM) for arg in args])
 
 
 def per_device(rows, cols, mask_params, target_bits, kern_real, kern_imag, socs_weights):
     tile = mask_params.shape
     whole = (tile[0] * rows, tile[1] * cols)
     kernels = kern_real.shape[1] // KS
-    place = jnp.stack([lax.axis_index("row"), lax.axis_index("col")]).astype(jnp.int32)
+    axis = lax.broadcasted_iota(jnp.int32, (8, 256), 0)
+    place = jnp.where(axis == 0, lax.axis_index("row"), lax.axis_index("col"))
+    weights = jnp.broadcast_to(socs_weights[:, None], (kernels, 128))
 
     def swaps(count, start):
         pairs = [(i, i + 1) for i in range(start, count - 1, 2)]
@@ -523,7 +533,6 @@
         [(n, 128), (n, 128)],
         [(128, 256)],
         [mask_params, target_bits],
-        0,
     )
     params, to_first, to_second = call(
         prep_kernel,
@@ -531,33 +540,30 @@
         [(n, 128), (176, 128), (176, 128)],
         [(128, 256)],
         [place, params, target, far, near],
-        1,
     )
     first, second = col_exchange(to_first, to_second)
     names = [(label, name) for label in ("wide", "slim") for name in COLUMN_TABLES]
     names += [("shared", name) for name in ROW_TABLES + ("wide_mirror", "slim_mirror")]
+    names += [("slim", "tap_cols")]
     tables = [jnp.asarray(made[label][name]) for label, name in names]
     inputs = [
         kern_real,
         kern_imag,
         jnp.asarray(shared["tap_rows"]),
         jnp.asarray(made["wide"]["tap_cols"]),
-        jnp.asarray(made["slim"]["tap_cols"]),
     ]
-    wide_spec, slim_spec, *held = pl.pallas_call(
-        functools.partial(setup_kernel, (wide, slim), len(tables)),
+    wide_spec, half_spec, *held = pl.pallas_call(
+        functools.partial(setup_kernel, wide, len(tables)),
         name="spectra",
         out_shape=[
-            pltpu.VMEM((2 * kernels * geo.freqs_up, 256), f32) for geo in (wide, slim)
+            pltpu.VMEM((2 * kernels * wide.freqs_up, 256), f32),
+            pltpu.VMEM((kernels * KS, 512), f32),
         ]
         + [pltpu.VMEM(table.shape, table.dtype) for table in tables],
         in_specs=[pl.BlockSpec(memory_space=pltpu.VMEM)] * len(inputs)
         + [pl.BlockSpec(memory_space=pltpu.HBM)] * len(tables),
         out_specs=[pl.BlockSpec(memory_space=pltpu.VMEM)] * (2 + len(tables)),
-        scratch_shapes=[
-            pltpu.VMEM((kernels * KS, 512), f32),
-            pltpu.SemaphoreType.DMA((len(tables),)),
-        ],
+        scratch_shapes=[pltpu.SemaphoreType.DMA((len(tables),))],
         compiler_params=pltpu.CompilerParams(vmem_limit_bytes=VMEM_LIMIT),
     )(*[pltpu.with_memory_space_constraint(arg, pltpu.HBM) for arg in inputs + tables])
     place_of = {key: table for key, table in zip(names, held)}
@@ -578,18 +584,23 @@
         "first",
         spreads(wide) + [(slim.mask_up, 128), (2, slim.half_up, 128)],
         [(wide.mask_up, 128), (wide.half + wide.half_up, 128), fields(wide)],
-        [place, socs_weights, params, target, first, second, wide_spec]
+        [place, weights, params, target, first, second, wide_spec]
         + [place_of["shared", "wide_mirror"], *tabs("wide")],
-        2,
     )
     far, near = row_exchange(to_far, to_near)
+    (slim_spec,) = call(
+        functools.partial(slim_kernel, slim),
+        "slim",
+        [(2 * kernels * slim.freqs_up, 256)],
+        [],
+        [half_spec, place_of["slim", "tap_cols"]],
+    )
     spread, to_far, to_near, params = call(
         functools.partial(second_kernel, slim, tile, whole),
         "second",
         spreads(slim) + [(slim.grad_up, 128)],
         [fields(slim)],
-        [place, socs_weights, spread, far, near, params, goal, slim_spec, *tabs("slim")],
-        2,
+        [place, weights, spread, far, near, params, goal, slim_spec, *tabs("slim")],
     )
     far, near = row_exchange(to_far, to_near)
     params, to_first, to_second = call(
@@ -598,26 +609,29 @@
         [(slim.grad_up, 128), (64, 128), (64, 128)],
         [],
         [place, spread, far, near, params],
-        1,
     )
     first, second = col_exchange(to_first, to_second)
     spread, to_far, to_near, intensity = call(
         functools.partial(third_kernel, slim, tile, whole),
         "third",
-        spreads(slim) + [jax.ShapeDtypeStruct(tile, f32)],
-        [(slim.mask_up, 128), (256, 128), fields(slim)],
-        [place, socs_weights, params, first, second, goal, slim_spec]
-        + [place_of["shared", "slim_mirror"], *tabs("slim")],
-        2,
+        spreads(slim) + [(2, slim.half_up, 128)],
+        [(slim.mask_up, 128), fields(slim)],
+        [place, weights, params, first, second, goal, slim_spec, *tabs("slim")],
     )
     far, near = row_exchange(to_far, to_near)
+    (intensity,) = call(
+        functools.partial(intensity_kernel, n),
+        "intensity",
+        [jax.ShapeDtypeStruct(tile, f32)],
+        [(256, 128)],
+        [intensity, place_of["shared", "slim_mirror"]],
+    )
     (mask_grad,) = call(
         functools.partial(final_kernel, n),
         "final",
         [jax.ShapeDtypeStruct(tile, f32)],
         [(256, 128)],
         [place, spread, far, near],
-        1,
     )
     return mask_grad, intensity
 

time: 81.9 us -> 77.1 us (0.941)
  Pallas kernels: 28.8 us -> 25.6 us
  waiting for transfers between devices: 15.3 us -> 12.4 us
  starting transfers between devices: 35 us -> 36 us
    pallas_call x7 -> x9, Pallas kernels: 23 us -> 20.7 us  [call(): pl.pallas_call(kernel, name=name, out_shape=[shape if isinstance(shape, j...]
    ppermute x4, waiting for transfers between devices: 10.1 us -> 8.12 us  [row_exchange(): far = lax.ppermute(to_far, 'row', swaps(rows, 1))]
    ppermute x2, starting transfers between devices: 15.4 us -> 16.4 us  [col_exchange(): return (first, lax.ppermute(to_second, 'col', swaps(cols, 1)))]
    ppermute x2, waiting for transfers between devices: 5.19 us -> 4.31 us  [col_exchange(): return (first, lax.ppermute(to_second, 'col', swaps(cols, 1)))]
    pallas_call x1, Pallas kernels: 5.77 us -> 4.91 us  [per_device(): pl.pallas_call(functools.partial(setup_kernel, wide, len(tables)), name='...]
  transfers between devices with their start and end apart: 12 -> 12, of which waited for: 5 -> 5; matrix products, arithmetic and copies ran while one was open for 1% -> 1% of each run, Pallas kernels for 7% -> 9%
where the time goes in v3:
time: 77.1 us; the launch traced here: 76.7 us
  starting transfers between devices  36 us (47%)
  Pallas kernels  25.6 us (33%)
  waiting for transfers between devices  12.4 us (16%)
  local copies, waits for them, and re-layouts  1.76 us (2%)
  between operations  0.83 us (1%)
    pallas_call x9, Pallas kernels, call(): pl.pallas_call(kernel, name=name, out_shape=[shape if isinstance(shape, j...  20.7 us
    ppermute x4, starting transfers between devices, row_exchange(): far = lax.ppermute(to_far, 'row', swaps(rows, 1))  18.1 us
    ppermute x2, starting transfers between devices, col_exchange(): return (first, lax.ppermute(to_second, 'col', swaps(cols, 1)))  16.4 us
    ppermute x4, waiting for transfers between devices, row_exchange(): far = lax.ppermute(to_far, 'row', swaps(rows, 1))  8.12 us
    pallas_call x1, Pallas kernels, per_device(): pl.pallas_call(functools.partial(setup_kernel, wide, len(tables)), name='...  4.91 us
    ppermute x2, waiting for transfers between devices, col_exchange(): return (first, lax.ppermute(to_second, 'col', swaps(cols, 1)))  4.31 us
    unnamed x5, local copies, waits for them, and re-layouts  1.62 us
  transfers between devices with their start and end apart: 12, of which 5 were waited for; matrix products, arithmetic and copies ran while one was open for 1% of the time, Pallas kernels for 9%

profile of v3, /device:TPU:38, one launch (start us, length us, event | category | flops | bytes accessed | tf_op | source)
XLA Modules:
  0.0 76.7 jit_solution(1307941535456992227)
XLA Ops:
  0.6 0.1 collective-permute-start.1
  0.7 4.6 %collective-permute-start = (f32[64,150]{1,0:T(8,128)}, f32[64,150]{1,0:T(8,128)S(1)}, u32[]{:S(2)}, u32[]{:S(2)}) collective-permute-start(f32[64,150]{1,0:T(8,128)} %own.1), channel_id=1, source_target_pairs={{8,16},{24,32},{40,48},{56,64},{72,80},{88,96},{104,112},{120,128}... | collective-permute-start | bytes 115208 | tf_op jit(solution)/shard_map/ppermute | solution.py:516
  5.3 0.8 %copy.30.bits = s32[64,5]{1,0:T(8,128)S(1)} copy(s32[64,5]{0,1:T(8,128)} %param.29) | data formatting | bytes 2560 | tf_op args[1]
  6.1 0.0 copy-start
  6.1 0.8 %copy-done = f32[64,150]{1,0:T(8,128)S(1)} copy-done((f32[64,150]{1,0:T(8,128)S(1)}, f32[64,150]{1,0:T(8,128)}, u32[]{:S(2)}) %copy-start) | copy-done | bytes 38424
  6.9 0.2 early.1
  7.1 0.0 collective-permute-done.1.within
  7.2 1.5 %collective-permute-done.across = f32[64,150]{1,0:T(8,128)S(1)} collective-permute-done((f32[64,150]{1,0:T(8,128)}, f32[64,150]{1,0:T(8,128)S(1)}, u32[]{:S(2)}, u32[]{:S(2)}) %collective-permute-start) | collective-permute-done | bytes 38432 | tf_op jit(solution)/shard_map/ppermute | solution.py:516
  8.6 0.1 iota.7.place
  8.7 0.1 prep.1
  8.8 0.9 %collective-permute-start.2 = (f32[176,128]{1,0:T(8,128)S(1)}, f32[176,128]{1,0:T(8,128)S(1)}, u32[]{:S(2)}, u32[]{:S(2)}) collective-permute-start(f32[176,128]{1,0:T(8,128)S(1)} %get-tuple-element.49), channel_id=1, source_target_pairs={{0,1},{2,3},{4,5},{6,7},{1,0},{3,2},{5,4},{7,6},{8,9},{10,11},{12,... | collective-permute-start | bytes 270344 | tf_op jit(solution)/shard_map/ppermute | solution.py:520
  9.8 0.0 copy-start.1
  9.8 8.9 %collective-permute-start.3 = (f32[176,128]{1,0:T(8,128)S(1)}, f32[176,128]{1,0:T(8,128)S(1)}, u32[]{:S(2)}, u32[]{:S(2)}) collective-permute-start(f32[176,128]{1,0:T(8,128)S(1)} %get-tuple-element.50), channel_id=1, source_target_pairs={{1,2},{3,4},{5,6},{2,1},{4,3},{6,5},{9,10},{11,12},{13,14},{10,9},... | collective-permute-start | bytes 270344 | tf_op jit(solution)/shard_map/ppermute | solution.py:521
  18.7 4.9 %spectra.1 = (f32[4992,256]{1,0:T(8,128)S(1)}, f32[768,512]{1,0:T(8,128)S(1)}, bf16[416,1248]{1,0:T(8,128)(2,1)S(1)}, bf16[176,624]{1,0:T(8,128)(2,1)S(1)}, bf16...) custom-call(f32[64,768]{1,0:T(8,128)} %kern_real.1, ...), custom_call_target="tpu_custom_call" | custom-call | tf_op jit(solution)/shard_map/spectra/pallas_call | solution.py:555
  23.6 0.0 collective-permute-done.2.first
  23.6 0.0 collective-permute-done.3.second
  23.6 0.0 copy-done.1
  23.6 0.1 broadcast_in_dim.16.weights
  23.7 7.8 %first.1 = (f32[288,128]{1,0:T(8,128)S(1)}, f32[144,128]{1,0:T(8,128)S(1)}, f32[144,128]{1,0:T(8,128)S(1)}, f32[288,128]{1,0:T(8,128)S(1)}, f32[2,112,128]{2,1,0:T(8,128)S(1)}) custom-call(s32[8,256]{1,0:T(8,128)S(1)} %iota.7.place, f32[12,128]{1,0:T(8,128)S(1)} %broadcast_in_dim.16.weights, f32[150,128]{1,0:T(8,128)S(1)} %get-tuple-element.48.own, ...), custom_call_target="tpu_custom_call" | custom-call | tf_op jit(solution)/shard_map/first/pallas_call | solution.py:489
  31.5 4.9 %collective-permute-start.4 = (f32[144,128]{1,0:T(8,128)S(1)}, f32[144,128]{1,0:T(8,128)S(1)}, u32[]{:S(2)}, u32[]{:S(2)}) collective-permute-start(f32[144,128]{1,0:T(8,128)S(1)} %get-tuple-element.66), channel_id=1, source_target_pairs={{8,16},{24,32},{40,48},{56,64},{72,80},{88,96},{104,112},{120,128}... | collective-permute-start | bytes 221192 | tf_op jit(solution)/shard_map/ppermute | solution.py:516
  36.4 0.3 collective-permute-start.5
  36.7 1.1 %slim.1.spec = f32[3456,256]{1,0:T(8,128)S(1)} custom-call(f32[768,512]{1,0:T(8,128)S(1)} %get-tuple-element.70.half, bf16[144,384]{1,0:T(8,128)(2,1)S(1)} %get-tuple-element.71.tap_cols), custom_call_target="tpu_custom_call" | custom-call | tf_op jit(solution)/shard_map/slim/pallas_call | solution.py:489
  37.8 1.5 %collective-permute-done.4.far = f32[144,128]{1,0:T(8,128)S(1)} collective-permute-done((f32[144,128]{1,0:T(8,128)S(1)}, f32[144,128]{1,0:T(8,128)S(1)}, u32[]{:S(2)}, u32[]{:S(2)}) %collective-permute-start.4) | collective-permute-done | bytes 73760 | tf_op jit(solution)/shard_map/ppermute | solution.py:516
  39.3 0.0 collective-permute-done.5.near
  39.3 4.9 %second.1 = (f32[160,128]{1,0:T(8,128)S(1)}, f32[80,128]{1,0:T(8,128)S(1)}, f32[80,128]{1,0:T(8,128)S(1)}, f32[160,128]{1,0:T(8,128)S(1)}) custom-call(s32[8,256]{1,0:T(8,128)S(1)} %iota.7.place, f32[12,128]{1,0:T(8,128)S(1)} %broadcast_in_dim.16.weights, f32[288,128]{1,0:T(8,128)S(1)} %get-tuple-element.65.own, f32[144,128]{1,0:T(8,128)S(1)} %collective-permute-done.4.far, ...), custom_call_target="tpu_custom_call" | custom-call | tf_op jit(solution)/shard_map/second/pallas_call | solution.py:489
  44.2 4.9 %collective-permute-start.6 = (f32[80,128]{1,0:T(8,128)S(1)}, f32[80,128]{1,0:T(8,128)S(1)}, u32[]{:S(2)}, u32[]{:S(2)}) collective-permute-start(f32[80,128]{1,0:T(8,128)S(1)} %get-tuple-element.79), channel_id=1, source_target_pairs={{8,16},{24,32},{40,48},{56,64},{72,80},{88,96},{104,112},{120,128}... | collective-permute-start | bytes 122888 | tf_op jit(solution)/shard_map/ppermute | solution.py:516
  49.1 0.1 collective-permute-start.7
  49.2 2.4 %collective-permute-done.6.far = f32[80,128]{1,0:T(8,128)S(1)} collective-permute-done((f32[80,128]{1,0:T(8,128)S(1)}, f32[80,128]{1,0:T(8,128)S(1)}, u32[]{:S(2)}, u32[]{:S(2)}) %collective-permute-start.6) | collective-permute-done | bytes 40992 | tf_op jit(solution)/shard_map/ppermute | solution.py:516
  51.6 0.0 collective-permute-done.7.near
  51.6 0.1 update.1
  51.7 0.1 collective-permute-start.8
  51.8 7.5 %collective-permute-start.9 = (f32[64,128]{1,0:T(8,128)S(1)}, f32[64,128]{1,0:T(8,128)S(1)}, u32[]{:S(2)}, u32[]{:S(2)}) collective-permute-start(f32[64,128]{1,0:T(8,128)S(1)} %get-tuple-element.84), channel_id=1, source_target_pairs={{1,2},{3,4},{5,6},{2,1},{4,3},{6,5},{9,10},{11,12},{13,14},{10,9},... | collective-permute-start | bytes 98312 | tf_op jit(solution)/shard_map/ppermute | solution.py:521
  59.3 0.0 collective-permute-done.8.first
  59.3 4.3 %collective-permute-done.9.second = f32[64,128]{1,0:T(8,128)S(1)} collective-permute-done((f32[64,128]{1,0:T(8,128)S(1)}, f32[64,128]{1,0:T(8,128)S(1)}, u32[]{:S(2)}, u32[]{:S(2)}) %collective-permute-start.9) | collective-permute-done | bytes 32800 | tf_op jit(solution)/shard_map/ppermute | solution.py:521
  63.6 4.8 %third.1 = (f32[160,128]{1,0:T(8,128)S(1)}, f32[80,128]{1,0:T(8,128)S(1)}, f32[80,128]{1,0:T(8,128)S(1)}, f32[2,112,128]{2,1,0:T(8,128)S(1)}) custom-call(s32[8,256]{1,0:T(8,128)S(1)} %iota.7.place, f32[12,128]{1,0:T(8,128)S(1)} %broadcast_in_dim.16.weights, f32[160,128]{1,0:T(8,128)S(1)} %get-tuple-element.82.own, ...), custom_call_target="tpu_custom_call" | custom-call | tf_op jit(solution)/shard_map/third/pallas_call | solution.py:489
  68.4 3.7 %collective-permute-start.10 = (f32[80,128]{1,0:T(8,128)S(1)}, f32[80,128]{1,0:T(8,128)S(1)}, u32[]{:S(2)}, u32[]{:S(2)}) collective-permute-start(f32[80,128]{1,0:T(8,128)S(1)} %get-tuple-element.86), channel_id=1, source_target_pairs={{8,16},{24,32},{40,48},{56,64},{72,80},{88,96},{104,112},{120,128}... | collective-permute-start | bytes 122888 | tf_op jit(solution)/shard_map/ppermute | solution.py:516
  72.2 0.1 collective-permute-start.11
  72.3 0.9 %intensity.1 = f32[64,150]{1,0:T(8,128)} custom-call(f32[2,112,128]{2,1,0:T(8,128)S(1)} %get-tuple-element.88.intensity, bf16[80,112]{1,0:T(8,128)(2,1)S(1)} %get-tuple-element.89.mirror), custom_call_target="tpu_custom_call" | custom-call | tf_op jit(solution)/shard_map/intensity/pallas_call | solution.py:489
  73.2 2.7 %collective-permute-done.10.far = f32[80,128]{1,0:T(8,128)S(1)} collective-permute-done((f32[80,128]{1,0:T(8,128)S(1)}, f32[80,128]{1,0:T(8,128)S(1)}, u32[]{:S(2)}, u32[]{:S(2)}) %collective-permute-start.10) | collective-permute-done | bytes 40992 | tf_op jit(solution)/shard_map/ppermute | solution.py:516
  75.9 0.0 collective-permute-done.11.near
  75.9 0.8 %final.1 = f32[64,150]{1,0:T(8,128)} custom-call(s32[8,256]{1,0:T(8,128)S(1)} %iota.7.place, f32[160,128]{1,0:T(8,128)S(1)} %get-tuple-element.85.own, f32[80,128]{1,0:T(8,128)S(1)} %collective-permute-done.10.far, f32[80,128]{1,0:T(8,128)S(1)} %collective-permute-done.11.near), custom_call_target="tpu_custom_call" | custom-call | tf_op jit(solution)/shard_map/final/pallas_call | solution.py:489
  (1 shorter events, 0.0 us)
Async XLA Ops:
  0.6 6.5 %collective-permute-start.1 = (f32[64,150]{1,0:T(8,128)}, f32[64,150]{1,0:T(8,128)S(1)}, u32[]{:S(2)}, u32[]{:S(2)}) collective-permute-start(f32[64,150]{1,0:T(8,128)} %own.1), channel_id=1, source_target_pairs={{0,8},{16,24},{32,40},{48,56},{64,72},{80,88},{96,104},{112,120},{... | collective-permute-start | bytes 115208 | tf_op jit(solution)/shard_map/ppermute | solution.py:517
  0.7 7.9 %collective-permute-start = (f32[64,150]{1,0:T(8,128)}, f32[64,150]{1,0:T(8,128)S(1)}, u32[]{:S(2)}, u32[]{:S(2)}) collective-permute-start(f32[64,150]{1,0:T(8,128)} %own.1), channel_id=1, source_target_pairs={{8,16},{24,32},{40,48},{56,64},{72,80},{88,96},{104,112},{120,128}... | collective-permute-start | bytes 115208 | tf_op jit(solution)/shard_map/ppermute | solution.py:516
  6.1 0.8 %copy-start = (f32[64,150]{1,0:T(8,128)S(1)}, f32[64,150]{1,0:T(8,128)}, u32[]{:S(2)}) copy-start(f32[64,150]{1,0:T(8,128)} %own.1) | copy-start | bytes 115204
  8.8 14.7 %collective-permute-start.2 = (f32[176,128]{1,0:T(8,128)S(1)}, f32[176,128]{1,0:T(8,128)S(1)}, u32[]{:S(2)}, u32[]{:S(2)}) collective-permute-start(f32[176,128]{1,0:T(8,128)S(1)} %get-tuple-element.49), channel_id=1, source_target_pairs={{0,1},{2,3},{4,5},{6,7},{1,0},{3,2},{5,4},{7,6},{8,9},{10,11},{12,... | collective-permute-start | bytes 270344 | tf_op jit(solution)/shard_map/ppermute | solution.py:520
  9.8 13.8 %copy-start.1 = (f32[12]{0:T(128)S(1)}, f32[12]{0:T(128)}, u32[]{:S(2)}) copy-start(f32[12]{0:T(128)} %param.32) | copy-start | bytes 148
  9.8 13.8 %collective-permute-start.3 = (f32[176,128]{1,0:T(8,128)S(1)}, f32[176,128]{1,0:T(8,128)S(1)}, u32[]{:S(2)}, u32[]{:S(2)}) collective-permute-start(f32[176,128]{1,0:T(8,128)S(1)} %get-tuple-element.50), channel_id=1, source_target_pairs={{1,2},{3,4},{5,6},{2,1},{4,3},{6,5},{9,10},{11,12},{13,14},{10,9},... | collective-permute-start | bytes 270344 | tf_op jit(solution)/shard_map/ppermute | solution.py:521
  31.5 7.8 %collective-permute-start.4 = (f32[144,128]{1,0:T(8,128)S(1)}, f32[144,128]{1,0:T(8,128)S(1)}, u32[]{:S(2)}, u32[]{:S(2)}) collective-permute-start(f32[144,128]{1,0:T(8,128)S(1)} %get-tuple-element.66), channel_id=1, source_target_pairs={{8,16},{24,32},{40,48},{56,64},{72,80},{88,96},{104,112},{120,128}... | collective-permute-start | bytes 221192 | tf_op jit(solution)/shard_map/ppermute | solution.py:516
  36.4 2.9 %collective-permute-start.5 = (f32[144,128]{1,0:T(8,128)S(1)}, f32[144,128]{1,0:T(8,128)S(1)}, u32[]{:S(2)}, u32[]{:S(2)}) collective-permute-start(f32[144,128]{1,0:T(8,128)S(1)} %get-tuple-element.67), channel_id=1, source_target_pairs={{0,8},{16,24},{32,40},{48,56},{64,72},{80,88},{96,104},{112,120},{... | collective-permute-start | bytes 221192 | tf_op jit(solution)/shard_map/ppermute | solution.py:517
  44.2 7.4 %collective-permute-start.6 = (f32[80,128]{1,0:T(8,128)S(1)}, f32[80,128]{1,0:T(8,128)S(1)}, u32[]{:S(2)}, u32[]{:S(2)}) collective-permute-start(f32[80,128]{1,0:T(8,128)S(1)} %get-tuple-element.79), channel_id=1, source_target_pairs={{8,16},{24,32},{40,48},{56,64},{72,80},{88,96},{104,112},{120,128}... | collective-permute-start | bytes 122888 | tf_op jit(solution)/shard_map/ppermute | solution.py:516
  49.1 2.5 %collective-permute-start.7 = (f32[80,128]{1,0:T(8,128)S(1)}, f32[80,128]{1,0:T(8,128)S(1)}, u32[]{:S(2)}, u32[]{:S(2)}) collective-permute-start(f32[80,128]{1,0:T(8,128)S(1)} %get-tuple-element.80), channel_id=1, source_target_pairs={{0,8},{16,24},{32,40},{48,56},{64,72},{80,88},{96,104},{112,120},{... | collective-permute-start | bytes 122888 | tf_op jit(solution)/shard_map/ppermute | solution.py:517
  51.7 7.6 %collective-permute-start.8 = (f32[64,128]{1,0:T(8,128)S(1)}, f32[64,128]{1,0:T(8,128)S(1)}, u32[]{:S(2)}, u32[]{:S(2)}) collective-permute-start(f32[64,128]{1,0:T(8,128)S(1)} %get-tuple-element.83), channel_id=1, source_target_pairs={{0,1},{2,3},{4,5},{6,7},{1,0},{3,2},{5,4},{7,6},{8,9},{10,11},{12,... | collective-permute-start | bytes 98312 | tf_op jit(solution)/shard_map/ppermute | solution.py:520
  51.8 11.8 %collective-permute-start.9 = (f32[64,128]{1,0:T(8,128)S(1)}, f32[64,128]{1,0:T(8,128)S(1)}, u32[]{:S(2)}, u32[]{:S(2)}) collective-permute-start(f32[64,128]{1,0:T(8,128)S(1)} %get-tuple-element.84), channel_id=1, source_target_pairs={{1,2},{3,4},{5,6},{2,1},{4,3},{6,5},{9,10},{11,12},{13,14},{10,9},... | collective-permute-start | bytes 98312 | tf_op jit(solution)/shard_map/ppermute | solution.py:521
  68.4 7.4 %collective-permute-start.10 = (f32[80,128]{1,0:T(8,128)S(1)}, f32[80,128]{1,0:T(8,128)S(1)}, u32[]{:S(2)}, u32[]{:S(2)}) collective-permute-start(f32[80,128]{1,0:T(8,128)S(1)} %get-tuple-element.86), channel_id=1, source_target_pairs={{8,16},{24,32},{40,48},{56,64},{72,80},{88,96},{104,112},{120,128}... | collective-permute-start | bytes 122888 | tf_op jit(solution)/shard_map/ppermute | solution.py:516
  72.2 3.7 %collective-permute-start.11 = (f32[80,128]{1,0:T(8,128)S(1)}, f32[80,128]{1,0:T(8,128)S(1)}, u32[]{:S(2)}, u32[]{:S(2)}) collective-permute-start(f32[80,128]{1,0:T(8,128)S(1)} %get-tuple-element.87), channel_id=1, source_target_pairs={{0,8},{16,24},{32,40},{48,56},{64,72},{80,88},{96,104},{112,120},{... | collective-permute-start | bytes 122888 | tf_op jit(solution)/shard_map/ppermute | solution.py:517

commit v4 on v3

--- a/solution.py
+++ b/solution.py
@@ -142,14 +142,24 @@
     )
 
 
-def left_dot(table, value):
+def chunks(count, parts):
+    units = count // 16
+    edges = [16 * (units * i // parts) for i in range(parts + 1)]
+    return list(zip(edges[:-1], edges[1:]))
+
+
+def left_dot(table, value, parts=1):
     high, low = split(value)
-    return dot(table, jnp.concatenate([high, low, high], 0))
-
-
-def right_dot(value, table):
+    stacked = jnp.concatenate([high, low, high], 0)
+    rows = [table[a:b, :] for a, b in chunks(table.shape[0], parts)]
+    return jnp.concatenate([dot(part, stacked) for part in rows], 0)
+
+
+def right_dot(value, table, parts=1):
     high, low = split(value)
-    return dot(jnp.concatenate([high, low, high], 1), table)
+    stacked = jnp.concatenate([high, low, high], 1)
+    rows = [stacked[a:b] for a, b in chunks(value.shape[0], parts)]
+    return jnp.concatenate([dot(part, table) for part in rows], 0)
 
 
 def sigmoid(value):
@@ -182,8 +192,15 @@
         out[(2 * k + 1) * count : (2 * k + 2) * count, :] = spec[:, 256:]
 
 
-def setup_kernel(geo, held, kern_real, kern_imag, tap_rows, tap_cols, *rest):
-    sources, (out, half), rest = rest[:held], rest[held : held + 2], rest[held + 2 :]
+def taps_kernel(kern_real, kern_imag, tap_rows, half):
+    both = jnp.concatenate([kern_real[...], kern_imag[...]], 0)
+    for start in range(0, both.shape[1], 128):
+        part = both[:, start : start + 128].T
+        half[start : start + 128, :] = right_dot(part, tap_rows[...])
+
+
+def setup_kernel(geo, held, half, tap_cols, *rest):
+    sources, out, rest = rest[:held], rest[held], rest[held + 1 :]
     targets, sems = rest[:held], rest[held]
     copies = [
         pltpu.make_async_copy(source, target, sems.at[index])
@@ -191,10 +208,6 @@
     ]
     for copy in copies:
         copy.start()
-    both = jnp.concatenate([kern_real[...], kern_imag[...]], 0)
-    for start in range(0, both.shape[1], 128):
-        part = both[:, start : start + 128].T
-        half[start : start + 128, :] = right_dot(part, tap_rows[...])
     column_spectra(geo, half, tap_cols, out)
     for copy in copies:
         copy.wait()
@@ -206,84 +219,93 @@
 
 def one_step(geo, mask, target, inside, weights, spec, tabs, fields):
     count = geo.freqs_up
-    group = kernels = fields.shape[1]
-    lane = lax.broadcasted_iota(jnp.int32, (count, 128), 1) < 64
-    across = left_dot(tabs["mask_cols"][...], mask)
+    kernels = fields.shape[1]
+    across = left_dot(tabs["mask_cols"], mask, 2)
     mask_spec = right_dot(
-        jnp.concatenate([across[:count], across[count:]], 1), tabs["mask_rows"][...]
-    )
-    mask_re, mask_im = mask_spec[:, :128], mask_spec[:, 128:]
-
-    def product(index):
-        place = spec[index * count : (index + 1) * count, :]
-        re, im = place[:, :128], place[:, 128:]
-        return jnp.concatenate(
-            [re * mask_re - im * mask_im, re * mask_im + im * mask_re], 1
+        jnp.concatenate([across[:count], across[count:]], 1), tabs["mask_rows"][...], 2
+    )
+
+    def place(index, start, stop):
+        value = spec[index * count + start : index * count + stop, :]
+        return value[:, :128], value[:, 128:]
+
+    evens, odds = [], []
+    for start, stop in chunks(count, 1):
+        size = stop - start
+        lane = lanes((size, 128))
+        mask_re, mask_im = mask_spec[start:stop, :128], mask_spec[start:stop, 128:]
+
+        def down(indices, table):
+            products = []
+            for index in indices:
+                re, im = place(index, start, stop)
+                products.append(
+                    jnp.concatenate(
+                        [re * mask_re - im * mask_im, re * mask_im + im * mask_re], 1
+                    )
+                )
+            high, low = split(jnp.concatenate(products, 0))
+            wide = dot(high, table[...])
+            got = wide[:, :128] + wide[:, 128:] + dot(low, table[:, :128])
+            return [got[i * size : (i + 1) * size] for i in range(len(indices))]
+
+        firsts = down(range(0, 2 * kernels, 2), tabs["field_rows"])
+        seconds = down(range(1, 2 * kernels, 2), tabs["field_rows_swapped"])
+        pairs = list(zip(firsts, seconds))
+        evens.append(jnp.concatenate([jnp.where(lane, a, b) for a, b in pairs], 1))
+        odds.append(
+            jnp.concatenate([swap_halves(jnp.where(lane, b, a)) for a, b in pairs], 1)
         )
-
-    def down(indices, table):
-        high, low = split(jnp.concatenate([product(i) for i in indices], 0))
-        wide = dot(high, table[...])
-        got = wide[:, :128] + wide[:, 128:] + dot(low, table[:, :128])
-        return [got[i * count : (i + 1) * count] for i in range(len(indices))]
-
+    even = left_dot(tabs["field_even"][...], jnp.concatenate(evens, 0))
+    odd = left_dot(tabs["field_odd"][...], jnp.concatenate(odds, 0))
     zero = jnp.zeros((geo.half_up, 128), f32)
     intensity = [zero, zero]
-    for k in range(0, kernels, group):
-        ks = range(k, k + group)
-        firsts = down([2 * j for j in ks], tabs["field_rows"])
-        seconds = down([2 * j + 1 for j in ks], tabs["field_rows_swapped"])
-        evens = [jnp.where(lane, a, b) for a, b in zip(firsts, seconds)]
-        odds = [swap_halves(jnp.where(lane, b, a)) for a, b in zip(firsts, seconds)]
-        even = left_dot(tabs["field_even"][...], jnp.concatenate(evens, 1))
-        odd = left_dot(tabs["field_odd"][...], jnp.concatenate(odds, 1))
-        for side, field in enumerate((even - odd, even + odd)):
-            for j in range(group):
-                own = field[:, j * 128 : (j + 1) * 128]
-                fields[side, k + j] = own
-                intensity[side] = intensity[side] + weights[k + j : k + j + 1, :] * (own * own)
+    for side, field in enumerate((even - odd, even + odd)):
+        for j in range(kernels):
+            own = field[:, j * 128 : (j + 1) * 128]
+            fields[side, j] = own
+            intensity[side] = intensity[side] + weights[j : j + 1, :] * (own * own)
     cotangent = []
     for side in (0, 1):
         intensity[side] = intensity[side] + swap_halves(intensity[side])
         resist = sigmoid(steepness * (intensity[side] - threshold))
         slope = 2.0 * (resist - target[side]) * steepness * resist * (1.0 - resist)
         cotangent.append(jnp.where(inside[side], slope, 0.0))
-    total_re = jnp.zeros((count, 128), f32)
-    total_im = jnp.zeros((count, 128), f32)
-    for k in range(0, kernels, group):
-        ks = range(k, k + group)
-        right, left = (
-            jnp.concatenate(
-                [
-                    (2.0 * weights[j : j + 1, :] * cotangent[side]) * fields[side, j]
-                    for j in ks
-                ],
-                1,
-            )
-            for side in (0, 1)
+    right, left = (
+        jnp.concatenate(
+            [
+                (2.0 * weights[j : j + 1, :] * cotangent[side]) * fields[side, j]
+                for j in range(kernels)
+            ],
+            1,
         )
-        even = left_dot(tabs["source_even"][...], right + left)
-        odd = left_dot(tabs["source_odd"][...], right - left)
-        res = [even[:, j * 128 : (j + 1) * 128] for j in range(group)]
-        ims = [swap_halves(odd[:, j * 128 : (j + 1) * 128]) for j in range(group)]
+        for side in (0, 1)
+    )
+    even = left_dot(tabs["source_even"][...], right + left)
+    odd = left_dot(tabs["source_odd"][...], right - left)
+    totals = []
+    for start, stop in chunks(count, 2):
+        size = stop - start
+        lane = lanes((size, 128))
+        res = [even[start:stop, j * 128 : (j + 1) * 128] for j in range(kernels)]
+        ims = [swap_halves(odd[start:stop, j * 128 : (j + 1) * 128]) for j in range(kernels)]
+        total_re = jnp.zeros((size, 128), f32)
+        total_im = jnp.zeros((size, 128), f32)
         for index, values, table in (
             (0, [jnp.where(lane, a, b) for a, b in zip(res, ims)], tabs["source_rows"]),
             (1, [jnp.where(lane, b, a) for a, b in zip(res, ims)], tabs["source_rows_swapped"]),
         ):
             got = right_dot(jnp.concatenate(values, 0), table[...])
-            for j in range(group):
-                got_re, got_im = (
-                    got[j * count : (j + 1) * count, :128],
-                    got[j * count : (j + 1) * count, 128:],
-                )
-                start = (2 * (k + j) + index) * count
-                place = spec[start : start + count, :]
-                re_k, im_k = place[:, :128], place[:, 128:]
-                total_re = total_re + (re_k * got_re + im_k * got_im)
-                total_im = total_im + (re_k * got_im - im_k * got_re)
-    back = right_dot(jnp.concatenate([total_re, total_im], 1), tabs["grad_rows"][...])
+            for j in range(kernels):
+                got_re = got[j * size : (j + 1) * size, :128]
+                got_im = got[j * size : (j + 1) * size, 128:]
+                re, im = place(2 * j + index, start, stop)
+                total_re = total_re + (re * got_re + im * got_im)
+                total_im = total_im + (re * got_im - im * got_re)
+        totals.append(jnp.concatenate([total_re, total_im], 1))
+    back = right_dot(jnp.concatenate(totals, 0), tabs["grad_rows"][...], 2)
     grad = left_dot(
-        tabs["grad_cols"][...], jnp.concatenate([back[:, :128], back[:, 128:]], 0)
+        tabs["grad_cols"], jnp.concatenate([back[:, :128], back[:, 128:]], 0), 2
     )
     return intensity, grad
 
@@ -316,12 +338,14 @@
     tall[...] = jnp.zeros_like(tall)
     tall[32:96, :cols] = own[...]
     params[...] = tall[...].T[:cols]
-    col = lax.broadcasted_iota(jnp.int32, (64, tall.shape[1]), 1)
-    word = jnp.zeros_like(col)
-    for index in range(bits.shape[1]):
-        word = jnp.where(col // 30 == index, bits[:, index : index + 1], word)
-    bit = jnp.bitwise_and(jnp.right_shift(word, col % 30), 1).astype(f32)
-    target[...] = jnp.concatenate([bit, bit], 0).T[:cols]
+    words = bits.shape[0]
+    width = cols // words
+    shift = lax.broadcasted_iota(jnp.int32, (width, 128), 0)
+    for index in range(words):
+        word = bits[index : index + 1, :]
+        word = jnp.broadcast_to(jnp.concatenate([word, word], 1), (width, 128))
+        bit = jnp.bitwise_and(jnp.right_shift(word, shift), 1).astype(f32)
+        target[index * width : (index + 1) * width, :] = bit
 
 
 def prep_kernel(place, own, target, across, within, params, to_first, to_second, tall):
@@ -485,7 +509,7 @@
     return table.astype(ml_dtypes.bfloat16)
 
 
-def call(kernel, name, out_shapes, scratch, args):
+def call(kernel, name, out_shapes, scratch, args, space=pltpu.VMEM):
     return pl.pallas_call(
         kernel,
         name=name,
@@ -497,7 +521,7 @@
         out_specs=[pl.BlockSpec(memory_space=pltpu.VMEM)] * len(out_shapes),
         scratch_shapes=[pltpu.VMEM(shape, f32) for shape in scratch],
         compiler_params=pltpu.CompilerParams(vmem_limit_bytes=VMEM_LIMIT),
-    )(*[pltpu.with_memory_space_constraint(arg, pltpu.VMEM) for arg in args])
+    )(*[pltpu.with_memory_space_constraint(arg, space) for arg in args])
 
 
 def per_device(rows, cols, mask_params, target_bits, kern_real, kern_imag, socs_weights):
@@ -532,8 +556,18 @@
         "early",
         [(n, 128), (n, 128)],
         [(128, 256)],
-        [mask_params, target_bits],
-    )
+        [mask_params, target_bits.T],
+        pltpu.HBM,
+    )
+    (half_spec,) = call(
+        taps_kernel,
+        "taps",
+        [(kernels * KS, 512)],
+        [],
+        [kern_real, kern_imag, jnp.asarray(shared["tap_rows"])],
+        pltpu.HBM,
+    )
+    near, half_spec = lax.optimization_barrier((near, half_spec))
     params, to_first, to_second = call(
         prep_kernel,
         "prep",
@@ -546,26 +580,19 @@
     names += [("shared", name) for name in ROW_TABLES + ("wide_mirror", "slim_mirror")]
     names += [("slim", "tap_cols")]
     tables = [jnp.asarray(made[label][name]) for label, name in names]
-    inputs = [
-        kern_real,
-        kern_imag,
-        jnp.asarray(shared["tap_rows"]),
-        jnp.asarray(made["wide"]["tap_cols"]),
-    ]
-    wide_spec, half_spec, *held = pl.pallas_call(
+    arrays = [half_spec, jnp.asarray(made["wide"]["tap_cols"])] + tables
+    spaces = [pltpu.VMEM] + [pltpu.HBM] * (1 + len(tables))
+    wide_spec, *held = pl.pallas_call(
         functools.partial(setup_kernel, wide, len(tables)),
         name="spectra",
-        out_shape=[
-            pltpu.VMEM((2 * kernels * wide.freqs_up, 256), f32),
-            pltpu.VMEM((kernels * KS, 512), f32),
-        ]
+        out_shape=[pltpu.VMEM((2 * kernels * wide.freqs_up, 256), f32)]
         + [pltpu.VMEM(table.shape, table.dtype) for table in tables],
-        in_specs=[pl.BlockSpec(memory_space=pltpu.VMEM)] * len(inputs)
+        in_specs=[pl.BlockSpec(memory_space=pltpu.VMEM)] * 2
         + [pl.BlockSpec(memory_space=pltpu.HBM)] * len(tables),
-        out_specs=[pl.BlockSpec(memory_space=pltpu.VMEM)] * (2 + len(tables)),
+        out_specs=[pl.BlockSpec(memory_space=pltpu.VMEM)] * (1 + len(tables)),
         scratch_shapes=[pltpu.SemaphoreType.DMA((len(tables),))],
         compiler_params=pltpu.CompilerParams(vmem_limit_bytes=VMEM_LIMIT),
-    )(*[pltpu.with_memory_space_constraint(arg, pltpu.HBM) for arg in inputs + tables])
+    )(*[pltpu.with_memory_space_constraint(*pair) for pair in zip(arrays, spaces)])
     place_of = {key: table for key, table in zip(names, held)}
 
     def tabs(label):

time: 77.1 us -> 75.9 us (0.984)
  local copies, waits for them, and re-layouts: 1.76 us -> 0.14 us
  Pallas kernels: 25.6 us -> 26.5 us
    unnamed x5 -> x2, local copies, waits for them, and re-layouts: 1.62 us -> 0.01 us
    pallas_call x9 -> x10, Pallas kernels: 20.7 us -> 22.3 us  [call(): pl.pallas_call(kernel, name=name, out_shape=[shape if isinstance(shape, j...]
    ppermute x4, starting transfers between devices: 18.1 us -> 16.9 us  [row_exchange(): far = lax.ppermute(to_far, 'row', swaps(rows, 1))]
    ppermute x2, starting transfers between devices: 16.4 us -> 17.5 us  [col_exchange(): return (first, lax.ppermute(to_second, 'col', swaps(cols, 1)))]
  transfers between devices with their start and end apart: 12 -> 12, of which waited for: 5 -> 5; matrix products, arithmetic and copies ran while one was open for 1% -> 0% of each run, Pallas kernels for 9% -> 12%
where the time goes in v4:
time: 75.9 us; the launch traced here: 75.4 us
  starting transfers between devices  36 us (47%)
  Pallas kernels  26.5 us (35%)
  waiting for transfers between devices  11.9 us (16%)
  between operations  0.82 us (1%)
    pallas_call x10, Pallas kernels, call(): pl.pallas_call(kernel, name=name, out_shape=[shape if isinstance(shape, j...  22.3 us
    ppermute x2, starting transfers between devices, col_exchange(): return (first, lax.ppermute(to_second, 'col', swaps(cols, 1)))  17.5 us
    ppermute x4, starting transfers between devices, row_exchange(): far = lax.ppermute(to_far, 'row', swaps(rows, 1))  16.9 us
    ppermute x4, waiting for transfers between devices, row_exchange(): far = lax.ppermute(to_far, 'row', swaps(rows, 1))  8.28 us
    pallas_call x1, Pallas kernels, per_device(): pl.pallas_call(functools.partial(setup_kernel, wide, len(tables)), name='...  4.23 us
    ppermute x2, waiting for transfers between devices, col_exchange(): return (first, lax.ppermute(to_second, 'col', swaps(cols, 1)))  3.61 us
  transfers between devices with their start and end apart: 12, of which 5 were waited for; matrix products, arithmetic and copies ran while one was open for 0% of the time, Pallas kernels for 12%

profile of v4, /device:TPU:38, one launch (start us, length us, event | category | flops | bytes accessed | tf_op | source)
XLA Modules:
  0.0 75.4 jit_solution(9997502763356210886)
XLA Ops:
  0.6 0.1 collective-permute-start.1
  0.7 4.6 %collective-permute-start = (f32[64,150]{1,0:T(8,128)}, f32[64,150]{1,0:T(8,128)S(1)}, u32[]{:S(2)}, u32[]{:S(2)}) collective-permute-start(f32[64,150]{1,0:T(8,128)} %own.1), channel_id=1, source_target_pairs={{8,16},{24,32},{40,48},{56,64},{72,80},{88,96},{104,112},{120,128}... | collective-permute-start | bytes 115208 | tf_op jit(solution)/shard_map/ppermute | solution.py:540
  5.3 1.0 %early.1 = (f32[150,128]{1,0:T(8,128)S(1)}, f32[150,128]{1,0:T(8,128)S(1)}) custom-call(f32[64,150]{1,0:T(8,128)} %own.1, s32[5,64]{1,0:T(8,128)} %bitcast.1), custom_call_target="tpu_custom_call" | custom-call | tf_op jit(solution)/shard_map/early/pallas_call | solution.py:513
  6.3 1.8 %taps.1.half = f32[768,512]{1,0:T(8,128)S(1)} custom-call(f32[64,768]{1,0:T(8,128)} %kern_real.1, f32[64,768]{1,0:T(8,128)} %kern_imag.1, bf16[384,512]{1,0:T(8,128)(2,1)} %constant.57.clone.tap_rows), custom_call_target="tpu_custom_call" | custom-call | tf_op jit(solution)/shard_map/taps/pallas_call | solution.py:513
  8.1 0.0 collective-permute-done.1.within
  8.1 0.5 collective-permute-done.across
  8.6 0.1 iota.7.place
  8.7 0.1 prep.1
  8.8 0.9 %collective-permute-start.2 = (f32[176,128]{1,0:T(8,128)S(1)}, f32[176,128]{1,0:T(8,128)S(1)}, u32[]{:S(2)}, u32[]{:S(2)}) collective-permute-start(f32[176,128]{1,0:T(8,128)S(1)} %get-tuple-element.51), channel_id=1, source_target_pairs={{0,1},{2,3},{4,5},{6,7},{1,0},{3,2},{5,4},{7,6},{8,9},{10,11},{12,... | collective-permute-start | bytes 270344 | tf_op jit(solution)/shard_map/ppermute | solution.py:544
  9.8 0.0 copy-start
  9.8 9.3 %collective-permute-start.3 = (f32[176,128]{1,0:T(8,128)S(1)}, f32[176,128]{1,0:T(8,128)S(1)}, u32[]{:S(2)}, u32[]{:S(2)}) collective-permute-start(f32[176,128]{1,0:T(8,128)S(1)} %get-tuple-element.52), channel_id=1, source_target_pairs={{1,2},{3,4},{5,6},{2,1},{4,3},{6,5},{9,10},{11,12},{13,14},{10,9},... | collective-permute-start | bytes 270344 | tf_op jit(solution)/shard_map/ppermute | solution.py:545
  19.0 4.2 %spectra.1 = (f32[4992,256]{1,0:T(8,128)S(1)}, bf16[416,1248]{1,0:T(8,128)(2,1)S(1)}, bf16[176,624]{1,0:T(8,128)(2,1)S(1)}, bf16[176,624]{1,0:T(8,128)(2,1)S(1)}...) custom-call(f32[768,512]{1,0:T(8,128)S(1)} %taps.1.half, ...), custom_call_target="tpu_custom_call" | custom-call | tf_op jit(solution)/shard_map/spectra/pallas_call | solution.py:585
  23.3 0.0 collective-permute-done.2.first
  23.3 0.0 collective-permute-done.3.second
  23.3 0.0 copy-done
  23.3 0.1 broadcast_in_dim.16.weights
  23.4 7.1 %first.1 = (f32[288,128]{1,0:T(8,128)S(1)}, f32[144,128]{1,0:T(8,128)S(1)}, f32[144,128]{1,0:T(8,128)S(1)}, f32[288,128]{1,0:T(8,128)S(1)}, f32[2,112,128]{2,1,0:T(8,128)S(1)}) custom-call(s32[8,256]{1,0:T(8,128)S(1)} %iota.7.place, f32[12,128]{1,0:T(8,128)S(1)} %broadcast_in_dim.16.weights, f32[150,128]{1,0:T(8,128)S(1)} %get-tuple-element.50.own, ...), custom_call_target="tpu_custom_call" | custom-call | tf_op jit(solution)/shard_map/first/pallas_call | solution.py:513
  30.5 4.5 %collective-permute-start.4 = (f32[144,128]{1,0:T(8,128)S(1)}, f32[144,128]{1,0:T(8,128)S(1)}, u32[]{:S(2)}, u32[]{:S(2)}) collective-permute-start(f32[144,128]{1,0:T(8,128)S(1)} %get-tuple-element.69), channel_id=1, source_target_pairs={{8,16},{24,32},{40,48},{56,64},{72,80},{88,96},{104,112},{120,128}... | collective-permute-start | bytes 221192 | tf_op jit(solution)/shard_map/ppermute | solution.py:540
  35.0 0.3 collective-permute-start.5
  35.3 1.1 %slim.1.spec = f32[3456,256]{1,0:T(8,128)S(1)} custom-call(f32[768,512]{1,0:T(8,128)S(1)} %taps.1.half, bf16[144,384]{1,0:T(8,128)(2,1)S(1)} %get-tuple-element.73.tap_cols), custom_call_target="tpu_custom_call" | custom-call | tf_op jit(solution)/shard_map/slim/pallas_call | solution.py:513
  36.4 1.9 %collective-permute-done.4.far = f32[144,128]{1,0:T(8,128)S(1)} collective-permute-done((f32[144,128]{1,0:T(8,128)S(1)}, f32[144,128]{1,0:T(8,128)S(1)}, u32[]{:S(2)}, u32[]{:S(2)}) %collective-permute-start.4) | collective-permute-done | bytes 73760 | tf_op jit(solution)/shard_map/ppermute | solution.py:540
  38.3 0.0 collective-permute-done.5.near
  38.3 4.7 %second.1 = (f32[160,128]{1,0:T(8,128)S(1)}, f32[80,128]{1,0:T(8,128)S(1)}, f32[80,128]{1,0:T(8,128)S(1)}, f32[160,128]{1,0:T(8,128)S(1)}) custom-call(s32[8,256]{1,0:T(8,128)S(1)} %iota.7.place, f32[12,128]{1,0:T(8,128)S(1)} %broadcast_in_dim.16.weights, f32[288,128]{1,0:T(8,128)S(1)} %get-tuple-element.68.own, f32[144,128]{1,0:T(8,128)S(1)} %collective-permute-done.4.far, ...), custom_call_target="tpu_custom_call" | custom-call | tf_op jit(solution)/shard_map/second/pallas_call | solution.py:513
  43.0 4.5 %collective-permute-start.6 = (f32[80,128]{1,0:T(8,128)S(1)}, f32[80,128]{1,0:T(8,128)S(1)}, u32[]{:S(2)}, u32[]{:S(2)}) collective-permute-start(f32[80,128]{1,0:T(8,128)S(1)} %get-tuple-element.81), channel_id=1, source_target_pairs={{8,16},{24,32},{40,48},{56,64},{72,80},{88,96},{104,112},{120,128}... | collective-permute-start | bytes 122888 | tf_op jit(solution)/shard_map/ppermute | solution.py:540
  47.5 0.1 collective-permute-start.7
  47.6 2.8 %collective-permute-done.6.far = f32[80,128]{1,0:T(8,128)S(1)} collective-permute-done((f32[80,128]{1,0:T(8,128)S(1)}, f32[80,128]{1,0:T(8,128)S(1)}, u32[]{:S(2)}, u32[]{:S(2)}) %collective-permute-start.6) | collective-permute-done | bytes 40992 | tf_op jit(solution)/shard_map/ppermute | solution.py:540
  50.4 0.0 collective-permute-done.7.near
  50.4 0.1 update.1
  50.6 0.1 collective-permute-start.8
  50.7 8.2 %collective-permute-start.9 = (f32[64,128]{1,0:T(8,128)S(1)}, f32[64,128]{1,0:T(8,128)S(1)}, u32[]{:S(2)}, u32[]{:S(2)}) collective-permute-start(f32[64,128]{1,0:T(8,128)S(1)} %get-tuple-element.86), channel_id=1, source_target_pairs={{1,2},{3,4},{5,6},{2,1},{4,3},{6,5},{9,10},{11,12},{13,14},{10,9},... | collective-permute-start | bytes 98312 | tf_op jit(solution)/shard_map/ppermute | solution.py:545
  58.9 0.0 collective-permute-done.8.first
  58.9 3.6 %collective-permute-done.9.second = f32[64,128]{1,0:T(8,128)S(1)} collective-permute-done((f32[64,128]{1,0:T(8,128)S(1)}, f32[64,128]{1,0:T(8,128)S(1)}, u32[]{:S(2)}, u32[]{:S(2)}) %collective-permute-start.9) | collective-permute-done | bytes 32800 | tf_op jit(solution)/shard_map/ppermute | solution.py:545
  62.5 4.6 %third.1 = (f32[160,128]{1,0:T(8,128)S(1)}, f32[80,128]{1,0:T(8,128)S(1)}, f32[80,128]{1,0:T(8,128)S(1)}, f32[2,112,128]{2,1,0:T(8,128)S(1)}) custom-call(s32[8,256]{1,0:T(8,128)S(1)} %iota.7.place, f32[12,128]{1,0:T(8,128)S(1)} %broadcast_in_dim.16.weights, f32[160,128]{1,0:T(8,128)S(1)} %get-tuple-element.84.own, ...), custom_call_target="tpu_custom_call" | custom-call | tf_op jit(solution)/shard_map/third/pallas_call | solution.py:513
  67.1 3.4 %collective-permute-start.10 = (f32[80,128]{1,0:T(8,128)S(1)}, f32[80,128]{1,0:T(8,128)S(1)}, u32[]{:S(2)}, u32[]{:S(2)}) collective-permute-start(f32[80,128]{1,0:T(8,128)S(1)} %get-tuple-element.88), channel_id=1, source_target_pairs={{8,16},{24,32},{40,48},{56,64},{72,80},{88,96},{104,112},{120,128}... | collective-permute-start | bytes 122888 | tf_op jit(solution)/shard_map/ppermute | solution.py:540
  70.5 0.1 collective-permute-start.11
  70.6 0.9 %intensity.1 = f32[64,150]{1,0:T(8,128)} custom-call(f32[2,112,128]{2,1,0:T(8,128)S(1)} %get-tuple-element.90.intensity, bf16[80,112]{1,0:T(8,128)(2,1)S(1)} %get-tuple-element.91.mirror), custom_call_target="tpu_custom_call" | custom-call | tf_op jit(solution)/shard_map/intensity/pallas_call | solution.py:513
  71.5 3.1 %collective-permute-done.10.far = f32[80,128]{1,0:T(8,128)S(1)} collective-permute-done((f32[80,128]{1,0:T(8,128)S(1)}, f32[80,128]{1,0:T(8,128)S(1)}, u32[]{:S(2)}, u32[]{:S(2)}) %collective-permute-start.10) | collective-permute-done | bytes 40992 | tf_op jit(solution)/shard_map/ppermute | solution.py:540
  74.6 0.0 collective-permute-done.11.near
  74.6 0.8 %final.1 = f32[64,150]{1,0:T(8,128)} custom-call(s32[8,256]{1,0:T(8,128)S(1)} %iota.7.place, f32[160,128]{1,0:T(8,128)S(1)} %get-tuple-element.87.own, f32[80,128]{1,0:T(8,128)S(1)} %collective-permute-done.10.far, f32[80,128]{1,0:T(8,128)S(1)} %collective-permute-done.11.near), custom_call_target="tpu_custom_call" | custom-call | tf_op jit(solution)/shard_map/final/pallas_call | solution.py:513
  (1 shorter events, 0.0 us)
Async XLA Ops:
  0.6 7.5 %collective-permute-start.1 = (f32[64,150]{1,0:T(8,128)}, f32[64,150]{1,0:T(8,128)S(1)}, u32[]{:S(2)}, u32[]{:S(2)}) collective-permute-start(f32[64,150]{1,0:T(8,128)} %own.1), channel_id=1, source_target_pairs={{0,8},{16,24},{32,40},{48,56},{64,72},{80,88},{96,104},{112,120},{... | collective-permute-start | bytes 115208 | tf_op jit(solution)/shard_map/ppermute | solution.py:541
  0.7 7.9 %collective-permute-start = (f32[64,150]{1,0:T(8,128)}, f32[64,150]{1,0:T(8,128)S(1)}, u32[]{:S(2)}, u32[]{:S(2)}) collective-permute-start(f32[64,150]{1,0:T(8,128)} %own.1), channel_id=1, source_target_pairs={{8,16},{24,32},{40,48},{56,64},{72,80},{88,96},{104,112},{120,128}... | collective-permute-start | bytes 115208 | tf_op jit(solution)/shard_map/ppermute | solution.py:540
  8.8 14.5 %collective-permute-start.2 = (f32[176,128]{1,0:T(8,128)S(1)}, f32[176,128]{1,0:T(8,128)S(1)}, u32[]{:S(2)}, u32[]{:S(2)}) collective-permute-start(f32[176,128]{1,0:T(8,128)S(1)} %get-tuple-element.51), channel_id=1, source_target_pairs={{0,1},{2,3},{4,5},{6,7},{1,0},{3,2},{5,4},{7,6},{8,9},{10,11},{12,... | collective-permute-start | bytes 270344 | tf_op jit(solution)/shard_map/ppermute | solution.py:544
  9.8 13.6 %copy-start = (f32[12]{0:T(128)S(1)}, f32[12]{0:T(128)}, u32[]{:S(2)}) copy-start(f32[12]{0:T(128)} %param.32) | copy-start | bytes 148
  9.8 13.5 %collective-permute-start.3 = (f32[176,128]{1,0:T(8,128)S(1)}, f32[176,128]{1,0:T(8,128)S(1)}, u32[]{:S(2)}, u32[]{:S(2)}) collective-permute-start(f32[176,128]{1,0:T(8,128)S(1)} %get-tuple-element.52), channel_id=1, source_target_pairs={{1,2},{3,4},{5,6},{2,1},{4,3},{6,5},{9,10},{11,12},{13,14},{10,9},... | collective-permute-start | bytes 270344 | tf_op jit(solution)/shard_map/ppermute | solution.py:545
  30.5 7.8 %collective-permute-start.4 = (f32[144,128]{1,0:T(8,128)S(1)}, f32[144,128]{1,0:T(8,128)S(1)}, u32[]{:S(2)}, u32[]{:S(2)}) collective-permute-start(f32[144,128]{1,0:T(8,128)S(1)} %get-tuple-element.69), channel_id=1, source_target_pairs={{8,16},{24,32},{40,48},{56,64},{72,80},{88,96},{104,112},{120,128}... | collective-permute-start | bytes 221192 | tf_op jit(solution)/shard_map/ppermute | solution.py:540
  35.0 3.3 %collective-permute-start.5 = (f32[144,128]{1,0:T(8,128)S(1)}, f32[144,128]{1,0:T(8,128)S(1)}, u32[]{:S(2)}, u32[]{:S(2)}) collective-permute-start(f32[144,128]{1,0:T(8,128)S(1)} %get-tuple-element.70), channel_id=1, source_target_pairs={{0,8},{16,24},{32,40},{48,56},{64,72},{80,88},{96,104},{112,120},{... | collective-permute-start | bytes 221192 | tf_op jit(solution)/shard_map/ppermute | solution.py:541
  43.0 7.4 %collective-permute-start.6 = (f32[80,128]{1,0:T(8,128)S(1)}, f32[80,128]{1,0:T(8,128)S(1)}, u32[]{:S(2)}, u32[]{:S(2)}) collective-permute-start(f32[80,128]{1,0:T(8,128)S(1)} %get-tuple-element.81), channel_id=1, source_target_pairs={{8,16},{24,32},{40,48},{56,64},{72,80},{88,96},{104,112},{120,128}... | collective-permute-start | bytes 122888 | tf_op jit(solution)/shard_map/ppermute | solution.py:540
  47.5 2.9 %collective-permute-start.7 = (f32[80,128]{1,0:T(8,128)S(1)}, f32[80,128]{1,0:T(8,128)S(1)}, u32[]{:S(2)}, u32[]{:S(2)}) collective-permute-start(f32[80,128]{1,0:T(8,128)S(1)} %get-tuple-element.82), channel_id=1, source_target_pairs={{0,8},{16,24},{32,40},{48,56},{64,72},{80,88},{96,104},{112,120},{... | collective-permute-start | bytes 122888 | tf_op jit(solution)/shard_map/ppermute | solution.py:541
  50.6 8.3 %collective-permute-start.8 = (f32[64,128]{1,0:T(8,128)S(1)}, f32[64,128]{1,0:T(8,128)S(1)}, u32[]{:S(2)}, u32[]{:S(2)}) collective-permute-start(f32[64,128]{1,0:T(8,128)S(1)} %get-tuple-element.85), channel_id=1, source_target_pairs={{0,1},{2,3},{4,5},{6,7},{1,0},{3,2},{5,4},{7,6},{8,9},{10,11},{12,... | collective-permute-start | bytes 98312 | tf_op jit(solution)/shard_map/ppermute | solution.py:544
  50.7 11.8 %collective-permute-start.9 = (f32[64,128]{1,0:T(8,128)S(1)}, f32[64,128]{1,0:T(8,128)S(1)}, u32[]{:S(2)}, u32[]{:S(2)}) collective-permute-start(f32[64,128]{1,0:T(8,128)S(1)} %get-tuple-element.86), channel_id=1, source_target_pairs={{1,2},{3,4},{5,6},{2,1},{4,3},{6,5},{9,10},{11,12},{13,14},{10,9},... | collective-permute-start | bytes 98312 | tf_op jit(solution)/shard_map/ppermute | solution.py:545
  67.1 7.4 %collective-permute-start.10 = (f32[80,128]{1,0:T(8,128)S(1)}, f32[80,128]{1,0:T(8,128)S(1)}, u32[]{:S(2)}, u32[]{:S(2)}) collective-permute-start(f32[80,128]{1,0:T(8,128)S(1)} %get-tuple-element.88), channel_id=1, source_target_pairs={{8,16},{24,32},{40,48},{56,64},{72,80},{88,96},{104,112},{120,128}... | collective-permute-start | bytes 122888 | tf_op jit(solution)/shard_map/ppermute | solution.py:540
  70.5 4.1 %collective-permute-start.11 = (f32[80,128]{1,0:T(8,128)S(1)}, f32[80,128]{1,0:T(8,128)S(1)}, u32[]{:S(2)}, u32[]{:S(2)}) collective-permute-start(f32[80,128]{1,0:T(8,128)S(1)} %get-tuple-element.89), channel_id=1, source_target_pairs={{0,8},{16,24},{32,40},{48,56},{64,72},{80,88},{96,104},{112,120},{... | collective-permute-start | bytes 122888 | tf_op jit(solution)/shard_map/ppermute | solution.py:541

commit v5 on v4

--- a/solution.py
+++ b/solution.py
@@ -54,22 +54,38 @@
 
 
 class Geometry:
-    def __init__(self, width):
+    def __init__(self, width, trim):
         self.mask = width
-        self.field = width - 2 * H
+        self.centre = width // 2 - H
+        self.half = self.centre - trim
         self.grad = width - 4 * H
         self.length = width | 1
         self.freqs = (self.length + 1) // 2
         self.freqs_up = up(self.freqs, 16)
         self.mask_up = up(self.mask, 16)
-        self.half = self.field // 2
         self.half_up = up(self.half, 16)
         self.grad_up = up(self.grad, 32)
+
+    def dense(self):
+        return 3 * self.half <= 512 < 3 * self.half_up
+
+    def source_stack(self, table):
+        table = grown(table, self.freqs_up, self.half_up)
+        if not self.dense():
+            return left_stack(table)
+        high, low = halves(table)
+        first, second = high.copy(), high.copy()
+        fit = 512 - 2 * self.half_up
+        spare = self.half_up - self.half
+        rest = self.half - fit
+        first[:, self.half :] = low[:, fit : fit + spare]
+        second[:, self.half : self.half + rest - spare] = low[:, fit + spare : self.half]
+        return np.concatenate([first, second, low[:, :fit]], 1)
 
     def tables(self):
         freq = np.arange(self.freqs)
         fu, hu = self.freqs_up, self.half_up
-        middle = H + (self.field - 1) / 2.0
+        middle = H + self.centre - 0.5
         weight = np.where(freq == 0, 1.0, 2.0) / (self.length * ROWS)
 
         def phases(places):
@@ -94,8 +110,8 @@
             mask_cols=left_stack(complex_table(mask, -1.0, fu, self.mask_up, 0)),
             field_even=left_stack(grown((np.cos(half) * weight[:, None]).T, hu, fu)),
             field_odd=left_stack(grown((np.sin(half) * weight[:, None]).T, hu, fu)),
-            source_even=left_stack(grown(np.cos(half), fu, hu)),
-            source_odd=left_stack(grown(-np.sin(half), fu, hu)),
+            source_even=self.source_stack(np.cos(half)),
+            source_odd=self.source_stack(-np.sin(half)),
             grad_cols=left_stack(grad_table),
             tap_cols=left_stack(complex_table(taps, 1.0, fu, KS, 1)),
         )
@@ -155,6 +171,21 @@
     return jnp.concatenate([dot(part, stacked) for part in rows], 0)
 
 
+def source_dot(geo, table, value):
+    if not geo.dense():
+        return left_dot(table[...], value)
+    fit = 512 - 2 * geo.half_up
+    spare = geo.half_up - geo.half
+    high, low = split(value)
+    tail_high, tail_low = high[fit:].astype(f32)[: geo.half - fit], low[fit:].astype(f32)
+    first = jnp.concatenate([tail_high, tail_high[:spare]], 0).astype(bf16)
+    rest = tail_high[spare:]
+    blank = jnp.zeros((spare - rest.shape[0], value.shape[1]), f32)
+    second = jnp.concatenate([tail_low[: geo.half - fit], rest, blank], 0).astype(bf16)
+    stacked = jnp.concatenate([high[:fit], first, low[:fit], second, high[:fit]], 0)
+    return dot(table[...], stacked)
+
+
 def right_dot(value, table, parts=1):
     high, low = split(value)
     stacked = jnp.concatenate([high, low, high], 1)
@@ -192,29 +223,34 @@
         out[(2 * k + 1) * count : (2 * k + 2) * count, :] = spec[:, 256:]
 
 
-def taps_kernel(kern_real, kern_imag, tap_rows, half):
-    both = jnp.concatenate([kern_real[...], kern_imag[...]], 0)
-    for start in range(0, both.shape[1], 128):
-        part = both[:, start : start + 128].T
-        half[start : start + 128, :] = right_dot(part, tap_rows[...])
-
-
-def setup_kernel(geo, held, half, tap_cols, *rest):
-    sources, out, rest = rest[:held], rest[held], rest[held + 1 :]
-    targets, sems = rest[:held], rest[held]
+def bring(sources, targets, sems):
     copies = [
         pltpu.make_async_copy(source, target, sems.at[index])
         for index, (source, target) in enumerate(zip(sources, targets))
     ]
     for copy in copies:
         copy.start()
+    return copies
+
+
+def setup_kernel(geo, held, kern_real, kern_imag, tap_rows, tap_cols, *rest):
+    sources, (half, out), rest = rest[:held], rest[held : held + 2], rest[held + 2 :]
+    copies = bring(sources, rest[:held], rest[held])
+    both = jnp.concatenate([kern_real[...], kern_imag[...]], 0)
+    for start in range(0, both.shape[1], 128):
+        part = both[:, start : start + 128].T
+        half[start : start + 128, :] = right_dot(part, tap_rows[...])
     column_spectra(geo, half, tap_cols, out)
     for copy in copies:
         copy.wait()
 
 
-def slim_kernel(geo, half, tap_cols, out):
+def slim_kernel(geo, held, half, tap_cols, *rest):
+    sources, out, rest = rest[:held], rest[held], rest[held + 1 :]
+    copies = bring(sources, rest[:held], rest[held])
     column_spectra(geo, half, tap_cols, out)
+    for copy in copies:
+        copy.wait()
 
 
 def one_step(geo, mask, target, inside, weights, spec, tabs, fields):
@@ -281,8 +317,8 @@
         )
         for side in (0, 1)
     )
-    even = left_dot(tabs["source_even"][...], right + left)
-    odd = left_dot(tabs["source_odd"][...], right - left)
+    even = source_dot(geo, tabs["source_even"], right + left)
+    odd = source_dot(geo, tabs["source_odd"], right - left)
     totals = []
     for start, stop in chunks(count, 2):
         size = stop - start
@@ -406,7 +442,7 @@
 
 
 def field_window(geo, place, tile, whole, col_offset):
-    middle = place[1:2, :128] * tile[1] + col_offset + H + geo.half
+    middle = place[1:2, :128] * tile[1] + col_offset + H + geo.centre
     step = lax.broadcasted_iota(jnp.int32, (geo.half_up, 128), 0)
     return [(col >= 0) & (col < whole[1]) for col in (middle + step, middle - 1 - step)]
 
@@ -434,7 +470,7 @@
         goal[start + 48 : start + 96, :] = jnp.where(left_lanes, turned, packed)
     goal[96 : 96 + cols, :] = target[...]
     goals = [
-        goal[geo.half : geo.half + geo.half_up, :],
+        goal[geo.centre : geo.centre + geo.half_up, :],
         dot(mirror[...], goal[0 : mirror.shape[1], :].astype(bf16)),
     ]
     for side in (0, 1):
@@ -544,11 +580,10 @@
         first = lax.ppermute(to_first, "col", swaps(cols, 0))
         return first, lax.ppermute(to_second, "col", swaps(cols, 1))
 
-    wide, slim = Geometry(tile[1] + 8 * H), Geometry(tile[1] + 4 * H)
+    wide, slim = Geometry(tile[1] + 8 * H, 1), Geometry(tile[1] + 4 * H, 0)
     shared = row_tables()
-    shared["wide_mirror"] = mirror_table(wide.half, wide.half_up, wide.half_up)
+    shared["wide_mirror"] = mirror_table(wide.centre, wide.half_up, wide.half_up)
     shared["slim_mirror"] = mirror_table(tile[1] // 2, up(tile[1] // 2, 16), slim.half_up)
-    made = {"wide": wide.tables(), "slim": slim.tables(), "shared": shared}
     n = tile[1]
     far, near = row_exchange(mask_params, mask_params)
     params, target = call(
@@ -559,15 +594,6 @@
         [mask_params, target_bits.T],
         pltpu.HBM,
     )
-    (half_spec,) = call(
-        taps_kernel,
-        "taps",
-        [(kernels * KS, 512)],
-        [],
-        [kern_real, kern_imag, jnp.asarray(shared["tap_rows"])],
-        pltpu.HBM,
-    )
-    near, half_spec = lax.optimization_barrier((near, half_spec))
     params, to_first, to_second = call(
         prep_kernel,
         "prep",
@@ -576,24 +602,42 @@
         [place, params, target, far, near],
     )
     first, second = col_exchange(to_first, to_second)
-    names = [(label, name) for label in ("wide", "slim") for name in COLUMN_TABLES]
-    names += [("shared", name) for name in ROW_TABLES + ("wide_mirror", "slim_mirror")]
-    names += [("slim", "tap_cols")]
-    tables = [jnp.asarray(made[label][name]) for label, name in names]
-    arrays = [half_spec, jnp.asarray(made["wide"]["tap_cols"])] + tables
-    spaces = [pltpu.VMEM] + [pltpu.HBM] * (1 + len(tables))
-    wide_spec, *held = pl.pallas_call(
-        functools.partial(setup_kernel, wide, len(tables)),
-        name="spectra",
-        out_shape=[pltpu.VMEM((2 * kernels * wide.freqs_up, 256), f32)]
-        + [pltpu.VMEM(table.shape, table.dtype) for table in tables],
-        in_specs=[pl.BlockSpec(memory_space=pltpu.VMEM)] * 2
-        + [pl.BlockSpec(memory_space=pltpu.HBM)] * len(tables),
-        out_specs=[pl.BlockSpec(memory_space=pltpu.VMEM)] * (1 + len(tables)),
-        scratch_shapes=[pltpu.SemaphoreType.DMA((len(tables),))],
-        compiler_params=pltpu.CompilerParams(vmem_limit_bytes=VMEM_LIMIT),
-    )(*[pltpu.with_memory_space_constraint(*pair) for pair in zip(arrays, spaces)])
-    place_of = {key: table for key, table in zip(names, held)}
+    made = {"wide": wide.tables(), "slim": slim.tables(), "shared": shared}
+    place_of = {}
+
+    def loader(kernel, name, geo, out_shapes, inputs, spaces, names):
+        tables = [jnp.asarray(made[label][part]) for label, part in names]
+        arrays = list(zip(inputs + tables, spaces + [pltpu.HBM] * len(tables)))
+        outs = pl.pallas_call(
+            functools.partial(kernel, geo, len(tables)),
+            name=name,
+            out_shape=[pltpu.VMEM(shape, f32) for shape in out_shapes]
+            + [pltpu.VMEM(table.shape, table.dtype) for table in tables],
+            in_specs=[pl.BlockSpec(memory_space=pltpu.VMEM)] * len(inputs)
+            + [pl.BlockSpec(memory_space=pltpu.HBM)] * len(tables),
+            out_specs=[pl.BlockSpec(memory_space=pltpu.VMEM)]
+            * (len(out_shapes) + len(tables)),
+            scratch_shapes=[pltpu.SemaphoreType.DMA((len(tables),))],
+            compiler_params=pltpu.CompilerParams(vmem_limit_bytes=VMEM_LIMIT),
+        )(*[pltpu.with_memory_space_constraint(*pair) for pair in arrays])
+        place_of.update(zip(names, outs[len(out_shapes) :]))
+        return outs[: len(out_shapes)]
+
+    half_spec, wide_spec = loader(
+        setup_kernel,
+        "spectra",
+        wide,
+        [(kernels * KS, 512), (2 * kernels * wide.freqs_up, 256)],
+        [
+            kern_real,
+            kern_imag,
+            jnp.asarray(shared["tap_rows"]),
+            jnp.asarray(made["wide"]["tap_cols"]),
+        ],
+        [pltpu.HBM] * 4,
+        [("wide", part) for part in COLUMN_TABLES]
+        + [("shared", part) for part in ROW_TABLES + ("wide_mirror",)],
+    )
 
     def tabs(label):
         return [place_of[label, name] for name in COLUMN_TABLES] + [
@@ -610,17 +654,19 @@
         functools.partial(first_kernel, wide, tile, whole),
         "first",
         spreads(wide) + [(slim.mask_up, 128), (2, slim.half_up, 128)],
-        [(wide.mask_up, 128), (wide.half + wide.half_up, 128), fields(wide)],
+        [(wide.mask_up, 128), (wide.centre + wide.half_up, 128), fields(wide)],
         [place, weights, params, target, first, second, wide_spec]
         + [place_of["shared", "wide_mirror"], *tabs("wide")],
     )
     far, near = row_exchange(to_far, to_near)
-    (slim_spec,) = call(
-        functools.partial(slim_kernel, slim),
+    (slim_spec,) = loader(
+        slim_kernel,
         "slim",
+        slim,
         [(2 * kernels * slim.freqs_up, 256)],
-        [],
-        [half_spec, place_of["slim", "tap_cols"]],
+        [half_spec, jnp.asarray(made["slim"]["tap_cols"])],
+        [pltpu.VMEM, pltpu.HBM],
+        [("slim", part) for part in COLUMN_TABLES] + [("shared", "slim_mirror")],
     )
     spread, to_far, to_near, params = call(
         functools.partial(second_kernel, slim, tile, whole),

time: 75.9 us -> 75.5 us (level)
  Pallas kernels: 26.5 us -> 25.7 us
    pallas_call x10 -> x8, Pallas kernels: 22.3 us -> 19 us  [call(): pl.pallas_call(kernel, name=name, out_shape=[shape if isinstance(shape, j...]
    pallas_call x1 -> x2, Pallas kernels: 4.23 us -> 6.62 us  [loader(): pl.pallas_call(functools.partial(kernel, geo, len(tables)), name=name, ou...]
    ppermute x4, starting transfers between devices: 16.9 us -> 18 us  [row_exchange(): far = lax.ppermute(to_far, 'row', swaps(rows, 1))]
  transfers between devices with their start and end apart: 12 -> 12, of which waited for: 5 -> 5; matrix products, arithmetic and copies ran while one was open for 0% -> 0% of each run, Pallas kernels for 12% -> 11%
where the time goes in v5:
time: 75.5 us; the launch traced here: 74.8 us
  starting transfers between devices  36.5 us (48%)
  Pallas kernels  25.7 us (34%)
  waiting for transfers between devices  11.7 us (15%)
  between operations  0.8 us (1%)
    pallas_call x8, Pallas kernels, call(): pl.pallas_call(kernel, name=name, out_shape=[shape if isinstance(shape, j...  19 us
    ppermute x4, starting transfers between devices, row_exchange(): far = lax.ppermute(to_far, 'row', swaps(rows, 1))  18 us
    ppermute x2, starting transfers between devices, col_exchange(): return (first, lax.ppermute(to_second, 'col', swaps(cols, 1)))  16.9 us
    ppermute x4, waiting for transfers between devices, row_exchange(): far = lax.ppermute(to_far, 'row', swaps(rows, 1))  7.86 us
    pallas_call x2, Pallas kernels, loader(): pl.pallas_call(functools.partial(kernel, geo, len(tables)), name=name, ou...  6.62 us
    ppermute x2, waiting for transfers between devices, col_exchange(): return (first, lax.ppermute(to_second, 'col', swaps(cols, 1)))  3.87 us
  transfers between devices with their start and end apart: 12, of which 5 were waited for; matrix products, arithmetic and copies ran while one was open for 0% of the time, Pallas kernels for 11%

profile of v5, /device:TPU:38, one launch (start us, length us, event | category | flops | bytes accessed | tf_op | source)
XLA Modules:
  0.0 74.8 jit_solution(16059387519423131503)
XLA Ops:
  0.6 0.1 collective-permute-start.1
  0.7 4.6 %collective-permute-start = (f32[64,150]{1,0:T(8,128)}, f32[64,150]{1,0:T(8,128)S(1)}, u32[]{:S(2)}, u32[]{:S(2)}) collective-permute-start(f32[64,150]{1,0:T(8,128)} %own.1), channel_id=1, source_target_pairs={{8,16},{24,32},{40,48},{56,64},{72,80},{88,96},{104,112},{120,128}... | collective-permute-start | bytes 115208 | tf_op jit(solution)/shard_map/ppermute | solution.py:576
  5.3 1.0 %early.1 = (f32[150,128]{1,0:T(8,128)S(1)}, f32[150,128]{1,0:T(8,128)S(1)}) custom-call(f32[64,150]{1,0:T(8,128)} %own.1, s32[5,64]{1,0:T(8,128)} %bitcast.1), custom_call_target="tpu_custom_call" | custom-call | tf_op jit(solution)/shard_map/early/pallas_call | solution.py:549
  6.3 0.0 collective-permute-done.1.within
  6.3 2.3 %collective-permute-done.across = f32[64,150]{1,0:T(8,128)S(1)} collective-permute-done((f32[64,150]{1,0:T(8,128)}, f32[64,150]{1,0:T(8,128)S(1)}, u32[]{:S(2)}, u32[]{:S(2)}) %collective-permute-start) | collective-permute-done | bytes 38432 | tf_op jit(solution)/shard_map/ppermute | solution.py:576
  8.6 0.1 iota.7.place
  8.7 0.1 prep.1
  8.8 0.9 %collective-permute-start.2 = (f32[176,128]{1,0:T(8,128)S(1)}, f32[176,128]{1,0:T(8,128)S(1)}, u32[]{:S(2)}, u32[]{:S(2)}) collective-permute-start(f32[176,128]{1,0:T(8,128)S(1)} %get-tuple-element.49), channel_id=1, source_target_pairs={{0,1},{2,3},{4,5},{6,7},{1,0},{3,2},{5,4},{7,6},{8,9},{10,11},{12,... | collective-permute-start | bytes 270344 | tf_op jit(solution)/shard_map/ppermute | solution.py:580
  9.8 0.0 copy-start
  9.8 8.9 %collective-permute-start.3 = (f32[176,128]{1,0:T(8,128)S(1)}, f32[176,128]{1,0:T(8,128)S(1)}, u32[]{:S(2)}, u32[]{:S(2)}) collective-permute-start(f32[176,128]{1,0:T(8,128)S(1)} %get-tuple-element.50), channel_id=1, source_target_pairs={{1,2},{3,4},{5,6},{2,1},{4,3},{6,5},{9,10},{11,12},{13,14},{10,9},... | collective-permute-start | bytes 270344 | tf_op jit(solution)/shard_map/ppermute | solution.py:581
  18.7 4.4 %spectra.1 = (f32[768,512]{1,0:T(8,128)S(1)}, f32[4992,256]{1,0:T(8,128)S(1)}, bf16[416,1248]{1,0:T(8,128)(2,1)S(1)}, bf16[176,624]{1,0:T(8,128)(2,1)S(1)}, bf16...) custom-call(f32[64,768]{1,0:T(8,128)} %kern_real.1, ...), custom_call_target="tpu_custom_call" | custom-call | tf_op jit(solution)/shard_map/spectra/pallas_call | solution.py:611
  23.1 0.0 collective-permute-done.2.first
  23.1 0.0 collective-permute-done.3.second
  23.1 0.0 copy-done
  23.1 0.1 broadcast_in_dim.16.weights
  23.2 6.8 %first.1 = (f32[288,128]{1,0:T(8,128)S(1)}, f32[144,128]{1,0:T(8,128)S(1)}, f32[144,128]{1,0:T(8,128)S(1)}, f32[288,128]{1,0:T(8,128)S(1)}, f32[2,112,128]{2,1,0:T(8,128)S(1)}) custom-call(s32[8,256]{1,0:T(8,128)S(1)} %iota.7.place, f32[12,128]{1,0:T(8,128)S(1)} %broadcast_in_dim.16.weights, f32[150,128]{1,0:T(8,128)S(1)} %get-tuple-element.48.own, ...), custom_call_target="tpu_custom_call" | custom-call | tf_op jit(solution)/shard_map/first/pallas_call | solution.py:549
  29.9 4.9 %collective-permute-start.4 = (f32[144,128]{1,0:T(8,128)S(1)}, f32[144,128]{1,0:T(8,128)S(1)}, u32[]{:S(2)}, u32[]{:S(2)}) collective-permute-start(f32[144,128]{1,0:T(8,128)S(1)} %get-tuple-element.66), channel_id=1, source_target_pairs={{8,16},{24,32},{40,48},{56,64},{72,80},{88,96},{104,112},{120,128}... | collective-permute-start | bytes 221192 | tf_op jit(solution)/shard_map/ppermute | solution.py:576
  34.8 0.3 collective-permute-start.5
  35.1 2.2 %slim.1 = (f32[3456,256]{1,0:T(8,128)S(1)}, bf16[288,864]{1,0:T(8,128)(2,1)S(1)}, bf16[112,432]{1,0:T(8,128)(2,1)S(1)}, bf16[112,432]{1,0:T(8,128)(2,1)S(1)}, bf...) custom-call(f32[768,512]{1,0:T(8,128)S(1)} %get-tuple-element.70.hal, ...), custom_call_target="tpu_custom_call" | custom-call | tf_op jit(solution)/shard_map/slim/pallas_call | solution.py:611
  37.4 0.4 collective-permute-done.4.far
  37.7 0.0 collective-permute-done.5.near
  37.7 4.8 %second.1 = (f32[160,128]{1,0:T(8,128)S(1)}, f32[80,128]{1,0:T(8,128)S(1)}, f32[80,128]{1,0:T(8,128)S(1)}, f32[160,128]{1,0:T(8,128)S(1)}) custom-call(s32[8,256]{1,0:T(8,128)S(1)} %iota.7.place, f32[12,128]{1,0:T(8,128)S(1)} %broadcast_in_dim.16.weights, f32[288,128]{1,0:T(8,128)S(1)} %get-tuple-element.65.own, f32[144,128]{1,0:T(8,128)S(1)} %collective-permute-done.4.far, ...), custom_call_target="tpu_custom_call" | custom-call | tf_op jit(solution)/shard_map/second/pallas_call | solution.py:549
  42.5 4.9 %collective-permute-start.6 = (f32[80,128]{1,0:T(8,128)S(1)}, f32[80,128]{1,0:T(8,128)S(1)}, u32[]{:S(2)}, u32[]{:S(2)}) collective-permute-start(f32[80,128]{1,0:T(8,128)S(1)} %get-tuple-element.79), channel_id=1, source_target_pairs={{8,16},{24,32},{40,48},{56,64},{72,80},{88,96},{104,112},{120,128}... | collective-permute-start | bytes 122888 | tf_op jit(solution)/shard_map/ppermute | solution.py:576
  47.4 0.1 collective-permute-start.7
  47.5 2.4 %collective-permute-done.6.far = f32[80,128]{1,0:T(8,128)S(1)} collective-permute-done((f32[80,128]{1,0:T(8,128)S(1)}, f32[80,128]{1,0:T(8,128)S(1)}, u32[]{:S(2)}, u32[]{:S(2)}) %collective-permute-start.6) | collective-permute-done | bytes 40992 | tf_op jit(solution)/shard_map/ppermute | solution.py:576
  49.9 0.0 collective-permute-done.7.near
  49.9 0.1 update.1
  50.0 0.1 collective-permute-start.8
  50.1 8.0 %collective-permute-start.9 = (f32[64,128]{1,0:T(8,128)S(1)}, f32[64,128]{1,0:T(8,128)S(1)}, u32[]{:S(2)}, u32[]{:S(2)}) collective-permute-start(f32[64,128]{1,0:T(8,128)S(1)} %get-tuple-element.84), channel_id=1, source_target_pairs={{1,2},{3,4},{5,6},{2,1},{4,3},{6,5},{9,10},{11,12},{13,14},{10,9},... | collective-permute-start | bytes 98312 | tf_op jit(solution)/shard_map/ppermute | solution.py:581
  58.1 0.0 collective-permute-done.8.first
  58.1 3.8 %collective-permute-done.9.second = f32[64,128]{1,0:T(8,128)S(1)} collective-permute-done((f32[64,128]{1,0:T(8,128)S(1)}, f32[64,128]{1,0:T(8,128)S(1)}, u32[]{:S(2)}, u32[]{:S(2)}) %collective-permute-start.9) | collective-permute-done | bytes 32800 | tf_op jit(solution)/shard_map/ppermute | solution.py:581
  62.0 4.6 %third.1 = (f32[160,128]{1,0:T(8,128)S(1)}, f32[80,128]{1,0:T(8,128)S(1)}, f32[80,128]{1,0:T(8,128)S(1)}, f32[2,112,128]{2,1,0:T(8,128)S(1)}) custom-call(s32[8,256]{1,0:T(8,128)S(1)} %iota.7.place, f32[12,128]{1,0:T(8,128)S(1)} %broadcast_in_dim.16.weights, f32[160,128]{1,0:T(8,128)S(1)} %get-tuple-element.82.own, ...), custom_call_target="tpu_custom_call" | custom-call | tf_op jit(solution)/shard_map/third/pallas_call | solution.py:549
  66.6 3.7 %collective-permute-start.10 = (f32[80,128]{1,0:T(8,128)S(1)}, f32[80,128]{1,0:T(8,128)S(1)}, u32[]{:S(2)}, u32[]{:S(2)}) collective-permute-start(f32[80,128]{1,0:T(8,128)S(1)} %get-tuple-element.86), channel_id=1, source_target_pairs={{8,16},{24,32},{40,48},{56,64},{72,80},{88,96},{104,112},{120,128}... | collective-permute-start | bytes 122888 | tf_op jit(solution)/shard_map/ppermute | solution.py:576
  70.3 0.1 collective-permute-start.11
  70.4 0.9 %intensity.1 = f32[64,150]{1,0:T(8,128)} custom-call(f32[2,112,128]{2,1,0:T(8,128)S(1)} %get-tuple-element.88.intensity, bf16[80,112]{1,0:T(8,128)(2,1)S(1)} %get-tuple-element.89.mirror), custom_call_target="tpu_custom_call" | custom-call | tf_op jit(solution)/shard_map/intensity/pallas_call | solution.py:549
  71.3 2.7 %collective-permute-done.10.far = f32[80,128]{1,0:T(8,128)S(1)} collective-permute-done((f32[80,128]{1,0:T(8,128)S(1)}, f32[80,128]{1,0:T(8,128)S(1)}, u32[]{:S(2)}, u32[]{:S(2)}) %collective-permute-start.10) | collective-permute-done | bytes 40992 | tf_op jit(solution)/shard_map/ppermute | solution.py:576
  74.0 0.0 collective-permute-done.11.near
  74.0 0.8 %final.1 = f32[64,150]{1,0:T(8,128)} custom-call(s32[8,256]{1,0:T(8,128)S(1)} %iota.7.place, f32[160,128]{1,0:T(8,128)S(1)} %get-tuple-element.85.own, f32[80,128]{1,0:T(8,128)S(1)} %collective-permute-done.10.far, f32[80,128]{1,0:T(8,128)S(1)} %collective-permute-done.11.near), custom_call_target="tpu_custom_call" | custom-call | tf_op jit(solution)/shard_map/final/pallas_call | solution.py:549
  (1 shorter events, 0.0 us)
Async XLA Ops:
  0.6 5.7 %collective-permute-start.1 = (f32[64,150]{1,0:T(8,128)}, f32[64,150]{1,0:T(8,128)S(1)}, u32[]{:S(2)}, u32[]{:S(2)}) collective-permute-start(f32[64,150]{1,0:T(8,128)} %own.1), channel_id=1, source_target_pairs={{0,8},{16,24},{32,40},{48,56},{64,72},{80,88},{96,104},{112,120},{... | collective-permute-start | bytes 115208 | tf_op jit(solution)/shard_map/ppermute | solution.py:577
  0.7 7.9 %collective-permute-start = (f32[64,150]{1,0:T(8,128)}, f32[64,150]{1,0:T(8,128)S(1)}, u32[]{:S(2)}, u32[]{:S(2)}) collective-permute-start(f32[64,150]{1,0:T(8,128)} %own.1), channel_id=1, source_target_pairs={{8,16},{24,32},{40,48},{56,64},{72,80},{88,96},{104,112},{120,128}... | collective-permute-start | bytes 115208 | tf_op jit(solution)/shard_map/ppermute | solution.py:576
  8.8 14.2 %collective-permute-start.2 = (f32[176,128]{1,0:T(8,128)S(1)}, f32[176,128]{1,0:T(8,128)S(1)}, u32[]{:S(2)}, u32[]{:S(2)}) collective-permute-start(f32[176,128]{1,0:T(8,128)S(1)} %get-tuple-element.49), channel_id=1, source_target_pairs={{0,1},{2,3},{4,5},{6,7},{1,0},{3,2},{5,4},{7,6},{8,9},{10,11},{12,... | collective-permute-start | bytes 270344 | tf_op jit(solution)/shard_map/ppermute | solution.py:580
  9.8 13.4 %copy-start = (f32[12]{0:T(128)S(1)}, f32[12]{0:T(128)}, u32[]{:S(2)}) copy-start(f32[12]{0:T(128)} %param.32) | copy-start | bytes 148
  9.8 13.4 %collective-permute-start.3 = (f32[176,128]{1,0:T(8,128)S(1)}, f32[176,128]{1,0:T(8,128)S(1)}, u32[]{:S(2)}, u32[]{:S(2)}) collective-permute-start(f32[176,128]{1,0:T(8,128)S(1)} %get-tuple-element.50), channel_id=1, source_target_pairs={{1,2},{3,4},{5,6},{2,1},{4,3},{6,5},{9,10},{11,12},{13,14},{10,9},... | collective-permute-start | bytes 270344 | tf_op jit(solution)/shard_map/ppermute | solution.py:581
  29.9 7.8 %collective-permute-start.4 = (f32[144,128]{1,0:T(8,128)S(1)}, f32[144,128]{1,0:T(8,128)S(1)}, u32[]{:S(2)}, u32[]{:S(2)}) collective-permute-start(f32[144,128]{1,0:T(8,128)S(1)} %get-tuple-element.66), channel_id=1, source_target_pairs={{8,16},{24,32},{40,48},{56,64},{72,80},{88,96},{104,112},{120,128}... | collective-permute-start | bytes 221192 | tf_op jit(solution)/shard_map/ppermute | solution.py:576
  34.8 2.9 %collective-permute-start.5 = (f32[144,128]{1,0:T(8,128)S(1)}, f32[144,128]{1,0:T(8,128)S(1)}, u32[]{:S(2)}, u32[]{:S(2)}) collective-permute-start(f32[144,128]{1,0:T(8,128)S(1)} %get-tuple-element.67), channel_id=1, source_target_pairs={{0,8},{16,24},{32,40},{48,56},{64,72},{80,88},{96,104},{112,120},{... | collective-permute-start | bytes 221192 | tf_op jit(solution)/shard_map/ppermute | solution.py:577
  42.5 7.4 %collective-permute-start.6 = (f32[80,128]{1,0:T(8,128)S(1)}, f32[80,128]{1,0:T(8,128)S(1)}, u32[]{:S(2)}, u32[]{:S(2)}) collective-permute-start(f32[80,128]{1,0:T(8,128)S(1)} %get-tuple-element.79), channel_id=1, source_target_pairs={{8,16},{24,32},{40,48},{56,64},{72,80},{88,96},{104,112},{120,128}... | collective-permute-start | bytes 122888 | tf_op jit(solution)/shard_map/ppermute | solution.py:576
  47.4 2.5 %collective-permute-start.7 = (f32[80,128]{1,0:T(8,128)S(1)}, f32[80,128]{1,0:T(8,128)S(1)}, u32[]{:S(2)}, u32[]{:S(2)}) collective-permute-start(f32[80,128]{1,0:T(8,128)S(1)} %get-tuple-element.80), channel_id=1, source_target_pairs={{0,8},{16,24},{32,40},{48,56},{64,72},{80,88},{96,104},{112,120},{... | collective-permute-start | bytes 122888 | tf_op jit(solution)/shard_map/ppermute | solution.py:577
  50.0 8.1 %collective-permute-start.8 = (f32[64,128]{1,0:T(8,128)S(1)}, f32[64,128]{1,0:T(8,128)S(1)}, u32[]{:S(2)}, u32[]{:S(2)}) collective-permute-start(f32[64,128]{1,0:T(8,128)S(1)} %get-tuple-element.83), channel_id=1, source_target_pairs={{0,1},{2,3},{4,5},{6,7},{1,0},{3,2},{5,4},{7,6},{8,9},{10,11},{12,... | collective-permute-start | bytes 98312 | tf_op jit(solution)/shard_map/ppermute | solution.py:580
  50.1 11.8 %collective-permute-start.9 = (f32[64,128]{1,0:T(8,128)S(1)}, f32[64,128]{1,0:T(8,128)S(1)}, u32[]{:S(2)}, u32[]{:S(2)}) collective-permute-start(f32[64,128]{1,0:T(8,128)S(1)} %get-tuple-element.84), channel_id=1, source_target_pairs={{1,2},{3,4},{5,6},{2,1},{4,3},{6,5},{9,10},{11,12},{13,14},{10,9},... | collective-permute-start | bytes 98312 | tf_op jit(solution)/shard_map/ppermute | solution.py:581
  66.6 7.4 %collective-permute-start.10 = (f32[80,128]{1,0:T(8,128)S(1)}, f32[80,128]{1,0:T(8,128)S(1)}, u32[]{:S(2)}, u32[]{:S(2)}) collective-permute-start(f32[80,128]{1,0:T(8,128)S(1)} %get-tuple-element.86), channel_id=1, source_target_pairs={{8,16},{24,32},{40,48},{56,64},{72,80},{88,96},{104,112},{120,128}... | collective-permute-start | bytes 122888 | tf_op jit(solution)/shard_map/ppermute | solution.py:576
  70.3 3.7 %collective-permute-start.11 = (f32[80,128]{1,0:T(8,128)S(1)}, f32[80,128]{1,0:T(8,128)S(1)}, u32[]{:S(2)}, u32[]{:S(2)}) collective-permute-start(f32[80,128]{1,0:T(8,128)S(1)} %get-tuple-element.87), channel_id=1, source_target_pairs={{0,8},{16,24},{32,40},{48,56},{64,72},{80,88},{96,104},{112,120},{... | collective-permute-start | bytes 122888 | tf_op jit(solution)/shard_map/ppermute | solution.py:577

commit v6 on v5

--- a/solution.py
+++ b/solution.py
@@ -594,6 +594,7 @@
         [mask_params, target_bits.T],
         pltpu.HBM,
     )
+    near, place, weights = lax.optimization_barrier((near, place, weights))
     params, to_first, to_second = call(
         prep_kernel,
         "prep",

time: 75.5 us -> 75.2 us (level)
    ppermute x4, waiting for transfers between devices: 7.86 us -> 7.1 us  [row_exchange(): far = lax.ppermute(to_far, 'row', swaps(rows, 1))]
  transfers between devices with their start and end apart: 12 -> 12, of which waited for: 5 -> 5; matrix products, arithmetic and copies ran while one was open for 0% -> 1% of each run, Pallas kernels for 11% -> 11%
where the time goes in v6:
time: 75.2 us; the launch traced here: 74.6 us
  starting transfers between devices  36.3 us (48%)
  Pallas kernels  25.7 us (34%)
  waiting for transfers between devices  11 us (15%)
  between operations  0.8 us (1%)
  local copies, waits for them, and re-layouts  0.79 us (1%)
    pallas_call x8, Pallas kernels, call(): pl.pallas_call(kernel, name=name, out_shape=[shape if isinstance(shape, j...  19.1 us
    ppermute x4, starting transfers between devices, row_exchange(): far = lax.ppermute(to_far, 'row', swaps(rows, 1))  18 us
    ppermute x2, starting transfers between devices, col_exchange(): return (first, lax.ppermute(to_second, 'col', swaps(cols, 1)))  16.8 us
    ppermute x4, waiting for transfers between devices, row_exchange(): far = lax.ppermute(to_far, 'row', swaps(rows, 1))  7.1 us
    pallas_call x2, Pallas kernels, loader(): pl.pallas_call(functools.partial(kernel, geo, len(tables)), name=name, ou...  6.63 us
    ppermute x2, waiting for transfers between devices, col_exchange(): return (first, lax.ppermute(to_second, 'col', swaps(cols, 1)))  3.85 us
  transfers between devices with their start and end apart: 12, of which 5 were waited for; matrix products, arithmetic and copies ran while one was open for 1% of the time, Pallas kernels for 11%

profile of v6, /device:TPU:38, one launch (start us, length us, event | category | flops | bytes accessed | tf_op | source)
XLA Modules:
  0.0 74.6 jit_solution(13345576184824802724)
XLA Ops:
  0.6 0.1 collective-permute-start
  0.7 4.6 %collective-permute-start.1 = (f32[64,150]{1,0:T(8,128)}, f32[64,150]{1,0:T(8,128)S(1)}, u32[]{:S(2)}, u32[]{:S(2)}) collective-permute-start(f32[64,150]{1,0:T(8,128)} %own.1), channel_id=1, source_target_pairs={{8,16},{24,32},{40,48},{56,64},{72,80},{88,96},{104,112},{120,128}... | collective-permute-start | bytes 115208 | tf_op jit(solution)/shard_map/ppermute | solution.py:576
  5.3 1.0 %early.1 = (f32[150,128]{1,0:T(8,128)S(1)}, f32[150,128]{1,0:T(8,128)S(1)}) custom-call(f32[64,150]{1,0:T(8,128)} %own.1, s32[5,64]{1,0:T(8,128)} %bitcast.1), custom_call_target="tpu_custom_call" | custom-call | tf_op jit(solution)/shard_map/early/pallas_call | solution.py:549
  6.3 0.0 collective-permute-done.within
  6.3 0.1 iota.7.place
  6.4 0.7 broadcast_in_dim.16.weights
  7.1 1.5 %collective-permute-done.1.across = f32[64,150]{1,0:T(8,128)S(1)} collective-permute-done((f32[64,150]{1,0:T(8,128)}, f32[64,150]{1,0:T(8,128)S(1)}, u32[]{:S(2)}, u32[]{:S(2)}) %collective-permute-start.1) | collective-permute-done | bytes 38432 | tf_op jit(solution)/shard_map/ppermute | solution.py:576
  8.6 0.1 prep.1
  8.8 0.9 %collective-permute-start.2 = (f32[176,128]{1,0:T(8,128)S(1)}, f32[176,128]{1,0:T(8,128)S(1)}, u32[]{:S(2)}, u32[]{:S(2)}) collective-permute-start(f32[176,128]{1,0:T(8,128)S(1)} %get-tuple-element.55), channel_id=1, source_target_pairs={{0,1},{2,3},{4,5},{6,7},{1,0},{3,2},{5,4},{7,6},{8,9},{10,11},{12,... | collective-permute-start | bytes 270344 | tf_op jit(solution)/shard_map/ppermute | solution.py:580
  9.7 8.8 %collective-permute-start.3 = (f32[176,128]{1,0:T(8,128)S(1)}, f32[176,128]{1,0:T(8,128)S(1)}, u32[]{:S(2)}, u32[]{:S(2)}) collective-permute-start(f32[176,128]{1,0:T(8,128)S(1)} %get-tuple-element.56), channel_id=1, source_target_pairs={{1,2},{3,4},{5,6},{2,1},{4,3},{6,5},{9,10},{11,12},{13,14},{10,9},... | collective-permute-start | bytes 270344 | tf_op jit(solution)/shard_map/ppermute | solution.py:581
  18.5 4.4 %spectra.1 = (f32[768,512]{1,0:T(8,128)S(1)}, f32[4992,256]{1,0:T(8,128)S(1)}, bf16[416,1248]{1,0:T(8,128)(2,1)S(1)}, bf16[176,624]{1,0:T(8,128)(2,1)S(1)}, bf16...) custom-call(f32[64,768]{1,0:T(8,128)} %kern_real.1, ...), custom_call_target="tpu_custom_call" | custom-call | tf_op jit(solution)/shard_map/spectra/pallas_call | solution.py:612
  22.9 0.0 collective-permute-done.2.first
  22.9 0.0 collective-permute-done.3.second
  22.9 6.8 %first.1 = (f32[288,128]{1,0:T(8,128)S(1)}, f32[144,128]{1,0:T(8,128)S(1)}, f32[144,128]{1,0:T(8,128)S(1)}, f32[288,128]{1,0:T(8,128)S(1)}, f32[2,112,128]{2,1,0:T(8,128)S(1)}) custom-call(s32[8,256]{1,0:T(8,128)S(1)} %iota.7.place, f32[12,128]{1,0:T(8,128)S(1)} %broadcast_in_dim.16.weights, f32[150,128]{1,0:T(8,128)S(1)} %get-tuple-element.54.own, ...), custom_call_target="tpu_custom_call" | custom-call | tf_op jit(solution)/shard_map/first/pallas_call | solution.py:549
  29.7 4.9 %collective-permute-start.4 = (f32[144,128]{1,0:T(8,128)S(1)}, f32[144,128]{1,0:T(8,128)S(1)}, u32[]{:S(2)}, u32[]{:S(2)}) collective-permute-start(f32[144,128]{1,0:T(8,128)S(1)} %get-tuple-element.72), channel_id=1, source_target_pairs={{8,16},{24,32},{40,48},{56,64},{72,80},{88,96},{104,112},{120,128}... | collective-permute-start | bytes 221192 | tf_op jit(solution)/shard_map/ppermute | solution.py:576
  34.5 0.3 collective-permute-start.5
  34.8 2.2 %slim.1 = (f32[3456,256]{1,0:T(8,128)S(1)}, bf16[288,864]{1,0:T(8,128)(2,1)S(1)}, bf16[112,432]{1,0:T(8,128)(2,1)S(1)}, bf16[112,432]{1,0:T(8,128)(2,1)S(1)}, bf...) custom-call(f32[768,512]{1,0:T(8,128)S(1)} %get-tuple-element.76.hal, ...), custom_call_target="tpu_custom_call" | custom-call | tf_op jit(solution)/shard_map/slim/pallas_call | solution.py:612
  37.1 0.4 collective-permute-done.4.far
  37.4 0.0 collective-permute-done.5.near
  37.4 4.8 %second.1 = (f32[160,128]{1,0:T(8,128)S(1)}, f32[80,128]{1,0:T(8,128)S(1)}, f32[80,128]{1,0:T(8,128)S(1)}, f32[160,128]{1,0:T(8,128)S(1)}) custom-call(s32[8,256]{1,0:T(8,128)S(1)} %iota.7.place, f32[12,128]{1,0:T(8,128)S(1)} %broadcast_in_dim.16.weights, f32[288,128]{1,0:T(8,128)S(1)} %get-tuple-element.71.own, f32[144,128]{1,0:T(8,128)S(1)} %collective-permute-done.4.far, ...), custom_call_target="tpu_custom_call" | custom-call | tf_op jit(solution)/shard_map/second/pallas_call | solution.py:549
  42.2 4.9 %collective-permute-start.6 = (f32[80,128]{1,0:T(8,128)S(1)}, f32[80,128]{1,0:T(8,128)S(1)}, u32[]{:S(2)}, u32[]{:S(2)}) collective-permute-start(f32[80,128]{1,0:T(8,128)S(1)} %get-tuple-element.85), channel_id=1, source_target_pairs={{8,16},{24,32},{40,48},{56,64},{72,80},{88,96},{104,112},{120,128}... | collective-permute-start | bytes 122888 | tf_op jit(solution)/shard_map/ppermute | solution.py:576
  47.1 0.1 collective-permute-start.7
  47.2 2.5 %collective-permute-done.6.far = f32[80,128]{1,0:T(8,128)S(1)} collective-permute-done((f32[80,128]{1,0:T(8,128)S(1)}, f32[80,128]{1,0:T(8,128)S(1)}, u32[]{:S(2)}, u32[]{:S(2)}) %collective-permute-start.6) | collective-permute-done | bytes 40992 | tf_op jit(solution)/shard_map/ppermute | solution.py:576
  49.6 0.0 collective-permute-done.7.near
  49.7 0.1 update.1
  49.8 0.1 collective-permute-start.8
  49.9 8.0 %collective-permute-start.9 = (f32[64,128]{1,0:T(8,128)S(1)}, f32[64,128]{1,0:T(8,128)S(1)}, u32[]{:S(2)}, u32[]{:S(2)}) collective-permute-start(f32[64,128]{1,0:T(8,128)S(1)} %get-tuple-element.90), channel_id=1, source_target_pairs={{1,2},{3,4},{5,6},{2,1},{4,3},{6,5},{9,10},{11,12},{13,14},{10,9},... | collective-permute-start | bytes 98312 | tf_op jit(solution)/shard_map/ppermute | solution.py:581
  57.9 0.0 collective-permute-done.8.first
  57.9 3.8 %collective-permute-done.9.second = f32[64,128]{1,0:T(8,128)S(1)} collective-permute-done((f32[64,128]{1,0:T(8,128)S(1)}, f32[64,128]{1,0:T(8,128)S(1)}, u32[]{:S(2)}, u32[]{:S(2)}) %collective-permute-start.9) | collective-permute-done | bytes 32800 | tf_op jit(solution)/shard_map/ppermute | solution.py:581
  61.7 4.6 %third.1 = (f32[160,128]{1,0:T(8,128)S(1)}, f32[80,128]{1,0:T(8,128)S(1)}, f32[80,128]{1,0:T(8,128)S(1)}, f32[2,112,128]{2,1,0:T(8,128)S(1)}) custom-call(s32[8,256]{1,0:T(8,128)S(1)} %iota.7.place, f32[12,128]{1,0:T(8,128)S(1)} %broadcast_in_dim.16.weights, f32[160,128]{1,0:T(8,128)S(1)} %get-tuple-element.88.own, ...), custom_call_target="tpu_custom_call" | custom-call | tf_op jit(solution)/shard_map/third/pallas_call | solution.py:549
  66.3 3.7 %collective-permute-start.10 = (f32[80,128]{1,0:T(8,128)S(1)}, f32[80,128]{1,0:T(8,128)S(1)}, u32[]{:S(2)}, u32[]{:S(2)}) collective-permute-start(f32[80,128]{1,0:T(8,128)S(1)} %get-tuple-element.92), channel_id=1, source_target_pairs={{8,16},{24,32},{40,48},{56,64},{72,80},{88,96},{104,112},{120,128}... | collective-permute-start | bytes 122888 | tf_op jit(solution)/shard_map/ppermute | solution.py:576
  70.1 0.1 collective-permute-start.11
  70.2 0.9 %intensity.1 = f32[64,150]{1,0:T(8,128)} custom-call(f32[2,112,128]{2,1,0:T(8,128)S(1)} %get-tuple-element.94.intensity, bf16[80,112]{1,0:T(8,128)(2,1)S(1)} %get-tuple-element.95.mirror), custom_call_target="tpu_custom_call" | custom-call | tf_op jit(solution)/shard_map/intensity/pallas_call | solution.py:549
  71.0 2.7 %collective-permute-done.10.far = f32[80,128]{1,0:T(8,128)S(1)} collective-permute-done((f32[80,128]{1,0:T(8,128)S(1)}, f32[80,128]{1,0:T(8,128)S(1)}, u32[]{:S(2)}, u32[]{:S(2)}) %collective-permute-start.10) | collective-permute-done | bytes 40992 | tf_op jit(solution)/shard_map/ppermute | solution.py:576
  73.8 0.0 collective-permute-done.11.near
  73.8 0.8 %final.1 = f32[64,150]{1,0:T(8,128)} custom-call(s32[8,256]{1,0:T(8,128)S(1)} %iota.7.place, f32[160,128]{1,0:T(8,128)S(1)} %get-tuple-element.91.own, f32[80,128]{1,0:T(8,128)S(1)} %collective-permute-done.10.far, f32[80,128]{1,0:T(8,128)S(1)} %collective-permute-done.11.near), custom_call_target="tpu_custom_call" | custom-call | tf_op jit(solution)/shard_map/final/pallas_call | solution.py:549
  (1 shorter events, 0.0 us)
Async XLA Ops:
  0.6 5.7 %collective-permute-start = (f32[64,150]{1,0:T(8,128)}, f32[64,150]{1,0:T(8,128)S(1)}, u32[]{:S(2)}, u32[]{:S(2)}) collective-permute-start(f32[64,150]{1,0:T(8,128)} %own.1), channel_id=1, source_target_pairs={{0,8},{16,24},{32,40},{48,56},{64,72},{80,88},{96,104},{112,120},{... | collective-permute-start | bytes 115208 | tf_op jit(solution)/shard_map/ppermute | solution.py:577
  0.7 7.9 %collective-permute-start.1 = (f32[64,150]{1,0:T(8,128)}, f32[64,150]{1,0:T(8,128)S(1)}, u32[]{:S(2)}, u32[]{:S(2)}) collective-permute-start(f32[64,150]{1,0:T(8,128)} %own.1), channel_id=1, source_target_pairs={{8,16},{24,32},{40,48},{56,64},{72,80},{88,96},{104,112},{120,128}... | collective-permute-start | bytes 115208 | tf_op jit(solution)/shard_map/ppermute | solution.py:576
  8.8 14.1 %collective-permute-start.2 = (f32[176,128]{1,0:T(8,128)S(1)}, f32[176,128]{1,0:T(8,128)S(1)}, u32[]{:S(2)}, u32[]{:S(2)}) collective-permute-start(f32[176,128]{1,0:T(8,128)S(1)} %get-tuple-element.55), channel_id=1, source_target_pairs={{0,1},{2,3},{4,5},{6,7},{1,0},{3,2},{5,4},{7,6},{8,9},{10,11},{12,... | collective-permute-start | bytes 270344 | tf_op jit(solution)/shard_map/ppermute | solution.py:580
  9.7 13.2 %collective-permute-start.3 = (f32[176,128]{1,0:T(8,128)S(1)}, f32[176,128]{1,0:T(8,128)S(1)}, u32[]{:S(2)}, u32[]{:S(2)}) collective-permute-start(f32[176,128]{1,0:T(8,128)S(1)} %get-tuple-element.56), channel_id=1, source_target_pairs={{1,2},{3,4},{5,6},{2,1},{4,3},{6,5},{9,10},{11,12},{13,14},{10,9},... | collective-permute-start | bytes 270344 | tf_op jit(solution)/shard_map/ppermute | solution.py:581
  29.7 7.8 %collective-permute-start.4 = (f32[144,128]{1,0:T(8,128)S(1)}, f32[144,128]{1,0:T(8,128)S(1)}, u32[]{:S(2)}, u32[]{:S(2)}) collective-permute-start(f32[144,128]{1,0:T(8,128)S(1)} %get-tuple-element.72), channel_id=1, source_target_pairs={{8,16},{24,32},{40,48},{56,64},{72,80},{88,96},{104,112},{120,128}... | collective-permute-start | bytes 221192 | tf_op jit(solution)/shard_map/ppermute | solution.py:576
  34.5 2.9 %collective-permute-start.5 = (f32[144,128]{1,0:T(8,128)S(1)}, f32[144,128]{1,0:T(8,128)S(1)}, u32[]{:S(2)}, u32[]{:S(2)}) collective-permute-start(f32[144,128]{1,0:T(8,128)S(1)} %get-tuple-element.73), channel_id=1, source_target_pairs={{0,8},{16,24},{32,40},{48,56},{64,72},{80,88},{96,104},{112,120},{... | collective-permute-start | bytes 221192 | tf_op jit(solution)/shard_map/ppermute | solution.py:577
  42.2 7.4 %collective-permute-start.6 = (f32[80,128]{1,0:T(8,128)S(1)}, f32[80,128]{1,0:T(8,128)S(1)}, u32[]{:S(2)}, u32[]{:S(2)}) collective-permute-start(f32[80,128]{1,0:T(8,128)S(1)} %get-tuple-element.85), channel_id=1, source_target_pairs={{8,16},{24,32},{40,48},{56,64},{72,80},{88,96},{104,112},{120,128}... | collective-permute-start | bytes 122888 | tf_op jit(solution)/shard_map/ppermute | solution.py:576
  47.1 2.6 %collective-permute-start.7 = (f32[80,128]{1,0:T(8,128)S(1)}, f32[80,128]{1,0:T(8,128)S(1)}, u32[]{:S(2)}, u32[]{:S(2)}) collective-permute-start(f32[80,128]{1,0:T(8,128)S(1)} %get-tuple-element.86), channel_id=1, source_target_pairs={{0,8},{16,24},{32,40},{48,56},{64,72},{80,88},{96,104},{112,120},{... | collective-permute-start | bytes 122888 | tf_op jit(solution)/shard_map/ppermute | solution.py:577
  49.8 8.1 %collective-permute-start.8 = (f32[64,128]{1,0:T(8,128)S(1)}, f32[64,128]{1,0:T(8,128)S(1)}, u32[]{:S(2)}, u32[]{:S(2)}) collective-permute-start(f32[64,128]{1,0:T(8,128)S(1)} %get-tuple-element.89), channel_id=1, source_target_pairs={{0,1},{2,3},{4,5},{6,7},{1,0},{3,2},{5,4},{7,6},{8,9},{10,11},{12,... | collective-permute-start | bytes 98312 | tf_op jit(solution)/shard_map/ppermute | solution.py:580
  49.9 11.8 %collective-permute-start.9 = (f32[64,128]{1,0:T(8,128)S(1)}, f32[64,128]{1,0:T(8,128)S(1)}, u32[]{:S(2)}, u32[]{:S(2)}) collective-permute-start(f32[64,128]{1,0:T(8,128)S(1)} %get-tuple-element.90), channel_id=1, source_target_pairs={{1,2},{3,4},{5,6},{2,1},{4,3},{6,5},{9,10},{11,12},{13,14},{10,9},... | collective-permute-start | bytes 98312 | tf_op jit(solution)/shard_map/ppermute | solution.py:581
  66.3 7.4 %collective-permute-start.10 = (f32[80,128]{1,0:T(8,128)S(1)}, f32[80,128]{1,0:T(8,128)S(1)}, u32[]{:S(2)}, u32[]{:S(2)}) collective-permute-start(f32[80,128]{1,0:T(8,128)S(1)} %get-tuple-element.92), channel_id=1, source_target_pairs={{8,16},{24,32},{40,48},{56,64},{72,80},{88,96},{104,112},{120,128}... | collective-permute-start | bytes 122888 | tf_op jit(solution)/shard_map/ppermute | solution.py:576
  70.1 3.7 %collective-permute-start.11 = (f32[80,128]{1,0:T(8,128)S(1)}, f32[80,128]{1,0:T(8,128)S(1)}, u32[]{:S(2)}, u32[]{:S(2)}) collective-permute-start(f32[80,128]{1,0:T(8,128)S(1)} %get-tuple-element.93), channel_id=1, source_target_pairs={{0,8},{16,24},{32,40},{48,56},{64,72},{80,88},{96,104},{112,120},{... | collective-permute-start | bytes 122888 | tf_op jit(solution)/shard_map/ppermute | solution.py:577

commit v7 on v6

--- a/solution.py
+++ b/solution.py
@@ -413,6 +413,38 @@
     left_lanes = lanes((half, 128))
     to_far[...] = jnp.where(left_lanes, straight[:half], crossed[half:])
     to_near[...] = jnp.where(left_lanes, crossed[:half], straight[half:])
+
+
+def last_spread_out(place, grad, spread, to_far, to_near):
+    size = to_far.shape[0]
+    quarter = lax.broadcasted_iota(jnp.int32, (size, 128), 1) // 32
+    spread[...] = grad
+    top = bottom = jnp.zeros((size, 128), f32)
+    for index in range(4):
+        part = grad[index * size : (index + 1) * size]
+        here = quarter == index
+        top = jnp.where(here, pltpu.roll(part, 32 * index, 1), top)
+        bottom = jnp.where(here, pltpu.roll(part, (32 * index + 32) % 128, 1), bottom)
+    even = is_even(place, 0, (size, 128))
+    to_far[...] = jnp.where(even, top, bottom)
+    to_near[...] = jnp.where(even, bottom, top)
+
+
+def last_gathered(place, spread, far, near):
+    size = far.shape[0]
+    even = is_even(place, 0, far.shape)
+    above = jnp.where(even, far[...], near[...])
+    below = jnp.where(even, near[...], far[...])
+    upper = lanes(far.shape)
+    parts = [
+        jnp.where(
+            upper,
+            pltpu.roll(above, (160 - 32 * index) % 128, 1),
+            pltpu.roll(below, (192 - 32 * index) % 128, 1),
+        )
+        for index in range(4)
+    ]
+    return spread[...] + jnp.concatenate(parts, 0)
 
 
 def gathered(place, spread, far, near):
@@ -518,7 +550,7 @@
     inside = field_window(geo, place, tile, whole, -64)
     goals = [goal[0], goal[1]]
     intensity, grad = one_step(geo, mask, goals, inside, weights, spec, tabs, fields)
-    spread_out(place, grad, spread, to_far, to_near)
+    last_spread_out(place, grad, spread, to_far, to_near)
     for side in (0, 1):
         intensity_out[side] = intensity[side]
 
@@ -535,7 +567,7 @@
 
 def final_kernel(cols, place, own, far, near, out, wide):
     wide[...] = jnp.zeros_like(wide)
-    wide[0 : own.shape[0], :] = gathered(place, own, far, near)
+    wide[0 : own.shape[0], :] = last_gathered(place, own, far, near)
     out[...] = wide[...].T[H : H + 64, :cols]
 
 
@@ -688,7 +720,7 @@
     spread, to_far, to_near, intensity = call(
         functools.partial(third_kernel, slim, tile, whole),
         "third",
-        spreads(slim) + [(2, slim.half_up, 128)],
+        spreads(slim)[:1] + [(slim.grad_up // 4, 128)] * 2 + [(2, slim.half_up, 128)],
         [(slim.mask_up, 128), fields(slim)],
         [place, weights, params, first, second, goal, slim_spec, *tabs("slim")],
     )

time: 75.2 us -> 75 us (level)
  no operation moved by 1% of the time
where the time goes in v7:
time: 75 us; the launch traced here: 74.4 us
  starting transfers between devices  36.3 us (48%)
  Pallas kernels  25.7 us (34%)
  waiting for transfers between devices  10.8 us (14%)
  between operations  0.8 us (1%)
  local copies, waits for them, and re-layouts  0.79 us (1%)
    pallas_call x8, Pallas kernels, call(): pl.pallas_call(kernel, name=name, out_shape=[shape if isinstance(shape, j...  19.1 us
    ppermute x4, starting transfers between devices, row_exchange(): far = lax.ppermute(to_far, 'row', swaps(rows, 1))  18 us
    ppermute x2, starting transfers between devices, col_exchange(): return (first, lax.ppermute(to_second, 'col', swaps(cols, 1)))  16.8 us
    ppermute x4, waiting for transfers between devices, row_exchange(): far = lax.ppermute(to_far, 'row', swaps(rows, 1))  6.89 us
    pallas_call x2, Pallas kernels, loader(): pl.pallas_call(functools.partial(kernel, geo, len(tables)), name=name, ou...  6.63 us
    ppermute x2, waiting for transfers between devices, col_exchange(): return (first, lax.ppermute(to_second, 'col', swaps(cols, 1)))  3.85 us
  transfers between devices with their start and end apart: 12, of which 5 were waited for; matrix products, arithmetic and copies ran while one was open for 1% of the time, Pallas kernels for 11%

profile of v7, /device:TPU:38, one launch (start us, length us, event | category | flops | bytes accessed | tf_op | source)
XLA Modules:
  0.0 74.4 jit_solution(9011977694274895640)
XLA Ops:
  0.6 0.1 collective-permute-start
  0.7 4.6 %collective-permute-start.1 = (f32[64,150]{1,0:T(8,128)}, f32[64,150]{1,0:T(8,128)S(1)}, u32[]{:S(2)}, u32[]{:S(2)}) collective-permute-start(f32[64,150]{1,0:T(8,128)} %own.1), channel_id=1, source_target_pairs={{8,16},{24,32},{40,48},{56,64},{72,80},{88,96},{104,112},{120,128}... | collective-permute-start | bytes 115208 | tf_op jit(solution)/shard_map/ppermute | solution.py:608
  5.3 1.0 %early.1 = (f32[150,128]{1,0:T(8,128)S(1)}, f32[150,128]{1,0:T(8,128)S(1)}) custom-call(f32[64,150]{1,0:T(8,128)} %own.1, s32[5,64]{1,0:T(8,128)} %bitcast.1), custom_call_target="tpu_custom_call" | custom-call | tf_op jit(solution)/shard_map/early/pallas_call | solution.py:581
  6.3 0.0 collective-permute-done.within
  6.3 0.1 iota.7.place
  6.4 0.7 broadcast_in_dim.16.weights
  7.1 1.5 %collective-permute-done.1.across = f32[64,150]{1,0:T(8,128)S(1)} collective-permute-done((f32[64,150]{1,0:T(8,128)}, f32[64,150]{1,0:T(8,128)S(1)}, u32[]{:S(2)}, u32[]{:S(2)}) %collective-permute-start.1) | collective-permute-done | bytes 38432 | tf_op jit(solution)/shard_map/ppermute | solution.py:608
  8.6 0.1 prep.1
  8.8 0.9 %collective-permute-start.2 = (f32[176,128]{1,0:T(8,128)S(1)}, f32[176,128]{1,0:T(8,128)S(1)}, u32[]{:S(2)}, u32[]{:S(2)}) collective-permute-start(f32[176,128]{1,0:T(8,128)S(1)} %get-tuple-element.55), channel_id=1, source_target_pairs={{0,1},{2,3},{4,5},{6,7},{1,0},{3,2},{5,4},{7,6},{8,9},{10,11},{12,... | collective-permute-start | bytes 270344 | tf_op jit(solution)/shard_map/ppermute | solution.py:612
  9.7 8.8 %collective-permute-start.3 = (f32[176,128]{1,0:T(8,128)S(1)}, f32[176,128]{1,0:T(8,128)S(1)}, u32[]{:S(2)}, u32[]{:S(2)}) collective-permute-start(f32[176,128]{1,0:T(8,128)S(1)} %get-tuple-element.56), channel_id=1, source_target_pairs={{1,2},{3,4},{5,6},{2,1},{4,3},{6,5},{9,10},{11,12},{13,14},{10,9},... | collective-permute-start | bytes 270344 | tf_op jit(solution)/shard_map/ppermute | solution.py:613
  18.5 4.4 %spectra.1 = (f32[768,512]{1,0:T(8,128)S(1)}, f32[4992,256]{1,0:T(8,128)S(1)}, bf16[416,1248]{1,0:T(8,128)(2,1)S(1)}, bf16[176,624]{1,0:T(8,128)(2,1)S(1)}, bf16...) custom-call(f32[64,768]{1,0:T(8,128)} %kern_real.1, ...), custom_call_target="tpu_custom_call" | custom-call | tf_op jit(solution)/shard_map/spectra/pallas_call | solution.py:644
  22.9 0.0 collective-permute-done.2.first
  22.9 0.0 collective-permute-done.3.second
  22.9 6.8 %first.1 = (f32[288,128]{1,0:T(8,128)S(1)}, f32[144,128]{1,0:T(8,128)S(1)}, f32[144,128]{1,0:T(8,128)S(1)}, f32[288,128]{1,0:T(8,128)S(1)}, f32[2,112,128]{2,1,0:T(8,128)S(1)}) custom-call(s32[8,256]{1,0:T(8,128)S(1)} %iota.7.place, f32[12,128]{1,0:T(8,128)S(1)} %broadcast_in_dim.16.weights, f32[150,128]{1,0:T(8,128)S(1)} %get-tuple-element.54.own, ...), custom_call_target="tpu_custom_call" | custom-call | tf_op jit(solution)/shard_map/first/pallas_call | solution.py:581
  29.7 4.9 %collective-permute-start.4 = (f32[144,128]{1,0:T(8,128)S(1)}, f32[144,128]{1,0:T(8,128)S(1)}, u32[]{:S(2)}, u32[]{:S(2)}) collective-permute-start(f32[144,128]{1,0:T(8,128)S(1)} %get-tuple-element.72), channel_id=1, source_target_pairs={{8,16},{24,32},{40,48},{56,64},{72,80},{88,96},{104,112},{120,128}... | collective-permute-start | bytes 221192 | tf_op jit(solution)/shard_map/ppermute | solution.py:608
  34.5 0.3 collective-permute-start.5
  34.8 2.2 %slim.1 = (f32[3456,256]{1,0:T(8,128)S(1)}, bf16[288,864]{1,0:T(8,128)(2,1)S(1)}, bf16[112,432]{1,0:T(8,128)(2,1)S(1)}, bf16[112,432]{1,0:T(8,128)(2,1)S(1)}, bf...) custom-call(f32[768,512]{1,0:T(8,128)S(1)} %get-tuple-element.76.hal, ...), custom_call_target="tpu_custom_call" | custom-call | tf_op jit(solution)/shard_map/slim/pallas_call | solution.py:644
  37.1 0.4 collective-permute-done.4.far
  37.4 0.0 collective-permute-done.5.near
  37.4 4.8 %second.1 = (f32[160,128]{1,0:T(8,128)S(1)}, f32[80,128]{1,0:T(8,128)S(1)}, f32[80,128]{1,0:T(8,128)S(1)}, f32[160,128]{1,0:T(8,128)S(1)}) custom-call(s32[8,256]{1,0:T(8,128)S(1)} %iota.7.place, f32[12,128]{1,0:T(8,128)S(1)} %broadcast_in_dim.16.weights, f32[288,128]{1,0:T(8,128)S(1)} %get-tuple-element.71.own, f32[144,128]{1,0:T(8,128)S(1)} %collective-permute-done.4.far, ...), custom_call_target="tpu_custom_call" | custom-call | tf_op jit(solution)/shard_map/second/pallas_call | solution.py:581
  42.2 4.9 %collective-permute-start.6 = (f32[80,128]{1,0:T(8,128)S(1)}, f32[80,128]{1,0:T(8,128)S(1)}, u32[]{:S(2)}, u32[]{:S(2)}) collective-permute-start(f32[80,128]{1,0:T(8,128)S(1)} %get-tuple-element.85), channel_id=1, source_target_pairs={{8,16},{24,32},{40,48},{56,64},{72,80},{88,96},{104,112},{120,128}... | collective-permute-start | bytes 122888 | tf_op jit(solution)/shard_map/ppermute | solution.py:608
  47.1 0.1 collective-permute-start.7
  47.2 2.5 %collective-permute-done.6.far = f32[80,128]{1,0:T(8,128)S(1)} collective-permute-done((f32[80,128]{1,0:T(8,128)S(1)}, f32[80,128]{1,0:T(8,128)S(1)}, u32[]{:S(2)}, u32[]{:S(2)}) %collective-permute-start.6) | collective-permute-done | bytes 40992 | tf_op jit(solution)/shard_map/ppermute | solution.py:608
  49.6 0.0 collective-permute-done.7.near
  49.7 0.1 update.1
  49.8 0.1 collective-permute-start.8
  49.9 8.0 %collective-permute-start.9 = (f32[64,128]{1,0:T(8,128)S(1)}, f32[64,128]{1,0:T(8,128)S(1)}, u32[]{:S(2)}, u32[]{:S(2)}) collective-permute-start(f32[64,128]{1,0:T(8,128)S(1)} %get-tuple-element.90), channel_id=1, source_target_pairs={{1,2},{3,4},{5,6},{2,1},{4,3},{6,5},{9,10},{11,12},{13,14},{10,9},... | collective-permute-start | bytes 98312 | tf_op jit(solution)/shard_map/ppermute | solution.py:613
  57.9 0.0 collective-permute-done.8.first
  57.9 3.8 %collective-permute-done.9.second = f32[64,128]{1,0:T(8,128)S(1)} collective-permute-done((f32[64,128]{1,0:T(8,128)S(1)}, f32[64,128]{1,0:T(8,128)S(1)}, u32[]{:S(2)}, u32[]{:S(2)}) %collective-permute-start.9) | collective-permute-done | bytes 32800 | tf_op jit(solution)/shard_map/ppermute | solution.py:613
  61.7 4.7 %third.1 = (f32[160,128]{1,0:T(8,128)S(1)}, f32[40,128]{1,0:T(8,128)S(1)}, f32[40,128]{1,0:T(8,128)S(1)}, f32[2,112,128]{2,1,0:T(8,128)S(1)}) custom-call(s32[8,256]{1,0:T(8,128)S(1)} %iota.7.place, f32[12,128]{1,0:T(8,128)S(1)} %broadcast_in_dim.16.weights, f32[160,128]{1,0:T(8,128)S(1)} %get-tuple-element.88.own, ...), custom_call_target="tpu_custom_call" | custom-call | tf_op jit(solution)/shard_map/third/pallas_call | solution.py:581
  66.3 3.7 %collective-permute-start.10 = (f32[40,128]{1,0:T(8,128)S(1)}, f32[40,128]{1,0:T(8,128)S(1)}, u32[]{:S(2)}, u32[]{:S(2)}) collective-permute-start(f32[40,128]{1,0:T(8,128)S(1)} %get-tuple-element.92), channel_id=1, source_target_pairs={{8,16},{24,32},{40,48},{56,64},{72,80},{88,96},{104,112},{120,128}... | collective-permute-start | bytes 61448 | tf_op jit(solution)/shard_map/ppermute | solution.py:608
  70.1 0.1 collective-permute-start.11
  70.2 0.9 %intensity.1 = f32[64,150]{1,0:T(8,128)} custom-call(f32[2,112,128]{2,1,0:T(8,128)S(1)} %get-tuple-element.94.intensity, bf16[80,112]{1,0:T(8,128)(2,1)S(1)} %get-tuple-element.95.mirror), custom_call_target="tpu_custom_call" | custom-call | tf_op jit(solution)/shard_map/intensity/pallas_call | solution.py:581
  71.0 2.5 %collective-permute-done.10.far = f32[40,128]{1,0:T(8,128)S(1)} collective-permute-done((f32[40,128]{1,0:T(8,128)S(1)}, f32[40,128]{1,0:T(8,128)S(1)}, u32[]{:S(2)}, u32[]{:S(2)}) %collective-permute-start.10) | collective-permute-done | bytes 20512 | tf_op jit(solution)/shard_map/ppermute | solution.py:608
  73.6 0.0 collective-permute-done.11.near
  73.6 0.8 %final.1 = f32[64,150]{1,0:T(8,128)} custom-call(s32[8,256]{1,0:T(8,128)S(1)} %iota.7.place, f32[160,128]{1,0:T(8,128)S(1)} %get-tuple-element.91.own, f32[40,128]{1,0:T(8,128)S(1)} %collective-permute-done.10.far, f32[40,128]{1,0:T(8,128)S(1)} %collective-permute-done.11.near), custom_call_target="tpu_custom_call" | custom-call | tf_op jit(solution)/shard_map/final/pallas_call | solution.py:581
  (1 shorter events, 0.0 us)
Async XLA Ops:
  0.6 5.7 %collective-permute-start = (f32[64,150]{1,0:T(8,128)}, f32[64,150]{1,0:T(8,128)S(1)}, u32[]{:S(2)}, u32[]{:S(2)}) collective-permute-start(f32[64,150]{1,0:T(8,128)} %own.1), channel_id=1, source_target_pairs={{0,8},{16,24},{32,40},{48,56},{64,72},{80,88},{96,104},{112,120},{... | collective-permute-start | bytes 115208 | tf_op jit(solution)/shard_map/ppermute | solution.py:609
  0.7 7.9 %collective-permute-start.1 = (f32[64,150]{1,0:T(8,128)}, f32[64,150]{1,0:T(8,128)S(1)}, u32[]{:S(2)}, u32[]{:S(2)}) collective-permute-start(f32[64,150]{1,0:T(8,128)} %own.1), channel_id=1, source_target_pairs={{8,16},{24,32},{40,48},{56,64},{72,80},{88,96},{104,112},{120,128}... | collective-permute-start | bytes 115208 | tf_op jit(solution)/shard_map/ppermute | solution.py:608
  8.8 14.1 %collective-permute-start.2 = (f32[176,128]{1,0:T(8,128)S(1)}, f32[176,128]{1,0:T(8,128)S(1)}, u32[]{:S(2)}, u32[]{:S(2)}) collective-permute-start(f32[176,128]{1,0:T(8,128)S(1)} %get-tuple-element.55), channel_id=1, source_target_pairs={{0,1},{2,3},{4,5},{6,7},{1,0},{3,2},{5,4},{7,6},{8,9},{10,11},{12,... | collective-permute-start | bytes 270344 | tf_op jit(solution)/shard_map/ppermute | solution.py:612
  9.7 13.2 %collective-permute-start.3 = (f32[176,128]{1,0:T(8,128)S(1)}, f32[176,128]{1,0:T(8,128)S(1)}, u32[]{:S(2)}, u32[]{:S(2)}) collective-permute-start(f32[176,128]{1,0:T(8,128)S(1)} %get-tuple-element.56), channel_id=1, source_target_pairs={{1,2},{3,4},{5,6},{2,1},{4,3},{6,5},{9,10},{11,12},{13,14},{10,9},... | collective-permute-start | bytes 270344 | tf_op jit(solution)/shard_map/ppermute | solution.py:613
  29.7 7.8 %collective-permute-start.4 = (f32[144,128]{1,0:T(8,128)S(1)}, f32[144,128]{1,0:T(8,128)S(1)}, u32[]{:S(2)}, u32[]{:S(2)}) collective-permute-start(f32[144,128]{1,0:T(8,128)S(1)} %get-tuple-element.72), channel_id=1, source_target_pairs={{8,16},{24,32},{40,48},{56,64},{72,80},{88,96},{104,112},{120,128}... | collective-permute-start | bytes 221192 | tf_op jit(solution)/shard_map/ppermute | solution.py:608
  34.5 2.9 %collective-permute-start.5 = (f32[144,128]{1,0:T(8,128)S(1)}, f32[144,128]{1,0:T(8,128)S(1)}, u32[]{:S(2)}, u32[]{:S(2)}) collective-permute-start(f32[144,128]{1,0:T(8,128)S(1)} %get-tuple-element.73), channel_id=1, source_target_pairs={{0,8},{16,24},{32,40},{48,56},{64,72},{80,88},{96,104},{112,120},{... | collective-permute-start | bytes 221192 | tf_op jit(solution)/shard_map/ppermute | solution.py:609
  42.2 7.4 %collective-permute-start.6 = (f32[80,128]{1,0:T(8,128)S(1)}, f32[80,128]{1,0:T(8,128)S(1)}, u32[]{:S(2)}, u32[]{:S(2)}) collective-permute-start(f32[80,128]{1,0:T(8,128)S(1)} %get-tuple-element.85), channel_id=1, source_target_pairs={{8,16},{24,32},{40,48},{56,64},{72,80},{88,96},{104,112},{120,128}... | collective-permute-start | bytes 122888 | tf_op jit(solution)/shard_map/ppermute | solution.py:608
  47.1 2.6 %collective-permute-start.7 = (f32[80,128]{1,0:T(8,128)S(1)}, f32[80,128]{1,0:T(8,128)S(1)}, u32[]{:S(2)}, u32[]{:S(2)}) collective-permute-start(f32[80,128]{1,0:T(8,128)S(1)} %get-tuple-element.86), channel_id=1, source_target_pairs={{0,8},{16,24},{32,40},{48,56},{64,72},{80,88},{96,104},{112,120},{... | collective-permute-start | bytes 122888 | tf_op jit(solution)/shard_map/ppermute | solution.py:609
  49.8 8.1 %collective-permute-start.8 = (f32[64,128]{1,0:T(8,128)S(1)}, f32[64,128]{1,0:T(8,128)S(1)}, u32[]{:S(2)}, u32[]{:S(2)}) collective-permute-start(f32[64,128]{1,0:T(8,128)S(1)} %get-tuple-element.89), channel_id=1, source_target_pairs={{0,1},{2,3},{4,5},{6,7},{1,0},{3,2},{5,4},{7,6},{8,9},{10,11},{12,... | collective-permute-start | bytes 98312 | tf_op jit(solution)/shard_map/ppermute | solution.py:612
  49.9 11.8 %collective-permute-start.9 = (f32[64,128]{1,0:T(8,128)S(1)}, f32[64,128]{1,0:T(8,128)S(1)}, u32[]{:S(2)}, u32[]{:S(2)}) collective-permute-start(f32[64,128]{1,0:T(8,128)S(1)} %get-tuple-element.90), channel_id=1, source_target_pairs={{1,2},{3,4},{5,6},{2,1},{4,3},{6,5},{9,10},{11,12},{13,14},{10,9},... | collective-permute-start | bytes 98312 | tf_op jit(solution)/shard_map/ppermute | solution.py:613
  66.3 7.2 %collective-permute-start.10 = (f32[40,128]{1,0:T(8,128)S(1)}, f32[40,128]{1,0:T(8,128)S(1)}, u32[]{:S(2)}, u32[]{:S(2)}) collective-permute-start(f32[40,128]{1,0:T(8,128)S(1)} %get-tuple-element.92), channel_id=1, source_target_pairs={{8,16},{24,32},{40,48},{56,64},{72,80},{88,96},{104,112},{120,128}... | collective-permute-start | bytes 61448 | tf_op jit(solution)/shard_map/ppermute | solution.py:608
  70.1 3.5 %collective-permute-start.11 = (f32[40,128]{1,0:T(8,128)S(1)}, f32[40,128]{1,0:T(8,128)S(1)}, u32[]{:S(2)}, u32[]{:S(2)}) collective-permute-start(f32[40,128]{1,0:T(8,128)S(1)} %get-tuple-element.93), channel_id=1, source_target_pairs={{0,8},{16,24},{32,40},{48,56},{64,72},{80,88},{96,104},{112,120},{... | collective-permute-start | bytes 61448 | tf_op jit(solution)/shard_map/ppermute | solution.py:609

commit v8 on v7

--- a/solution.py
+++ b/solution.py
@@ -266,7 +266,7 @@
         return value[:, :128], value[:, 128:]
 
     evens, odds = [], []
-    for start, stop in chunks(count, 1):
+    for start, stop in chunks(count, 2 if geo.dense() else 1):
         size = stop - start
         lane = lanes((size, 128))
         mask_re, mask_im = mask_spec[start:stop, :128], mask_spec[start:stop, 128:]

time: 75 us -> 75.1 us (level)
  no operation moved by 1% of the time
where the time goes in v8:
time: 75.1 us; the launch traced here: 74.4 us
  starting transfers between devices  36.3 us (48%)
  Pallas kernels  25.8 us (34%)
  waiting for transfers between devices  10.7 us (14%)
  between operations  0.8 us (1%)
  local copies, waits for them, and re-layouts  0.79 us (1%)
    pallas_call x8, Pallas kernels, call(): pl.pallas_call(kernel, name=name, out_shape=[shape if isinstance(shape, j...  19.1 us
    ppermute x4, starting transfers between devices, row_exchange(): far = lax.ppermute(to_far, 'row', swaps(rows, 1))  18 us
    ppermute x2, starting transfers between devices, col_exchange(): return (first, lax.ppermute(to_second, 'col', swaps(cols, 1)))  16.8 us
    ppermute x4, waiting for transfers between devices, row_exchange(): far = lax.ppermute(to_far, 'row', swaps(rows, 1))  6.88 us
    pallas_call x2, Pallas kernels, loader(): pl.pallas_call(functools.partial(kernel, geo, len(tables)), name=name, ou...  6.63 us
    ppermute x2, waiting for transfers between devices, col_exchange(): return (first, lax.ppermute(to_second, 'col', swaps(cols, 1)))  3.85 us
  transfers between devices with their start and end apart: 12, of which 5 were waited for; matrix products, arithmetic and copies ran while one was open for 1% of the time, Pallas kernels for 11%

profile of v8, /device:TPU:38, one launch (start us, length us, event | category | flops | bytes accessed | tf_op | source)
XLA Modules:
  0.0 74.4 jit_solution(6729305377218014691)
XLA Ops:
  0.6 0.1 collective-permute-start
  0.7 4.6 %collective-permute-start.1 = (f32[64,150]{1,0:T(8,128)}, f32[64,150]{1,0:T(8,128)S(1)}, u32[]{:S(2)}, u32[]{:S(2)}) collective-permute-start(f32[64,150]{1,0:T(8,128)} %own.1), channel_id=1, source_target_pairs={{8,16},{24,32},{40,48},{56,64},{72,80},{88,96},{104,112},{120,128}... | collective-permute-start | bytes 115208 | tf_op jit(solution)/shard_map/ppermute | solution.py:608
  5.3 1.0 %early.1 = (f32[150,128]{1,0:T(8,128)S(1)}, f32[150,128]{1,0:T(8,128)S(1)}) custom-call(f32[64,150]{1,0:T(8,128)} %own.1, s32[5,64]{1,0:T(8,128)} %bitcast.1), custom_call_target="tpu_custom_call" | custom-call | tf_op jit(solution)/shard_map/early/pallas_call | solution.py:581
  6.3 0.0 collective-permute-done.within
  6.3 0.1 iota.7.place
  6.4 0.7 broadcast_in_dim.16.weights
  7.1 1.5 %collective-permute-done.1.across = f32[64,150]{1,0:T(8,128)S(1)} collective-permute-done((f32[64,150]{1,0:T(8,128)}, f32[64,150]{1,0:T(8,128)S(1)}, u32[]{:S(2)}, u32[]{:S(2)}) %collective-permute-start.1) | collective-permute-done | bytes 38432 | tf_op jit(solution)/shard_map/ppermute | solution.py:608
  8.6 0.1 prep.1
  8.8 0.9 %collective-permute-start.2 = (f32[176,128]{1,0:T(8,128)S(1)}, f32[176,128]{1,0:T(8,128)S(1)}, u32[]{:S(2)}, u32[]{:S(2)}) collective-permute-start(f32[176,128]{1,0:T(8,128)S(1)} %get-tuple-element.55), channel_id=1, source_target_pairs={{0,1},{2,3},{4,5},{6,7},{1,0},{3,2},{5,4},{7,6},{8,9},{10,11},{12,... | collective-permute-start | bytes 270344 | tf_op jit(solution)/shard_map/ppermute | solution.py:612
  9.7 8.8 %collective-permute-start.3 = (f32[176,128]{1,0:T(8,128)S(1)}, f32[176,128]{1,0:T(8,128)S(1)}, u32[]{:S(2)}, u32[]{:S(2)}) collective-permute-start(f32[176,128]{1,0:T(8,128)S(1)} %get-tuple-element.56), channel_id=1, source_target_pairs={{1,2},{3,4},{5,6},{2,1},{4,3},{6,5},{9,10},{11,12},{13,14},{10,9},... | collective-permute-start | bytes 270344 | tf_op jit(solution)/shard_map/ppermute | solution.py:613
  18.5 4.4 %spectra.1 = (f32[768,512]{1,0:T(8,128)S(1)}, f32[4992,256]{1,0:T(8,128)S(1)}, bf16[416,1248]{1,0:T(8,128)(2,1)S(1)}, bf16[176,624]{1,0:T(8,128)(2,1)S(1)}, bf16...) custom-call(f32[64,768]{1,0:T(8,128)} %kern_real.1, ...), custom_call_target="tpu_custom_call" | custom-call | tf_op jit(solution)/shard_map/spectra/pallas_call | solution.py:644
  22.9 0.0 collective-permute-done.2.first
  22.9 0.0 collective-permute-done.3.second
  22.9 6.8 %first.1 = (f32[288,128]{1,0:T(8,128)S(1)}, f32[144,128]{1,0:T(8,128)S(1)}, f32[144,128]{1,0:T(8,128)S(1)}, f32[288,128]{1,0:T(8,128)S(1)}, f32[2,112,128]{2,1,0:T(8,128)S(1)}) custom-call(s32[8,256]{1,0:T(8,128)S(1)} %iota.7.place, f32[12,128]{1,0:T(8,128)S(1)} %broadcast_in_dim.16.weights, f32[150,128]{1,0:T(8,128)S(1)} %get-tuple-element.54.own, ...), custom_call_target="tpu_custom_call" | custom-call | tf_op jit(solution)/shard_map/first/pallas_call | solution.py:581
  29.7 4.9 %collective-permute-start.4 = (f32[144,128]{1,0:T(8,128)S(1)}, f32[144,128]{1,0:T(8,128)S(1)}, u32[]{:S(2)}, u32[]{:S(2)}) collective-permute-start(f32[144,128]{1,0:T(8,128)S(1)} %get-tuple-element.72), channel_id=1, source_target_pairs={{8,16},{24,32},{40,48},{56,64},{72,80},{88,96},{104,112},{120,128}... | collective-permute-start | bytes 221192 | tf_op jit(solution)/shard_map/ppermute | solution.py:608
  34.6 0.3 collective-permute-start.5
  34.9 2.2 %slim.1 = (f32[3456,256]{1,0:T(8,128)S(1)}, bf16[288,864]{1,0:T(8,128)(2,1)S(1)}, bf16[112,432]{1,0:T(8,128)(2,1)S(1)}, bf16[112,432]{1,0:T(8,128)(2,1)S(1)}, bf...) custom-call(f32[768,512]{1,0:T(8,128)S(1)} %get-tuple-element.76.hal, ...), custom_call_target="tpu_custom_call" | custom-call | tf_op jit(solution)/shard_map/slim/pallas_call | solution.py:644
  37.1 0.4 collective-permute-done.4.far
  37.5 0.0 collective-permute-done.5.near
  37.5 4.8 %second.1 = (f32[160,128]{1,0:T(8,128)S(1)}, f32[80,128]{1,0:T(8,128)S(1)}, f32[80,128]{1,0:T(8,128)S(1)}, f32[160,128]{1,0:T(8,128)S(1)}) custom-call(s32[8,256]{1,0:T(8,128)S(1)} %iota.7.place, f32[12,128]{1,0:T(8,128)S(1)} %broadcast_in_dim.16.weights, f32[288,128]{1,0:T(8,128)S(1)} %get-tuple-element.71.own, f32[144,128]{1,0:T(8,128)S(1)} %collective-permute-done.4.far, ...), custom_call_target="tpu_custom_call" | custom-call | tf_op jit(solution)/shard_map/second/pallas_call | solution.py:581
  42.3 4.9 %collective-permute-start.6 = (f32[80,128]{1,0:T(8,128)S(1)}, f32[80,128]{1,0:T(8,128)S(1)}, u32[]{:S(2)}, u32[]{:S(2)}) collective-permute-start(f32[80,128]{1,0:T(8,128)S(1)} %get-tuple-element.85), channel_id=1, source_target_pairs={{8,16},{24,32},{40,48},{56,64},{72,80},{88,96},{104,112},{120,128}... | collective-permute-start | bytes 122888 | tf_op jit(solution)/shard_map/ppermute | solution.py:608
  47.2 0.1 collective-permute-start.7
  47.3 2.5 %collective-permute-done.6.far = f32[80,128]{1,0:T(8,128)S(1)} collective-permute-done((f32[80,128]{1,0:T(8,128)S(1)}, f32[80,128]{1,0:T(8,128)S(1)}, u32[]{:S(2)}, u32[]{:S(2)}) %collective-permute-start.6) | collective-permute-done | bytes 40992 | tf_op jit(solution)/shard_map/ppermute | solution.py:608
  49.7 0.0 collective-permute-done.7.near
  49.7 0.1 update.1
  49.8 0.1 collective-permute-start.8
  49.9 8.0 %collective-permute-start.9 = (f32[64,128]{1,0:T(8,128)S(1)}, f32[64,128]{1,0:T(8,128)S(1)}, u32[]{:S(2)}, u32[]{:S(2)}) collective-permute-start(f32[64,128]{1,0:T(8,128)S(1)} %get-tuple-element.90), channel_id=1, source_target_pairs={{1,2},{3,4},{5,6},{2,1},{4,3},{6,5},{9,10},{11,12},{13,14},{10,9},... | collective-permute-start | bytes 98312 | tf_op jit(solution)/shard_map/ppermute | solution.py:613
  57.9 0.0 collective-permute-done.8.first
  57.9 3.8 %collective-permute-done.9.second = f32[64,128]{1,0:T(8,128)S(1)} collective-permute-done((f32[64,128]{1,0:T(8,128)S(1)}, f32[64,128]{1,0:T(8,128)S(1)}, u32[]{:S(2)}, u32[]{:S(2)}) %collective-permute-start.9) | collective-permute-done | bytes 32800 | tf_op jit(solution)/shard_map/ppermute | solution.py:613
  61.7 4.6 %third.1 = (f32[160,128]{1,0:T(8,128)S(1)}, f32[40,128]{1,0:T(8,128)S(1)}, f32[40,128]{1,0:T(8,128)S(1)}, f32[2,112,128]{2,1,0:T(8,128)S(1)}) custom-call(s32[8,256]{1,0:T(8,128)S(1)} %iota.7.place, f32[12,128]{1,0:T(8,128)S(1)} %broadcast_in_dim.16.weights, f32[160,128]{1,0:T(8,128)S(1)} %get-tuple-element.88.own, ...), custom_call_target="tpu_custom_call" | custom-call | tf_op jit(solution)/shard_map/third/pallas_call | solution.py:581
  66.4 3.7 %collective-permute-start.10 = (f32[40,128]{1,0:T(8,128)S(1)}, f32[40,128]{1,0:T(8,128)S(1)}, u32[]{:S(2)}, u32[]{:S(2)}) collective-permute-start(f32[40,128]{1,0:T(8,128)S(1)} %get-tuple-element.92), channel_id=1, source_target_pairs={{8,16},{24,32},{40,48},{56,64},{72,80},{88,96},{104,112},{120,128}... | collective-permute-start | bytes 61448 | tf_op jit(solution)/shard_map/ppermute | solution.py:608
  70.1 0.1 collective-permute-start.11
  70.2 0.9 %intensity.1 = f32[64,150]{1,0:T(8,128)} custom-call(f32[2,112,128]{2,1,0:T(8,128)S(1)} %get-tuple-element.94.intensity, bf16[80,112]{1,0:T(8,128)(2,1)S(1)} %get-tuple-element.95.mirror), custom_call_target="tpu_custom_call" | custom-call | tf_op jit(solution)/shard_map/intensity/pallas_call | solution.py:581
  71.1 2.5 %collective-permute-done.10.far = f32[40,128]{1,0:T(8,128)S(1)} collective-permute-done((f32[40,128]{1,0:T(8,128)S(1)}, f32[40,128]{1,0:T(8,128)S(1)}, u32[]{:S(2)}, u32[]{:S(2)}) %collective-permute-start.10) | collective-permute-done | bytes 20512 | tf_op jit(solution)/shard_map/ppermute | solution.py:608
  73.6 0.0 collective-permute-done.11.near
  73.6 0.8 %final.1 = f32[64,150]{1,0:T(8,128)} custom-call(s32[8,256]{1,0:T(8,128)S(1)} %iota.7.place, f32[160,128]{1,0:T(8,128)S(1)} %get-tuple-element.91.own, f32[40,128]{1,0:T(8,128)S(1)} %collective-permute-done.10.far, f32[40,128]{1,0:T(8,128)S(1)} %collective-permute-done.11.near), custom_call_target="tpu_custom_call" | custom-call | tf_op jit(solution)/shard_map/final/pallas_call | solution.py:581
  (1 shorter events, 0.0 us)
Async XLA Ops:
  0.6 5.7 %collective-permute-start = (f32[64,150]{1,0:T(8,128)}, f32[64,150]{1,0:T(8,128)S(1)}, u32[]{:S(2)}, u32[]{:S(2)}) collective-permute-start(f32[64,150]{1,0:T(8,128)} %own.1), channel_id=1, source_target_pairs={{0,8},{16,24},{32,40},{48,56},{64,72},{80,88},{96,104},{112,120},{... | collective-permute-start | bytes 115208 | tf_op jit(solution)/shard_map/ppermute | solution.py:609
  0.7 7.9 %collective-permute-start.1 = (f32[64,150]{1,0:T(8,128)}, f32[64,150]{1,0:T(8,128)S(1)}, u32[]{:S(2)}, u32[]{:S(2)}) collective-permute-start(f32[64,150]{1,0:T(8,128)} %own.1), channel_id=1, source_target_pairs={{8,16},{24,32},{40,48},{56,64},{72,80},{88,96},{104,112},{120,128}... | collective-permute-start | bytes 115208 | tf_op jit(solution)/shard_map/ppermute | solution.py:608
  8.8 14.1 %collective-permute-start.2 = (f32[176,128]{1,0:T(8,128)S(1)}, f32[176,128]{1,0:T(8,128)S(1)}, u32[]{:S(2)}, u32[]{:S(2)}) collective-permute-start(f32[176,128]{1,0:T(8,128)S(1)} %get-tuple-element.55), channel_id=1, source_target_pairs={{0,1},{2,3},{4,5},{6,7},{1,0},{3,2},{5,4},{7,6},{8,9},{10,11},{12,... | collective-permute-start | bytes 270344 | tf_op jit(solution)/shard_map/ppermute | solution.py:612
  9.7 13.2 %collective-permute-start.3 = (f32[176,128]{1,0:T(8,128)S(1)}, f32[176,128]{1,0:T(8,128)S(1)}, u32[]{:S(2)}, u32[]{:S(2)}) collective-permute-start(f32[176,128]{1,0:T(8,128)S(1)} %get-tuple-element.56), channel_id=1, source_target_pairs={{1,2},{3,4},{5,6},{2,1},{4,3},{6,5},{9,10},{11,12},{13,14},{10,9},... | collective-permute-start | bytes 270344 | tf_op jit(solution)/shard_map/ppermute | solution.py:613
  29.7 7.8 %collective-permute-start.4 = (f32[144,128]{1,0:T(8,128)S(1)}, f32[144,128]{1,0:T(8,128)S(1)}, u32[]{:S(2)}, u32[]{:S(2)}) collective-permute-start(f32[144,128]{1,0:T(8,128)S(1)} %get-tuple-element.72), channel_id=1, source_target_pairs={{8,16},{24,32},{40,48},{56,64},{72,80},{88,96},{104,112},{120,128}... | collective-permute-start | bytes 221192 | tf_op jit(solution)/shard_map/ppermute | solution.py:608
  34.6 2.9 %collective-permute-start.5 = (f32[144,128]{1,0:T(8,128)S(1)}, f32[144,128]{1,0:T(8,128)S(1)}, u32[]{:S(2)}, u32[]{:S(2)}) collective-permute-start(f32[144,128]{1,0:T(8,128)S(1)} %get-tuple-element.73), channel_id=1, source_target_pairs={{0,8},{16,24},{32,40},{48,56},{64,72},{80,88},{96,104},{112,120},{... | collective-permute-start | bytes 221192 | tf_op jit(solution)/shard_map/ppermute | solution.py:609
  42.3 7.4 %collective-permute-start.6 = (f32[80,128]{1,0:T(8,128)S(1)}, f32[80,128]{1,0:T(8,128)S(1)}, u32[]{:S(2)}, u32[]{:S(2)}) collective-permute-start(f32[80,128]{1,0:T(8,128)S(1)} %get-tuple-element.85), channel_id=1, source_target_pairs={{8,16},{24,32},{40,48},{56,64},{72,80},{88,96},{104,112},{120,128}... | collective-permute-start | bytes 122888 | tf_op jit(solution)/shard_map/ppermute | solution.py:608
  47.2 2.6 %collective-permute-start.7 = (f32[80,128]{1,0:T(8,128)S(1)}, f32[80,128]{1,0:T(8,128)S(1)}, u32[]{:S(2)}, u32[]{:S(2)}) collective-permute-start(f32[80,128]{1,0:T(8,128)S(1)} %get-tuple-element.86), channel_id=1, source_target_pairs={{0,8},{16,24},{32,40},{48,56},{64,72},{80,88},{96,104},{112,120},{... | collective-permute-start | bytes 122888 | tf_op jit(solution)/shard_map/ppermute | solution.py:609
  49.8 8.1 %collective-permute-start.8 = (f32[64,128]{1,0:T(8,128)S(1)}, f32[64,128]{1,0:T(8,128)S(1)}, u32[]{:S(2)}, u32[]{:S(2)}) collective-permute-start(f32[64,128]{1,0:T(8,128)S(1)} %get-tuple-element.89), channel_id=1, source_target_pairs={{0,1},{2,3},{4,5},{6,7},{1,0},{3,2},{5,4},{7,6},{8,9},{10,11},{12,... | collective-permute-start | bytes 98312 | tf_op jit(solution)/shard_map/ppermute | solution.py:612
  49.9 11.8 %collective-permute-start.9 = (f32[64,128]{1,0:T(8,128)S(1)}, f32[64,128]{1,0:T(8,128)S(1)}, u32[]{:S(2)}, u32[]{:S(2)}) collective-permute-start(f32[64,128]{1,0:T(8,128)S(1)} %get-tuple-element.90), channel_id=1, source_target_pairs={{1,2},{3,4},{5,6},{2,1},{4,3},{6,5},{9,10},{11,12},{13,14},{10,9},... | collective-permute-start | bytes 98312 | tf_op jit(solution)/shard_map/ppermute | solution.py:613
  66.4 7.2 %collective-permute-start.10 = (f32[40,128]{1,0:T(8,128)S(1)}, f32[40,128]{1,0:T(8,128)S(1)}, u32[]{:S(2)}, u32[]{:S(2)}) collective-permute-start(f32[40,128]{1,0:T(8,128)S(1)} %get-tuple-element.92), channel_id=1, source_target_pairs={{8,16},{24,32},{40,48},{56,64},{72,80},{88,96},{104,112},{120,128}... | collective-permute-start | bytes 61448 | tf_op jit(solution)/shard_map/ppermute | solution.py:608
  70.1 3.5 %collective-permute-start.11 = (f32[40,128]{1,0:T(8,128)S(1)}, f32[40,128]{1,0:T(8,128)S(1)}, u32[]{:S(2)}, u32[]{:S(2)}) collective-permute-start(f32[40,128]{1,0:T(8,128)S(1)} %get-tuple-element.93), channel_id=1, source_target_pairs={{0,8},{16,24},{32,40},{48,56},{64,72},{80,88},{96,104},{112,120},{... | collective-permute-start | bytes 61448 | tf_op jit(solution)/shard_map/ppermute | solution.py:609
